TPU v7x, 32 devices: a whole 2x2x4 slice. The times are simulated.
32 devices in a mesh: groups: 2 (over x), ctx: 16 (over z, y, core).
Axes of the slice: x: 2, y: 2, z: 4, core: 2. Of those that a mesh axis runs over, the one named last changes fastest.
Arguments:
- queries: bfloat16 [4096, 8192], P(('groups', 'ctx')), parts along dimension 0, may hold values from -112 to 112
- keys: bfloat16 [4096, 1024], P(('groups', 'ctx')), parts along dimension 0, may hold values from -4.04 to 4.04
- values: bfloat16 [4096, 1024], P(('groups', 'ctx')), parts along dimension 0, may hold values from -4 to 4
- norm_gain: float32 [8192], replicated, may hold values from 0.1 to 1.9
- expert_ids: int32 [4096, 2], P(('groups', 'ctx')), parts along dimension 0, may hold values from 0 to 15, as said below
- gates: float32 [4096, 2], P(('groups', 'ctx')), parts along dimension 0, may hold values from 0.2 to 1
- w_gate: bfloat16 [8192, 12288], P(None, 'ctx'), may hold values from -0.0625 to 0.0625
- w_up: bfloat16 [8192, 12288], P(None, 'ctx'), may hold values from -0.0625 to 0.0625
- w_down: bfloat16 [12288, 8192], P('ctx'), may hold values from -0.0546875 to 0.0546875
Outputs:
- attention: bfloat16 [4096, 8192], P(('groups', 'ctx')), parts along dimension 0
- mixed: bfloat16 [4096, 8192], P(('groups', 'ctx')), parts along dimension 0
There are 2 independent parts, one for each index of `groups`. A program takes and returns all parts, laid end to end along the dimension named above; an argument that names none is the same for every part. Nothing has to cross between parts.
Inputs may be any that keep to these rules, and one draw needn't show every extreme that they name: `expert_ids`: each token names two different experts. In each aligned block of 128 rows (the rows of one device) between 8 and 16 rows name expert 0, and in some block exactly 16 do.
All inputs are finite; a program needn't handle non-finite values.
Results may differ from a plain program's by a relative error of at most 0.02.
Values may be sent and summed in bfloat16 or wider, within the bound.
No kernel may reach another device: no remote copies, remote signals or barrier semaphores. Data moves between devices by JAX's collectives and lax.ppermute only.
A program may use at most 128 MiB of HBM per device.

v0:
```python
import math

import jax
import jax.numpy as jnp
from jax import lax
from jax.sharding import PartitionSpec as P

HQ = 64
HK = 8
DH = 128
CAP = 16


masked_value = -1e30


def attend_piece(state, key_part, value_part, query_rows, first_pos):
    nrows = query_rows.shape[0]
    group = HQ // HK
    scale = 1.0 / math.sqrt(DH)
    plen = key_part.shape[0]
    width = math.gcd(plen, 512)
    count = plen // width
    heads = query_rows.reshape(nrows, HK, group, DH)
    query_pos = first_pos + jnp.arange(nrows, dtype=jnp.int32)
    last_pos = first_pos + nrows - 1
    key_blocks = key_part.reshape(count, width, HK, DH)
    value_blocks = value_part.reshape(count, width, HK, DH)

    def block_step(carry, inputs):
        key_block, value_block, index = inputs
        key_start = index * width

        def compute(current):
            top, total, accum = current
            scores = (
                jnp.einsum("qhgd,khd->qhgk", heads, key_block, preferred_element_type=jnp.float32)
                * scale
            )
            key_pos = key_start + jnp.arange(width, dtype=jnp.int32)
            allowed = (key_pos[None, :] <= query_pos[:, None])[:, None, None, :]
            scores = jnp.where(allowed, scores, masked_value)
            new_top = jnp.maximum(top, jnp.max(scores, axis=-1))
            weights = jnp.where(allowed, jnp.exp(scores - new_top[..., None]), 0.0)
            factor = jnp.exp(top - new_top)
            total = total * factor + jnp.sum(weights, axis=-1)
            update = jnp.einsum(
                "qhgk,khd->qhgd",
                weights.astype(jnp.bfloat16),
                value_block,
                preferred_element_type=jnp.float32,
            )
            accum = accum * factor[..., None] + update
            return (new_top, total, accum)

        carry = lax.cond(key_start <= last_pos, compute, lambda current: current, carry)
        return (carry, None)

    indices = jnp.arange(count, dtype=jnp.int32)
    state, _ = lax.scan(block_step, state, (key_blocks, value_blocks, indices))
    return state


def run_attention(keys, values, row_sets):
    group = HQ // HK
    initial = []
    for query_rows, first_pos in row_sets:
        nrows = query_rows.shape[0]
        initial.append(
            (
                jnp.full((nrows, HK, group), masked_value, jnp.float32),
                jnp.zeros((nrows, HK, group), jnp.float32),
                jnp.zeros((nrows, HK, group, DH), jnp.float32),
            )
        )

    def fold(carry, pieces):
        key_part, value_part = pieces
        return tuple(
            (
                attend_piece(state, key_part, value_part, query_rows, first_pos)
                for state, (query_rows, first_pos) in zip(carry, row_sets)
            )
        )

    final = fold(
        tuple(initial),
        (
            lax.all_gather(keys, "ctx", axis=0, tiled=True),
            lax.all_gather(values, "ctx", axis=0, tiled=True),
        ),
    )
    results = []
    for (top, total, accum), (query_rows, first_pos) in zip(final, row_sets):
        results.append(
            (accum / total[..., None]).reshape(query_rows.shape[0], HQ * DH).astype(jnp.bfloat16)
        )
    return results


def per_device(queries, keys, values, norm_gain, expert_ids, gates, w_gate, w_up, w_down):
    device = lax.axis_index("ctx")
    tokens = queries.shape[0]
    results = run_attention(keys, values, [(queries, device * tokens)])
    attention = results[0]
    wide = attention.astype(jnp.float32)
    factor = lax.rsqrt(jnp.mean(wide * wide, axis=-1, keepdims=True) + 1e-05)
    normed = (wide * factor * norm_gain[None, :]).astype(jnp.bfloat16)
    hits = (expert_ids == 0).astype(jnp.int32)
    chosen = jnp.sum(hits, axis=1)
    slot = jnp.cumsum(chosen) - chosen
    table = jnp.logical_and(
        slot[None, :] == jnp.arange(CAP, dtype=jnp.int32)[:, None], chosen[None, :] > 0
    )
    table = table.astype(jnp.bfloat16)
    picked_rows = jnp.dot(table, normed, preferred_element_type=jnp.float32).astype(jnp.bfloat16)
    piece = lax.all_gather(picked_rows, "ctx", axis=0, tiled=True)
    gate = jnp.dot(piece, w_gate, preferred_element_type=jnp.float32)
    upper = jnp.dot(piece, w_up, preferred_element_type=jnp.float32)
    hidden = (jax.nn.silu(gate) * upper).astype(jnp.bfloat16)
    summed = lax.psum_scatter(
        jnp.dot(hidden, w_down, preferred_element_type=jnp.float32).astype(jnp.bfloat16),
        "ctx",
        scatter_dimension=0,
        tiled=True,
    )
    spread_back = jnp.dot(table.T, summed, preferred_element_type=jnp.float32)
    weight = jnp.sum(gates * hits.astype(jnp.float32), axis=1)
    mixed = (spread_back * weight[:, None]).astype(jnp.bfloat16)
    return (attention, mixed)


def solution(mesh):
    placed = (
        P(("groups", "ctx"), None),
        P(("groups", "ctx"), None),
        P(("groups", "ctx"), None),
        P(),
        P(("groups", "ctx"), None),
        P(("groups", "ctx"), None),
        P(None, "ctx"),
        P(None, "ctx"),
        P("ctx", None),
    )
    return jax.shard_map(
        per_device,
        mesh=mesh,
        in_specs=placed,
        out_specs=(P(("groups", "ctx"), None), P(("groups", "ctx"), None)),
        check_vma=False,
    )
```

profile of v0, /device:TPU:0, one launch (start us, length us, event | category | flops | bytes accessed | tf_op | source)
XLA Modules:
  0.0 366.3 jit_solution(15307245015577546017)
XLA Ops:
  7.2 0.7 all-gather.4.cloned.1.call-update
  7.9 0.7 all-gather.6.cloned.1.call-update
  8.7 3.2 copy.15
  11.9 2.6 copy.17
  14.7 0.2 reduce-window.8
  15.0 48.4 %all-gather.4.cloned.1.call-done = bf16[2048,1024]{1,0:T(8,128)(2,1)} async-done(((bf16[128,1024]{1,0:T(8,128)(2,1)}), bf16[2048,1024]{1,0:T(8,128)(2,1)}) %all-gather.4.cloned.1.call-update) | async-done | bytes 4194320 | tf_op jit(solution)/shard_map/all_gather | solution.py:89
  63.5 3.3 copy.24
  66.7 2.9 copy.16
  69.6 45.1 %all-gather.6.cloned.1.call-done = bf16[2048,1024]{1,0:T(8,128)(2,1)} async-done(((bf16[128,1024]{1,0:T(8,128)(2,1)}), bf16[2048,1024]{1,0:T(8,128)(2,1)}) %all-gather.6.cloned.1.call-update) | async-done | bytes 4194320 | tf_op jit(solution)/shard_map/all_gather | solution.py:90
  114.7 3.3 copy.25
  118.0 2.9 copy.18
  120.9 2.5 broadcast_in_dim.48
  123.3 22.6 %while.15 = (s32[]{:T(128)}, f32[128,8,8]{0,2,1:T(8,128)S(1)}, f32[128,8,8]{0,2,1:T(8,128)S(1)}, f32[128,8,8,128]{3,0,2,1:T(8,128)}, s32[4]{0:T(128)S(1)}, /*ind...) while((s32[]{:T(128)}, f32[128,8,8]{0,2,1:T(8,128)S(1)}, ...), condition=%wide.region_5.6_spmd.clone, body=%wide.region_0.5_spmd.clone.sunk | while | flops 2204189184 | bytes 63708456 | solution.py:60
  123.3 0.6 dynamic_slice.33
  124.6 17.5 %conditional.3 = ((f32[128,8,8]{0,2,1:T(8,128)S(1)}, f32[128,8,8]{0,2,1:T(8,128)S(1)}, f32[128,8,8,128]{3,0,2,1:T(8,128)})) conditional(s32[]{:T(128)} %convert_element_type.79, (f32[128,8,8]{0,2,1:T(8,128)S(1)}, f32[128,8,8]{0,2,1:T(8,128)S(1)}, f32[128,8,8,128]{3,0,2,1:T(8,128)}) %tuple.44, (s32[]{:T(128)}, s32[]{:T(128)}, ...), branch_computations={%region_1.1_spmd, %region_2.4_spmd} | conditional | flops 2204189184 | bytes 63707688 | solution.py:56
  124.8 4.2 %fusion.2 = (f32[128,8,8]{0,2,1:T(8,128)S(1)}, f32[8,512,128,8]{2,1,3,0:T(8,128)S(1)}) fusion(pred[128,512]{0,1:T(8,128)(4,1)S(1)} %broadcast_compare_fusion, bf16[128,8,8,128]{3,0,2,1:T(8,128)(2,1)} %get-tuple-element.116, bf16[4,512,8,128]{3,1,2,0:T(8,128)(2,1)} %get-tuple-element.114, s32[]{:T(128)} %get-tuple-element.115), kind=kOutput, calls=%fused_computation.3 | convolution fusion | flops 1086316544 | bytes 20021760 | tf_op jit(solution)/shard_map/while/body/eval_jaxpr/cond/branch_1_fun/qhgd,khd->qhgk/dot_general | solution.py:37
  129.0 4.2 %fusion.4 = f32[128,8,8]{0,2,1:T(8,128)S(1)} fusion(f32[8,512,128,8]{2,1,3,0:T(8,128)S(1)} %get-tuple-element.204, f32[128,8,8]{0,2,1:T(8,128)S(1)} %max.4, pred[128,512]{0,1:T(8,128)(4,1)S(1)} %broadcast_compare_fusion), kind=kLoop, calls=%fused_computation.5 | loop fusion | flops 20963328 | bytes 16908288 | tf_op jit(solution)/shard_map/while/body/eval_jaxpr/cond/branch_1_fun/reduce_sum | solution.py:46
  133.3 8.8 %bitcast_add_fusion = f32[128,8,8,128]{3,0,2,1:T(8,128)} fusion(f32[128,8,8,128]{3,0,2,1:T(8,128)} %get-tuple-element.118, f32[8,512,128,8]{2,1,3,0:T(8,128)S(1)} %get-tuple-element.204, f32[128,8,8]{0,2,1:T(8,128)S(1)} %max.4, pred[128,512]{0,1:T(8,128)(4,1)S(1)} %broadcast_compare_fusion, f32[128,8,8]{0,2,1:T(8,128)S(1)} %get-tuple-element.200, ...), kind=kOutput, calls=%fused_computation.8 | convolution fusion | flops 1096810496 | bytes 26345984 | tf_op jit(solution)/shard_map/while/body/eval_jaxpr/cond/branch_1_fun/qhgk,khd->qhgd/dot_general | solution.py:47
  142.1 0.6 dynamic_slice.33
  143.4 0.6 dynamic_slice.33
  144.7 0.6 dynamic_slice.33
  146.0 3.2 multiply_reduce_fusion
  149.2 1.4 copy.19
  150.6 1.8 copy.28
  152.4 1.3 copy-done
  153.7 1.4 convolution_convert_fusion.1
  155.1 101.7 %all-gather.8.cloned.1.call-done = bf16[256,8192]{1,0:T(8,128)(2,1)} async-done(((bf16[16,8192]{1,0:T(8,128)(2,1)}), bf16[256,8192]{1,0:T(8,128)(2,1)}) %all-gather.8.cloned.1.call-update) | async-done | bytes 4194320 | tf_op jit(solution)/shard_map/all_gather | solution.py:117
  256.8 8.8 %fusion.39 = f32[256,768]{1,0:T(8,128)S(1)} fusion(bf16[256,8192]{1,0:T(8,128)(2,1)} %all-gather.8.cloned.1.call-done, bf16[8192,768]{1,0:T(8,128)(2,1)} %param.19), kind=kOutput, calls=%fused_computation.54 | convolution fusion | flops 3221225472 | bytes 17563648 | tf_op jit(solution)/shard_map/dot_general | solution.py:118
  265.7 19.9 %convolution_convert_fusion = bf16[256,8192]{1,0:T(8,128)(2,1)} fusion(bf16[768,8192]{1,0:T(8,128)(2,1)} %param.21, bf16[256,8192]{1,0:T(8,128)(2,1)} %all-gather.8.cloned.1.call-done, bf16[8192,768]{1,0:T(8,128)(2,1)} %param.20, f32[256,768]{1,0:T(8,128)S(1)} %fusion.39), kind=kOutput, calls=%fused_computation.24 | convolution fusion | flops 6445727744 | bytes 34340864 | tf_op jit(solution)/shard_map/dot_general | solution.py:122
  285.6 0.6 copy-done.2
  286.3 70.4 %reduce-scatter.2.cloned.1.call-done = bf16[16,8192]{1,0:T(8,128)(2,1)} async-done(((bf16[256,8192]{1,0:T(8,128)(2,1)}), bf16[16,8192]{1,0:T(8,128)(2,1)}) %reduce-scatter.2.cloned.1.call-update) | async-done | bytes 262160 | tf_op jit(solution)/shard_map/reduce_scatter | solution.py:121
  356.7 3.0 fusion.20
  (45 shorter events, 0.7 us)
Async XLA Ops:
  7.2 56.3 %all-gather.4.cloned.1.call-start = ((), (), s32[]{:S(2)}) async-start(), calls=%async_computation.1 | async-start | bytes 4456448 | tf_op jit(solution)/shard_map/all_gather | solution.py:89
  7.9 106.8 %all-gather.6.cloned.1.call-start = ((), (), s32[]{:S(2)}) async-start(), calls=%async_computation.2 | async-start | bytes 4456448 | tf_op jit(solution)/shard_map/all_gather | solution.py:90
  8.6 248.2 %all-gather.8.cloned.1.call-start = ((), (), s32[]{:S(2)}) async-start(), calls=%async_computation.3 | async-start | bytes 4456448 | tf_op jit(solution)/shard_map/all_gather | solution.py:117
  8.7 5.8 %copy-start.1 = (s32[128,2]{0,1:T(2,128)S(1)}, s32[128,2]{0,1:T(2,128)}, u32[]{:S(2)}) copy-start(s32[128,2]{0,1:T(2,128)} %param.17) | copy-start | bytes 3076
  15.0 137.4 %copy-start.4 = (s32[128]{0:T(128)}, s32[128]{0:T(128)S(1)}, u32[]{:S(2)}) copy-start(s32[128]{0:T(128)S(1)} %sub.28) | copy-start | bytes 1540
  15.0 137.4 %copy-start.6 = (pred[128]{0:T(512)(128)(4,1)}, pred[128]{0:T(512)(128)(4,1)S(1)}, u32[]{:S(2)}) copy-start(pred[128]{0:T(512)(128)(4,1)S(1)} %broadcast_compare_fusion.1) | copy-start | bytes 388
  149.2 4.5 %copy-start.8 = (f32[8192]{0:T(1024)S(1)}, f32[8192]{0:T(1024)}, u32[]{:S(2)}) copy-start(f32[8192]{0:T(1024)} %param.16) | copy-start | bytes 98308
  152.3 1.3 copy-start
  155.1 201.6 %reduce-scatter.2.cloned.1.call-start = ((), (), s32[]{:S(2)}) async-start(), calls=%async_computation.4 | async-start | bytes 4456448 | tf_op jit(solution)/shard_map/reduce_scatter | solution.py:121
  285.6 0.7 copy-start.2
  285.6 0.7 copy-start.3
  285.6 71.1 %copy-start.5 = (s32[128]{0:T(128)S(1)}, s32[128]{0:T(128)}, u32[]{:S(2)}) copy-start(s32[128]{0:T(128)} %copy-done.4) | copy-start | bytes 1540
  285.6 71.1 %copy-start.7 = (pred[128]{0:T(512)(128)(4,1)S(1)}, pred[128]{0:T(512)(128)(4,1)}, u32[]{:S(2)}) copy-start(pred[128]{0:T(512)(128)(4,1)} %copy-done.6) | copy-start | bytes 388
Sparse Core Ops, SparseCore 0:
  10.2 53.2 all-gather.3
  65.6 49.0 all-gather.5
  155.2 101.5 all-gather.7
  285.7 70.9 reduce-scatter.1
where the time goes:
time: 367 us; the launch traced here: 366 us
  waiting for transfers between devices  267 us (73%)
  matrix products  46.1 us (13%)
  local copies, waits for them, and re-layouts  28.2 us (8%)
  between operations  13.9 us (4%)
  other arithmetic  7.95 us (2%)
    all_gather x1, waiting for transfers between devices, per_device(): piece = lax.all_gather(picked_rows, 'ctx', axis=0, tiled=True)  102 us
    reduce_scatter x1, waiting for transfers between devices, per_device(): lax.psum_scatter(jnp.dot(hidden, w_down, preferred_element_type=jnp.float...  70.4 us
    all_gather x1, waiting for transfers between devices, run_attention(): lax.all_gather(keys, 'ctx', axis=0, tiled=True)  48.4 us
    all_gather x1, waiting for transfers between devices, run_attention(): lax.all_gather(values, 'ctx', axis=0, tiled=True)  45.1 us
    unnamed x25, local copies, waits for them, and re-layouts  21.9 us
    dot_general x1, matrix products, per_device(): jnp.dot(hidden, w_down, preferred_element_type=jnp.float32)  19.9 us
    dot_general x1, matrix products, compute(): jnp.einsum('qhgk,khd->qhgd', weights.astype(jnp.bfloat16), value_block, p...  8.84 us
    dot_general x1, matrix products, per_device(): gate = jnp.dot(piece, w_gate, preferred_element_type=jnp.float32)  8.83 us
  transfers between devices with their start and end apart: 4, of which 4 were waited for; matrix products, arithmetic and copies ran while one was open for 3% of the time, Pallas kernels for 0%

commit v1 on v0

v1 whole, which is shorter than its diff:
```python
import functools
import math

import jax
import jax.numpy as jnp
from jax import lax
from jax.experimental import pallas as pl
from jax.experimental.pallas import tpu as pltpu
from jax.sharding import PartitionSpec as P

HQ = 64
HK = 8
DH = 128
CAP = 16
GROUP = HQ // HK
WIDE = GROUP * DH
LOG_SCALE = math.log2(math.e) / math.sqrt(DH)
MASKED = -1e30
STACK = 2
MIB = 1 << 20


def ring_order(chips):
    return list(range(0, chips, 2)) + list(range(1, chips, 2))[::-1]


def permutations(chips):
    order = ring_order(chips)
    right, left = [], []
    for place in range(chips):
        here, there = order[place], order[(place + 1) % chips]
        for core in range(2):
            right.append((2 * here + core, 2 * there + core))
            left.append((2 * there + core, 2 * here + core))
    sibling = [(i, i ^ 1) for i in range(2 * chips)]
    return right, left, sibling


def chip_at(me, step, chips):
    chip = me // 2
    place = jnp.where(chip % 2 == 0, chip // 2, chips - 1 - chip // 2)
    source = (place - step + 2 * chips) % chips
    return jnp.where(source < chips // 2, 2 * source, 2 * (chips - 1 - source) + 1)


def head_rows(q_ref, first):
    return jnp.concatenate(
        [q_ref[:, h * DH : (h + 1) * DH] for h in range(first, first + STACK)], axis=0
    )


def with_ones(values):
    return jnp.concatenate([values, jnp.ones_like(values)], axis=1)


def scores_of(queries, keys):
    return LOG_SCALE * lax.dot_general(
        queries, keys, (((1,), (1,)), ((), ())), preferred_element_type=jnp.float32
    )


def pack_stats(tops, totals, tokens):
    lane = lax.broadcasted_iota(jnp.int32, (tokens, DH), 1)
    tile = jnp.zeros((tokens, DH), jnp.float32)
    for h in range(GROUP):
        tile = jnp.where(lane == h, tops[h], tile)
        tile = jnp.where(lane == GROUP + h, totals[h], tile)
    return tile


def split_heads(stacked, tokens):
    return [stacked[i * tokens : (i + 1) * tokens] for i in range(STACK)]


def own_kernel(me_ref, q_ref, key_ref, value_ref, sib_key_ref, sib_value_ref, acc_ref, stat_ref):
    tokens = q_ref.shape[0]
    keys = jnp.concatenate([key_ref[...], sib_key_ref[...]], axis=0)
    values = with_ones(jnp.concatenate([value_ref[...], sib_value_ref[...]], axis=0))
    shape = (STACK * tokens, 2 * tokens)
    token = lax.broadcasted_iota(jnp.int32, shape, 0) % tokens
    column = lax.broadcasted_iota(jnp.int32, shape, 1)
    limit = jnp.where(me_ref[0] % 2 == 1, 2 * tokens, tokens)
    allowed = column <= jnp.where(column < tokens, token, limit - 1)
    tops, totals = [], []
    for first in range(0, GROUP, STACK):
        scores = jnp.where(allowed, scores_of(head_rows(q_ref, first), keys), MASKED)
        top = jnp.max(scores, axis=1, keepdims=True)
        weights = jnp.exp2(scores - top).astype(jnp.bfloat16)
        update = jnp.dot(weights, values, preferred_element_type=jnp.float32)
        acc_ref[0, first * tokens : (first + STACK) * tokens, :] = update[:, :DH]
        tops += split_heads(top, tokens)
        totals += split_heads(update[:, DH:], tokens)
    stat_ref[0] = pack_stats(tops, totals, tokens)


def fold_chip(q_ref, keys, values, acc_ref, stat_ref):
    tokens = q_ref.shape[0]
    values = with_ones(values)
    tops, totals = [], []
    stats = stat_ref[0]
    for first in range(0, GROUP, STACK):
        scores = scores_of(head_rows(q_ref, first), keys)
        old = jnp.concatenate([stats[:, h : h + 1] for h in range(first, first + STACK)], axis=0)
        total = jnp.concatenate(
            [stats[:, GROUP + h : GROUP + h + 1] for h in range(first, first + STACK)], axis=0
        )
        top = jnp.maximum(old, jnp.max(scores, axis=1, keepdims=True))
        factor = jnp.exp2(old - top)
        weights = jnp.exp2(scores - top).astype(jnp.bfloat16)
        update = jnp.dot(weights, values, preferred_element_type=jnp.float32)
        rows = slice(first * tokens, (first + STACK) * tokens)
        acc_ref[0, rows, :] = acc_ref[0, rows, :] * factor + update[:, :DH]
        tops += split_heads(top, tokens)
        totals += split_heads(total * factor + update[:, DH:], tokens)
    stat_ref[0] = pack_stats(tops, totals, tokens)


def step_kernel(chips, step, me_ref, q_ref, *refs):
    (rk, rv, rsk, rsv, lk, lv, lsk, lsv, acc_in, stat_in, acc_ref, stat_ref) = refs
    me = me_ref[0]
    acc_ref[...] = acc_in[...]
    stat_ref[...] = stat_in[...]
    for place, key, value, sib_key, sib_value in (
        (step, rk, rv, rsk, rsv),
        (-step, lk, lv, lsk, lsv),
    ):

        @pl.when(chip_at(me, place, chips) < me // 2)
        def _():
            keys = jnp.concatenate([key[...], sib_key[...]], axis=0)
            values = jnp.concatenate([value[...], sib_value[...]], axis=0)
            fold_chip(q_ref, keys, values, acc_ref, stat_ref)


def last_kernel(chips, me_ref, q_ref, *refs):
    (key, value, sib_key, sib_value, acc_in, stat_in, gain_ref, table_ref) = refs[:8]
    (out_ref, low_ref, high_ref, acc_ref, stat_ref) = refs[8:]
    tokens = q_ref.shape[0]
    head = pl.program_id(0)
    me = me_ref[0]
    acc_ref[...] = acc_in[...]
    stat_ref[...] = stat_in[...]

    @pl.when(chip_at(me, chips // 2, chips) < me // 2)
    def _():
        keys = jnp.concatenate([key[...], sib_key[...]], axis=0)
        values = jnp.concatenate([value[...], sib_value[...]], axis=0)
        fold_chip(q_ref, keys, values, acc_ref, stat_ref)

    stats = stat_ref[0]
    pieces = []
    for h in range(GROUP):
        total = stats[:, GROUP + h : GROUP + h + 1]
        pieces.append((acc_ref[0, h * tokens : (h + 1) * tokens, :] / total).astype(jnp.bfloat16))
    columns = pl.ds(pl.multiple_of(head * WIDE, WIDE), WIDE)
    out_ref[:, columns] = jnp.concatenate(pieces, axis=1)

    @pl.when(head == HK - 1)
    def _():
        width = out_ref.shape[1]
        picked = jnp.dot(table_ref[...], out_ref[...], preferred_element_type=jnp.float32)
        mean = jnp.sum(picked * picked, axis=1, keepdims=True) / width
        normed = (picked * lax.rsqrt(mean + 1e-05) * gain_ref[...]).astype(jnp.bfloat16)
        low_ref[...] = normed[:, : width // 2]
        high_ref[...] = normed[:, width // 2 :]


def attention_calls(me, queries, gain, table, chips, own, steps, opposite):
    tokens, width = queries.shape
    half = chips // 2
    head_block = pl.BlockSpec((tokens, WIDE), lambda g, me: (0, g))
    kv_block = pl.BlockSpec((tokens, DH), lambda g, me: (0, g))
    acc_block = pl.BlockSpec((1, GROUP * tokens, DH), lambda g, me: (g, 0, 0))
    stat_block = pl.BlockSpec((1, tokens, DH), lambda g, me: (g, 0, 0))
    state_shapes = [
        jax.ShapeDtypeStruct((HK, GROUP * tokens, DH), jnp.float32),
        jax.ShapeDtypeStruct((HK, tokens, DH), jnp.float32),
    ]
    params = pltpu.CompilerParams(
        dimension_semantics=("arbitrary",), vmem_limit_bytes=24 * MIB
    )

    def cost(keys):
        return pl.CostEstimate(
            flops=4 * tokens * width * keys, bytes_accessed=12 * MIB, transcendentals=tokens * HQ * keys
        )

    state = pl.pallas_call(
        own_kernel,
        grid_spec=pltpu.PrefetchScalarGridSpec(
            num_scalar_prefetch=1,
            grid=(HK,),
            in_specs=[head_block] + [kv_block] * 4,
            out_specs=[acc_block, stat_block],
        ),
        out_shape=state_shapes,
        compiler_params=params,
        cost_estimate=cost(2 * tokens),
        name="attend_own",
    )(me, queries, *own)
    for step, pieces in enumerate(steps, start=1):
        state = pl.pallas_call(
            functools.partial(step_kernel, chips, step),
            grid_spec=pltpu.PrefetchScalarGridSpec(
                num_scalar_prefetch=1,
                grid=(HK,),
                in_specs=[head_block] + [kv_block] * 8 + [acc_block, stat_block],
                out_specs=[acc_block, stat_block],
            ),
            out_shape=state_shapes,
            compiler_params=params,
            cost_estimate=cost(4 * tokens),
            name="attend_step",
        )(me, queries, *pieces, *state)
    whole = lambda shape: pl.BlockSpec(shape, lambda g, me: (0, 0))
    return pl.pallas_call(
        functools.partial(last_kernel, chips),
        grid_spec=pltpu.PrefetchScalarGridSpec(
            num_scalar_prefetch=1,
            grid=(HK,),
            in_specs=[head_block]
            + [kv_block] * 4
            + [acc_block, stat_block, whole((1, width)), whole((CAP, tokens))],
            out_specs=[whole((tokens, width)), whole((CAP, width // 2)), whole((CAP, width // 2))],
            scratch_shapes=[
                pltpu.VMEM((1, GROUP * tokens, DH), jnp.float32),
                pltpu.VMEM((1, tokens, DH), jnp.float32),
            ],
        ),
        out_shape=[
            jax.ShapeDtypeStruct((tokens, width), jnp.bfloat16),
            jax.ShapeDtypeStruct((CAP, width // 2), jnp.bfloat16),
            jax.ShapeDtypeStruct((CAP, width // 2), jnp.bfloat16),
        ],
        compiler_params=params,
        cost_estimate=cost(2 * tokens),
        name="attend_last",
    )(me, queries, *opposite, *state, gain, table)


def expert_kernel(count, depth_steps, *refs):
    lows, highs = refs[:count], refs[count : 2 * count]
    gate_ref, up_ref, down_ref, own_ref, sib_ref = refs[2 * count : 2 * count + 5]
    rows_ref, gate_sum, up_sum, hidden_ref, sems = refs[2 * count + 5 :]
    step = pl.program_id(0)
    half = rows_ref.shape[1] // 2
    depth = gate_ref.shape[0]

    @pl.when(step == 0)
    def _():
        copies = []
        for side, blocks in enumerate((lows, highs)):
            for j, block in enumerate(blocks):
                target = rows_ref.at[pl.ds(j * CAP, CAP), pl.ds(side * half, half)]
                copies.append(pltpu.make_async_copy(block, target, sems.at[side * count + j]))
        for copy in copies:
            copy.start()
        for copy in copies:
            copy.wait()
        gate_sum[...] = jnp.zeros_like(gate_sum)
        up_sum[...] = jnp.zeros_like(up_sum)

    @pl.when(step < depth_steps)
    def _():
        columns = pl.ds(pl.multiple_of(step * depth, depth), depth)
        part = rows_ref[:, columns]
        gate_sum[...] += jnp.dot(part, gate_ref[...], preferred_element_type=jnp.float32)
        up_sum[...] += jnp.dot(part, up_ref[...], preferred_element_type=jnp.float32)

    @pl.when(step == depth_steps - 1)
    def _():
        gate = gate_sum[...]
        hidden_ref[...] = (gate / (1.0 + jnp.exp(-gate)) * up_sum[...]).astype(jnp.bfloat16)

    @pl.when(step >= depth_steps)
    def _():
        part = jnp.dot(hidden_ref[...], down_ref[...], preferred_element_type=jnp.float32)
        part = part.astype(jnp.bfloat16)
        middle = part.shape[0] // 2
        own_ref[...] = part[:middle]
        sib_ref[...] = part[middle:]


def expert_call(lows, highs, w_gate, w_up, w_down):
    count = len(lows)
    rows = count * CAP
    width, units = w_gate.shape
    depth = min(1024, width)
    depth_steps = width // depth
    cols = min(1024, width)
    out_steps = width // cols
    weight_block = pl.BlockSpec((depth, units), lambda i: (jnp.minimum(i, depth_steps - 1), 0))
    down_block = pl.BlockSpec((units, cols), lambda i: (0, jnp.maximum(i - depth_steps, 0)))
    out_block = pl.BlockSpec((rows // 2, cols), lambda i: (0, jnp.maximum(i - depth_steps, 0)))
    anywhere = pl.BlockSpec(memory_space=pl.ANY)
    return pl.pallas_call(
        functools.partial(expert_kernel, count, depth_steps),
        grid=(depth_steps + out_steps,),
        in_specs=[anywhere] * (2 * count) + [weight_block, weight_block, down_block],
        out_specs=[out_block, out_block],
        out_shape=[jax.ShapeDtypeStruct((rows // 2, width), jnp.bfloat16)] * 2,
        scratch_shapes=[
            pltpu.VMEM((rows, width), jnp.bfloat16),
            pltpu.VMEM((rows, units), jnp.float32),
            pltpu.VMEM((rows, units), jnp.float32),
            pltpu.VMEM((rows, units), jnp.bfloat16),
            pltpu.SemaphoreType.DMA((2 * count,)),
        ],
        compiler_params=pltpu.CompilerParams(
            dimension_semantics=("arbitrary",), vmem_limit_bytes=40 * MIB
        ),
        cost_estimate=pl.CostEstimate(
            flops=6 * rows * width * units,
            bytes_accessed=6 * width * units + 4 * rows * width,
            transcendentals=rows * units,
        ),
        name="expert",
    )(*lows, *highs, w_gate, w_up, w_down)


def spread_kernel(own_ref, sib_ref, right_ref, left_ref, table_ref, weight_ref, out_ref):
    total = own_ref[...].astype(jnp.float32) + sib_ref[...].astype(jnp.float32)
    total += right_ref[...].astype(jnp.float32) + left_ref[...].astype(jnp.float32)
    spread = lax.dot_general(
        table_ref[...],
        total.astype(jnp.bfloat16),
        (((0,), (0,)), ((), ())),
        preferred_element_type=jnp.float32,
    )
    out_ref[...] = (spread * weight_ref[...]).astype(jnp.bfloat16)


def spread_call(own, sib, right, left, table, weight):
    tokens = table.shape[1]
    width = own.shape[1]
    cols = min(2048, width)
    block = pl.BlockSpec((CAP, cols), lambda i: (0, i))
    return pl.pallas_call(
        spread_kernel,
        grid=(width // cols,),
        in_specs=[block] * 4
        + [pl.BlockSpec((CAP, tokens), lambda i: (0, 0)), pl.BlockSpec((tokens, 1), lambda i: (0, 0))],
        out_specs=pl.BlockSpec((tokens, cols), lambda i: (0, i)),
        out_shape=jax.ShapeDtypeStruct((tokens, width), jnp.bfloat16),
        compiler_params=pltpu.CompilerParams(dimension_semantics=("arbitrary",)),
        name="spread",
    )(own, sib, right, left, table, weight)


def add(a, b):
    return (a.astype(jnp.float32) + b.astype(jnp.float32)).astype(jnp.bfloat16)


def per_device(chips, queries, keys, values, norm_gain, expert_ids, gates, w_gate, w_up, w_down):
    right, left, sibling = permutations(chips)
    half = chips // 2
    go_right = lambda x: lax.ppermute(x, "ctx", right)
    go_left = lambda x: lax.ppermute(x, "ctx", left)
    swap = lambda x: lax.ppermute(x, "ctx", sibling)

    me = lax.axis_index("ctx").astype(jnp.int32).reshape(1)
    tokens = queries.shape[0]
    hits = (expert_ids == 0).astype(jnp.float32)
    chosen = jnp.sum(hits, axis=1)
    position = jnp.arange(tokens, dtype=jnp.int32)
    before = (position[None, :] < position[:, None]).astype(jnp.float32)
    slot = jnp.sum(before * chosen[None, :], axis=1).astype(jnp.int32)
    table = jnp.logical_and(
        slot[None, :] == jnp.arange(CAP, dtype=jnp.int32)[:, None], chosen[None, :] > 0
    ).astype(jnp.bfloat16)
    weight = jnp.sum(gates * hits, axis=1, keepdims=True)

    own = (keys, values, swap(keys), swap(values))
    from_left, from_right = (keys, values), (keys, values)
    steps = []
    for _ in range(1, half):
        from_left = tuple(go_right(x) for x in from_left)
        from_right = tuple(go_left(x) for x in from_right)
        steps.append(
            (*from_left, *(swap(x) for x in from_left), *from_right, *(swap(x) for x in from_right))
        )
    far_keys, far_values = go_right(from_left[0]), go_left(from_right[1])
    opposite = (far_keys, far_values, swap(far_keys), swap(far_values))
    attention, low, high = attention_calls(
        me, queries, norm_gain[None, :], table, chips, own, steps, opposite
    )

    lows_right, highs_right, lows_left, highs_left = [low], [high], [low], [high]
    for _ in range(1, half):
        lows_right.append(go_right(lows_right[-1]))
        highs_right.append(go_right(highs_right[-1]))
        lows_left.append(go_left(lows_left[-1]))
        highs_left.append(go_left(highs_left[-1]))
    lows = lows_right + lows_left[1:] + [go_right(lows_right[-1])]
    highs = highs_right + highs_left[1:] + [go_left(highs_left[-1])]
    lows += [swap(x) for x in lows]
    highs += [swap(x) for x in highs]
    mine, theirs = expert_call(lows, highs, w_gate, w_up, w_down)

    other = swap(theirs)
    width = mine.shape[1]

    def block(index):
        rows = slice(index * CAP, (index + 1) * CAP)
        return mine[rows].astype(jnp.float32) + other[rows].astype(jnp.float32)

    far = block(chips - 1).astype(jnp.bfloat16)
    to_right = go_right(far[:, : width // 2])
    to_left = go_left(far[:, width // 2 :])
    for distance in range(half - 1, 0, -1):
        ahead, back = block(half - 1 + distance), block(distance)
        if distance == half - 1:
            ahead = jnp.concatenate(
                [ahead[:, : width // 2] + to_right.astype(jnp.float32), ahead[:, width // 2 :]], axis=1
            )
            back = jnp.concatenate(
                [back[:, : width // 2], back[:, width // 2 :] + to_left.astype(jnp.float32)], axis=1
            )
        else:
            ahead = ahead + to_right.astype(jnp.float32)
            back = back + to_left.astype(jnp.float32)
        to_right = go_right(ahead.astype(jnp.bfloat16))
        to_left = go_left(back.astype(jnp.bfloat16))
    mixed = spread_call(mine[:CAP], other[:CAP], to_right, to_left, table, weight)
    return (attention, mixed)


def solution(mesh):
    placed = (
        P(("groups", "ctx"), None),
        P(("groups", "ctx"), None),
        P(("groups", "ctx"), None),
        P(),
        P(("groups", "ctx"), None),
        P(("groups", "ctx"), None),
        P(None, "ctx"),
        P(None, "ctx"),
        P("ctx", None),
    )
    return jax.shard_map(
        functools.partial(per_device, mesh.shape["ctx"] // 2),
        mesh=mesh,
        in_specs=placed,
        out_specs=(P(("groups", "ctx"), None), P(("groups", "ctx"), None)),
        check_vma=False,
    )
```

time: 367 us -> 273 us (0.74)
  waiting for transfers between devices: 267 us -> 80.5 us
  starting transfers between devices: 0.16 us -> 128 us
  Pallas kernels: 0 us -> 49.4 us
  matrix products: 46.1 us -> 0 us
  local copies, waits for them, and re-layouts: 28.2 us -> 11.4 us
  between operations: 13.9 us -> 0.98 us
  other arithmetic: 7.95 us -> 1.48 us
    all_gather x3 -> x0, waiting for transfers between devices: 195 us -> none  [the longest x1 102 us: per_device(): piece = lax.all_gather(picked_rows, 'ctx', axis=0, tiled=True)]
    ppermute x0 -> x69, starting transfers between devices: none -> 128 us  [the longest x18 92.4 us: per_device(): go_right = lambda x: lax.ppermute(x, 'ctx', right)]
    ppermute x0 -> x69, waiting for transfers between devices: none -> 80.5 us  [the longest x18 39.3 us: per_device(): go_left = lambda x: lax.ppermute(x, 'ctx', left)]
    reduce_scatter x1 -> x0, waiting for transfers between devices: 70.4 us -> none  [per_device(): lax.psum_scatter(jnp.dot(hidden, w_down, preferred_element_type=jnp.float...]
    pallas_call x0 -> x7, Pallas kernels: none -> 49.4 us  [the longest x1 25.8 us: expert_call(): pl.pallas_call(functools.partial(expert_kernel, count, depth_steps), grid...]
    dot_general x6 -> x0, matrix products: 46.1 us -> none  [the longest x1 19.9 us: per_device(): jnp.dot(hidden, w_down, preferred_element_type=jnp.float32)]
    unnamed x25 -> x28, local copies, waits for them, and re-layouts: 21.9 us -> 8.21 us
    reduce_sum x4 -> x2, other arithmetic: 7.49 us -> 0.82 us  [the longest x1 0.71 us: per_device(): weight = jnp.sum(gates * hits, axis=1, keepdims=True)]
  transfers between devices with their start and end apart: 4 -> 69, of which waited for: 4 -> 23; matrix products, arithmetic and copies ran while one was open for 3% -> 2% of each run, Pallas kernels for 0% -> 5%
where the time goes in v1:
time: 273 us; the launch traced here: 272 us
  starting transfers between devices  128 us (47%)
  waiting for transfers between devices  80.5 us (29%)
  Pallas kernels  49.4 us (18%)
  local copies, waits for them, and re-layouts  11.4 us (4%)
    ppermute x18, starting transfers between devices, per_device(): go_right = lambda x: lax.ppermute(x, 'ctx', right)  92.4 us
    ppermute x18, waiting for transfers between devices, per_device(): go_left = lambda x: lax.ppermute(x, 'ctx', left)  39.3 us
    ppermute x18, waiting for transfers between devices, per_device(): go_right = lambda x: lax.ppermute(x, 'ctx', right)  36.3 us
    ppermute x18, starting transfers between devices, per_device(): go_left = lambda x: lax.ppermute(x, 'ctx', left)  30.6 us
    pallas_call x1, Pallas kernels, expert_call(): pl.pallas_call(functools.partial(expert_kernel, count, depth_steps), grid...  25.8 us
    pallas_call x3, Pallas kernels, attention_calls(): pl.pallas_call(functools.partial(step_kernel, chips, step), grid_spec=plt...  9.26 us
    unnamed x28, local copies, waits for them, and re-layouts  8.21 us
    pallas_call x1, Pallas kernels, attention_calls(): pl.pallas_call(own_kernel, grid_spec=pltpu.PrefetchScalarGridSpec(num_sca...  5.57 us
  transfers between devices with their start and end apart: 69, of which 23 were waited for; matrix products, arithmetic and copies ran while one was open for 2% of the time, Pallas kernels for 5%

profile of v1, /device:TPU:0, one launch (start us, length us, event | category | flops | bytes accessed | tf_op | source)
XLA Modules:
  0.0 272.0 jit_solution(8182869550715748088)
XLA Ops:
  1.1 2.6 collective-permute-start
  6.6 4.5 %collective-permute-done.refs_0_ = bf16[128,1024]{1,0:T(8,128)(2,1)S(1)} collective-permute-done((bf16[128,1024]{1,0:T(8,128)(2,1)}, bf16[128,1024]{1,0:T(8,128)(2,1)S(1)}, u32[]{:S(2)}, u32[]{:S(2)}) %collective-permute-start) | collective-permute-done | bytes 262176 | tf_op jit(solution)/shard_map/ppermute | solution.py:357
  11.1 5.4 %collective-permute-done.10.refs_1_ = bf16[128,1024]{1,0:T(8,128)(2,1)S(1)} collective-permute-done((bf16[128,1024]{1,0:T(8,128)(2,1)}, bf16[128,1024]{1,0:T(8,128)(2,1)S(1)}, u32[]{:S(2)}, u32[]{:S(2)}) %collective-permute-start.10) | collective-permute-done | bytes 262176 | tf_op jit(solution)/shard_map/ppermute | solution.py:357
  17.7 1.8 collective-permute-start.1
  21.8 5.0 %collective-permute-done.1.refs_0_ = bf16[128,1024]{1,0:T(8,128)(2,1)S(1)} collective-permute-done((bf16[128,1024]{1,0:T(8,128)(2,1)S(1)}, bf16[128,1024]{1,0:T(8,128)(2,1)S(1)}, u32[]{:S(2)}, u32[]{:S(2)}) %collective-permute-start.1) | collective-permute-done | bytes 262176 | tf_op jit(solution)/shard_map/ppermute | solution.py:357
  27.6 1.8 collective-permute-start.2
  29.4 2.8 %collective-permute-done.11.refs_1_ = bf16[128,1024]{1,0:T(8,128)(2,1)S(1)} collective-permute-done((bf16[128,1024]{1,0:T(8,128)(2,1)S(1)}, bf16[128,1024]{1,0:T(8,128)(2,1)S(1)}, u32[]{:S(2)}, u32[]{:S(2)}) %collective-permute-start.11) | collective-permute-done | bytes 262176 | tf_op jit(solution)/shard_map/ppermute | solution.py:357
  32.8 2.4 collective-permute-done.5.refs_5_
  40.2 4.9 %collective-permute-done.6.refs_5_ = bf16[128,1024]{1,0:T(8,128)(2,1)} collective-permute-done((bf16[128,1024]{1,0:T(8,128)(2,1)S(1)}, bf16[128,1024]{1,0:T(8,128)(2,1)}, u32[]{:S(2)}, u32[]{:S(2)}) %collective-permute-start.6) | collective-permute-done | bytes 262176 | tf_op jit(solution)/shard_map/ppermute | solution.py:358
  50.9 5.6 %attend_own.1 = (f32[8,1024,128]{2,1,0:T(8,128)S(1)}, f32[8,128,128]{2,1,0:T(8,128)S(1)}) custom-call(s32[1]{0:T(128)} %bitcast.me_ref, bf16[128,8192]{1,0:T(8,128)(2,1)S(1)} %copy-done, bf16[128,1024]{1,0:T(8,128)(2,1)S(1)} %copy-done.5, bf16[128,1024]{1,0:T(8,128)(2,1)S(1)} %copy-done.6, bf16[128,1024]{1,0:T(8,128)(2,1)S(1)} %copy-done.8, ...), custom_call_target="tpu_custom_call" | custom-call | flops 1073741824 | bytes 12582912 | tf_op jit(solution)/shard_map/attend_own/pallas_call | solution.py:188
  59.2 3.9 %attend_step.4 = (f32[8,1024,128]{2,1,0:T(8,128)S(1)}, f32[8,128,128]{2,1,0:T(8,128)S(1)}) custom-call(s32[1]{0:T(128)} %bitcast.me_ref, bf16[128,8192]{1,0:T(8,128)(2,1)S(1)} %copy-done, bf16[128,1024]{1,0:T(8,128)(2,1)S(1)} %collective-permute-done.1.refs_0_, bf16[128,1024]{1,0:T(8,128)(2,1)S(1)} %collective-permute-done.11.refs_1_, ...), custom_call_target="tpu_custom_call" | custom-call | flops 2147483648 | bytes 12582912 | tf_op jit(solution)/shard_map/attend_step/pallas_call | solution.py:202
  63.2 3.9 %attend_step.5 = (f32[8,1024,128]{2,1,0:T(8,128)S(1)}, f32[8,128,128]{2,1,0:T(8,128)S(1)}) custom-call(s32[1]{0:T(128)} %bitcast.me_ref, bf16[128,8192]{1,0:T(8,128)(2,1)S(1)} %copy-done, bf16[128,1024]{1,0:T(8,128)(2,1)S(1)} %collective-permute-done.2.refs_0_, bf16[128,1024]{1,0:T(8,128)(2,1)S(1)} %collective-permute-done.12.refs_1_, ...), custom_call_target="tpu_custom_call" | custom-call | flops 2147483648 | bytes 12582912 | tf_op jit(solution)/shard_map/attend_step/pallas_call | solution.py:202
  67.1 4.6 %attend_last.1 = (bf16[128,8192]{1,0:T(8,128)(2,1)}, bf16[16,4096]{1,0:T(8,128)(2,1)S(1)}, bf16[16,4096]{1,0:T(8,128)(2,1)S(1)}) custom-call(s32[1]{0:T(128)} %bitcast.me_ref, bf16[128,8192]{1,0:T(8,128)(2,1)S(1)} %copy-done, bf16[128,1024]{1,0:T(8,128)(2,1)S(1)} %collective-permute-done.3.refs_0_, bf16[128,1024]{1,0:T(8,128)(2,1)S(1)} %collective-permute-done.7.refs_1_, ...), custom_call_target="tpu_custom_call" | custom-call | flops 1073741824 | bytes 12582912 | tf_op jit(solution)/shard_map/attend_last/pallas_call | solution.py:216
  71.7 25.7 %collective-permute-start.30 = (bf16[16,4096]{1,0:T(8,128)(2,1)S(1)}, bf16[16,4096]{1,0:T(8,128)(2,1)S(1)}, u32[]{:S(2)}, u32[]{:S(2)}) collective-permute-start(bf16[16,4096]{1,0:T(8,128)(2,1)S(1)} %get-tuple-element.24.refs_0_), channel_id=1, source_target_pairs={{0,4},{1,5},{4,8},{5,9},{8,12},{9,13},{12,14},{13,15},{14,10},{15,... | collective-permute-start | bytes 393224 | tf_op jit(solution)/shard_map/ppermute | solution.py:357
  97.4 11.8 %collective-permute-start.33 = (bf16[16,4096]{1,0:T(8,128)(2,1)S(1)}, bf16[16,4096]{1,0:T(8,128)(2,1)S(1)}, u32[]{:S(2)}, u32[]{:S(2)}) collective-permute-start(bf16[16,4096]{1,0:T(8,128)(2,1)S(1)} %get-tuple-element.24.refs_0_), channel_id=1, source_target_pairs={{4,0},{5,1},{8,4},{9,5},{12,8},{13,9},{14,12},{15,13},{10,14},{11,... | collective-permute-start | bytes 393224 | tf_op jit(solution)/shard_map/ppermute | solution.py:358
  109.2 14.0 %collective-permute-start.45 = (bf16[16,4096]{1,0:T(8,128)(2,1)S(1)}, bf16[16,4096]{1,0:T(8,128)(2,1)S(1)}, u32[]{:S(2)}, u32[]{:S(2)}) collective-permute-start(bf16[16,4096]{1,0:T(8,128)(2,1)S(1)} %get-tuple-element.25.refs_16_), channel_id=1, source_target_pairs={{0,4},{1,5},{4,8},{5,9},{8,12},{9,13},{12,14},{13,15},{14,10},{15,... | collective-permute-start | bytes 393224 | tf_op jit(solution)/shard_map/ppermute | solution.py:357
  123.7 3.8 %collective-permute-done.48.refs_20_ = bf16[16,4096]{1,0:T(8,128)(2,1)S(1)} collective-permute-done((bf16[16,4096]{1,0:T(8,128)(2,1)S(1)}, bf16[16,4096]{1,0:T(8,128)(2,1)S(1)}, u32[]{:S(2)}, u32[]{:S(2)}) %collective-permute-start.48) | collective-permute-done | bytes 131104 | tf_op jit(solution)/shard_map/ppermute | solution.py:358
  127.4 27.5 %collective-permute-start.31 = (bf16[16,4096]{1,0:T(8,128)(2,1)S(1)}, bf16[16,4096]{1,0:T(8,128)(2,1)S(1)}, u32[]{:S(2)}, u32[]{:S(2)}) collective-permute-start(bf16[16,4096]{1,0:T(8,128)(2,1)S(1)} %collective-permute-done.30.refs_1_), channel_id=1, source_target_pairs={{0,4},{1,5},{4,8},{5,9},{8,12},{9,13},{12,14},{13,15},{14,10},{15,... | collective-permute-start | bytes 393224 | tf_op jit(solution)/shard_map/ppermute | solution.py:357
  154.9 13.5 %collective-permute-start.34 = (bf16[16,4096]{1,0:T(8,128)(2,1)S(1)}, bf16[16,4096]{1,0:T(8,128)(2,1)S(1)}, u32[]{:S(2)}, u32[]{:S(2)}) collective-permute-start(bf16[16,4096]{1,0:T(8,128)(2,1)S(1)} %collective-permute-done.33.refs_4_), channel_id=1, source_target_pairs={{4,0},{5,1},{8,4},{9,5},{12,8},{13,9},{14,12},{15,13},{10,14},{11,... | collective-permute-start | bytes 393224 | tf_op jit(solution)/shard_map/ppermute | solution.py:358
  169.2 3.1 %collective-permute-done.49.refs_21_ = bf16[16,4096]{1,0:T(8,128)(2,1)S(1)} collective-permute-done((bf16[16,4096]{1,0:T(8,128)(2,1)S(1)}, bf16[16,4096]{1,0:T(8,128)(2,1)S(1)}, u32[]{:S(2)}, u32[]{:S(2)}) %collective-permute-start.49) | collective-permute-done | bytes 131104 | tf_op jit(solution)/shard_map/ppermute | solution.py:358
  173.7 3.1 %collective-permute-start.32 = (bf16[16,4096]{1,0:T(8,128)(2,1)S(1)}, bf16[16,4096]{1,0:T(8,128)(2,1)S(1)}, u32[]{:S(2)}, u32[]{:S(2)}) collective-permute-start(bf16[16,4096]{1,0:T(8,128)(2,1)S(1)} %collective-permute-done.31.refs_2_), channel_id=1, source_target_pairs={{0,4},{1,5},{4,8},{5,9},{8,12},{9,13},{12,14},{13,15},{14,10},{15,... | collective-permute-start | bytes 393224 | tf_op jit(solution)/shard_map/ppermute | solution.py:357
  180.6 2.5 collective-permute-done.50.refs_22_
  183.2 2.1 collective-permute-done.35.refs_6_
  187.9 3.3 %collective-permute-done.36.refs_7_ = bf16[16,4096]{1,0:T(8,128)(2,1)S(1)} collective-permute-done((bf16[16,4096]{1,0:T(8,128)(2,1)S(1)}, bf16[16,4096]{1,0:T(8,128)(2,1)S(1)}, u32[]{:S(2)}, u32[]{:S(2)}) %collective-permute-start.36) | collective-permute-done | bytes 131104 | tf_op jit(solution)/shard_map/ppermute | solution.py:357
  194.2 25.8 %expert.1 = (bf16[128,8192]{1,0:T(8,128)(2,1)S(1)}, bf16[128,8192]{1,0:T(8,128)(2,1)S(1)}) custom-call(bf16[16,4096]{1,0:T(8,128)(2,1)S(1)} %get-tuple-element.24.refs_0_, bf16[16,4096]{1,0:T(8,128)(2,1)S(1)} %collective-permute-done.30.refs_1_, bf16[16,4096]{1,0:T(8,128)(2,1)S(1)} %collective-permute-done.31.refs_2_, ...), custom_call_target="tpu_custom_call" | custom-call | flops 9663676416 | bytes 46137344 | tf_op jit(solution)/shard_map/expert/pallas_call | solution.py:296
  220.4 3.8 %collective-permute-done.60 = bf16[128,8192]{1,0:T(8,128)(2,1)S(1)} collective-permute-done((bf16[128,8192]{1,0:T(8,128)(2,1)S(1)}, bf16[128,8192]{1,0:T(8,128)(2,1)S(1)}, u32[]{:S(2)}, u32[]{:S(2)}) %collective-permute-start.60) | collective-permute-done | bytes 2097184 | tf_op jit(solution)/shard_map/ppermute | solution.py:359
  224.7 5.4 %collective-permute-done.65 = bf16[16,4096]{1,0:T(8,128)(2,1)S(1)} collective-permute-done((bf16[16,4096]{1,0:T(8,128)(2,1)S(1)}, bf16[16,4096]{1,0:T(8,128)(2,1)S(1)}, u32[]{:S(2)}, u32[]{:S(2)}) %collective-permute-start.65) | collective-permute-done | bytes 131104 | tf_op jit(solution)/shard_map/ppermute | solution.py:358
  230.5 7.5 %collective-permute-done.66 = bf16[16,8192]{1,0:T(8,128)(2,1)S(1)} collective-permute-done((bf16[16,8192]{1,0:T(8,128)(2,1)S(1)}, bf16[16,8192]{1,0:T(8,128)(2,1)S(1)}, u32[]{:S(2)}, u32[]{:S(2)}) %collective-permute-start.66) | collective-permute-done | bytes 262176 | tf_op jit(solution)/shard_map/ppermute | solution.py:358
  240.2 4.8 %collective-permute-done.67 = bf16[16,8192]{1,0:T(8,128)(2,1)S(1)} collective-permute-done((bf16[16,8192]{1,0:T(8,128)(2,1)S(1)}, bf16[16,8192]{1,0:T(8,128)(2,1)S(1)}, u32[]{:S(2)}, u32[]{:S(2)}) %collective-permute-start.67) | collective-permute-done | bytes 262176 | tf_op jit(solution)/shard_map/ppermute | solution.py:358
  246.7 5.6 %collective-permute-done.62 = bf16[16,8192]{1,0:T(8,128)(2,1)S(1)} collective-permute-done((bf16[16,8192]{1,0:T(8,128)(2,1)S(1)}, bf16[16,8192]{1,0:T(8,128)(2,1)S(1)}, u32[]{:S(2)}, u32[]{:S(2)}) %collective-permute-start.62) | collective-permute-done | bytes 262176 | tf_op jit(solution)/shard_map/ppermute | solution.py:357
  254.5 6.1 %collective-permute-done.63 = bf16[16,8192]{1,0:T(8,128)(2,1)S(1)} collective-permute-done((bf16[16,8192]{1,0:T(8,128)(2,1)S(1)}, bf16[16,8192]{1,0:T(8,128)(2,1)S(1)}, u32[]{:S(2)}, u32[]{:S(2)}) %collective-permute-start.63) | collective-permute-done | bytes 262176 | tf_op jit(solution)/shard_map/ppermute | solution.py:357
  267.8 4.2 %spread.1 = bf16[128,8192]{1,0:T(8,128)(2,1)} custom-call(bf16[16,8192]{1,0:T(8,128)(2,1)} %slice.68.own_ref, bf16[16,8192]{1,0:T(8,128)(2,1)} %slice.90.sib_ref, bf16[16,8192]{1,0:T(8,128)(2,1)} %copy-done.13, bf16[16,8192]{1,0:T(8,128)(2,1)} %copy-done.12, bf16[16,128]{1,0:T(8,128)(2,1)} %copy-done.3, f32[128,1]{1,0:T(8,128)} %copy.12.weight_ref), custom_call_target="tpu_custom_call" | custom-call | tf_op jit(solution)/shard_map/spread/pallas_call | solution.py:338
  (161 shorter events, 48.4 us)
Async XLA Ops:
  1.1 10.0 %collective-permute-start = (bf16[128,1024]{1,0:T(8,128)(2,1)}, bf16[128,1024]{1,0:T(8,128)(2,1)S(1)}, u32[]{:S(2)}, u32[]{:S(2)}) collective-permute-start(bf16[128,1024]{1,0:T(8,128)(2,1)} %key_ref.1), channel_id=1, source_target_pairs={{0,4},{1,5},{4,8},{5,9},{8,12},{9,13},{12,14},{13,15},{14,10},{15,... | collective-permute-start | bytes 786440 | tf_op jit(solution)/shard_map/ppermute | solution.py:357
  3.8 12.7 %collective-permute-start.10 = (bf16[128,1024]{1,0:T(8,128)(2,1)}, bf16[128,1024]{1,0:T(8,128)(2,1)S(1)}, u32[]{:S(2)}, u32[]{:S(2)}) collective-permute-start(bf16[128,1024]{1,0:T(8,128)(2,1)} %value_ref.1), channel_id=1, source_target_pairs={{0,4},{1,5},{4,8},{5,9},{8,12},{9,13},{12,14},{13,15},{14,10},{15,... | collective-permute-start | bytes 786440 | tf_op jit(solution)/shard_map/ppermute | solution.py:357
  5.4 11.1 %collective-permute-start.15 = (bf16[128,1024]{1,0:T(8,128)(2,1)}, bf16[128,1024]{1,0:T(8,128)(2,1)S(1)}, u32[]{:S(2)}, u32[]{:S(2)}) collective-permute-start(bf16[128,1024]{1,0:T(8,128)(2,1)} %key_ref.1), channel_id=1, source_target_pairs={{4,0},{5,1},{8,4},{9,5},{12,8},{13,9},{14,12},{15,13},{10,14},{11,... | collective-permute-start | bytes 786440 | tf_op jit(solution)/shard_map/ppermute | solution.py:358
  5.8 11.2 %collective-permute-start.29 = (bf16[128,1024]{1,0:T(8,128)(2,1)}, bf16[128,1024]{1,0:T(8,128)(2,1)S(1)}, u32[]{:S(2)}, u32[]{:S(2)}) collective-permute-start(bf16[128,1024]{1,0:T(8,128)(2,1)} %value_ref.1), channel_id=1, source_target_pairs={{0,1},{1,0},{2,3},{3,2},{4,5},{5,4},{6,7},{7,6},{8,9},{9,8},{10,11... | collective-permute-start | bytes 786440 | tf_op jit(solution)/shard_map/ppermute | solution.py:359
  6.5 13.0 %collective-permute-start.4 = (bf16[128,1024]{1,0:T(8,128)(2,1)}, bf16[128,1024]{1,0:T(8,128)(2,1)S(1)}, u32[]{:S(2)}, u32[]{:S(2)}) collective-permute-start(bf16[128,1024]{1,0:T(8,128)(2,1)} %value_ref.1), channel_id=1, source_target_pairs={{4,0},{5,1},{8,4},{9,5},{12,8},{13,9},{14,12},{15,13},{10,14},{11,... | collective-permute-start | bytes 786440 | tf_op jit(solution)/shard_map/ppermute | solution.py:358
  11.1 8.4 %collective-permute-start.24 = (bf16[128,1024]{1,0:T(8,128)(2,1)S(1)}, bf16[128,1024]{1,0:T(8,128)(2,1)S(1)}, u32[]{:S(2)}, u32[]{:S(2)}) collective-permute-start(bf16[128,1024]{1,0:T(8,128)(2,1)S(1)} %collective-permute-done.refs_0_), channel_id=1, source_target_pairs={{0,1},{1,0},{2,3},{3,2},{4,5},{5,4},{6,7},{7,6},{8,9},{9,8},{10,11... | collective-permute-start | bytes 786440 | tf_op jit(solution)/shard_map/ppermute | solution.py:359
  17.7 9.2 %collective-permute-start.1 = (bf16[128,1024]{1,0:T(8,128)(2,1)S(1)}, bf16[128,1024]{1,0:T(8,128)(2,1)S(1)}, u32[]{:S(2)}, u32[]{:S(2)}) collective-permute-start(bf16[128,1024]{1,0:T(8,128)(2,1)S(1)} %collective-permute-done.refs_0_), channel_id=1, source_target_pairs={{0,4},{1,5},{4,8},{5,9},{8,12},{9,13},{12,14},{13,15},{14,10},{15,... | collective-permute-start | bytes 786440 | tf_op jit(solution)/shard_map/ppermute | solution.py:357
  19.5 12.7 %collective-permute-start.11 = (bf16[128,1024]{1,0:T(8,128)(2,1)S(1)}, bf16[128,1024]{1,0:T(8,128)(2,1)S(1)}, u32[]{:S(2)}, u32[]{:S(2)}) collective-permute-start(bf16[128,1024]{1,0:T(8,128)(2,1)S(1)} %collective-permute-done.10.refs_1_), channel_id=1, source_target_pairs={{0,4},{1,5},{4,8},{5,9},{8,12},{9,13},{12,14},{13,15},{14,10},{15,... | collective-permute-start | bytes 786440 | tf_op jit(solution)/shard_map/ppermute | solution.py:357
  21.1 11.1 %collective-permute-start.16 = (bf16[128,1024]{1,0:T(8,128)(2,1)S(1)}, bf16[128,1024]{1,0:T(8,128)(2,1)S(1)}, u32[]{:S(2)}, u32[]{:S(2)}) collective-permute-start(bf16[128,1024]{1,0:T(8,128)(2,1)S(1)} %collective-permute-done.15.refs_4_), channel_id=1, source_target_pairs={{4,0},{5,1},{8,4},{9,5},{12,8},{13,9},{14,12},{15,13},{10,14},{11,... | collective-permute-start | bytes 786440 | tf_op jit(solution)/shard_map/ppermute | solution.py:358
  21.6 13.5 %collective-permute-start.5 = (bf16[128,1024]{1,0:T(8,128)(2,1)S(1)}, bf16[128,1024]{1,0:T(8,128)(2,1)S(1)}, u32[]{:S(2)}, u32[]{:S(2)}) collective-permute-start(bf16[128,1024]{1,0:T(8,128)(2,1)S(1)} %collective-permute-done.4.refs_5_), channel_id=1, source_target_pairs={{4,0},{5,1},{8,4},{9,5},{12,8},{13,9},{14,12},{15,13},{10,14},{11,... | collective-permute-start | bytes 786440 | tf_op jit(solution)/shard_map/ppermute | solution.py:358
  26.9 8.3 %collective-permute-start.20 = (bf16[128,1024]{1,0:T(8,128)(2,1)S(1)}, bf16[128,1024]{1,0:T(8,128)(2,1)S(1)}, u32[]{:S(2)}, u32[]{:S(2)}) collective-permute-start(bf16[128,1024]{1,0:T(8,128)(2,1)S(1)} %collective-permute-done.1.refs_0_), channel_id=1, source_target_pairs={{0,1},{1,0},{2,3},{3,2},{4,5},{5,4},{6,7},{7,6},{8,9},{9,8},{10,11... | collective-permute-start | bytes 786440 | tf_op jit(solution)/shard_map/ppermute | solution.py:359
  27.6 10.9 %collective-permute-start.2 = (bf16[128,1024]{1,0:T(8,128)(2,1)S(1)}, bf16[128,1024]{1,0:T(8,128)(2,1)S(1)}, u32[]{:S(2)}, u32[]{:S(2)}) collective-permute-start(bf16[128,1024]{1,0:T(8,128)(2,1)S(1)} %collective-permute-done.1.refs_0_), channel_id=1, source_target_pairs={{0,4},{1,5},{4,8},{5,9},{8,12},{9,13},{12,14},{13,15},{14,10},{15,... | collective-permute-start | bytes 786440 | tf_op jit(solution)/shard_map/ppermute | solution.py:357
  35.8 9.2 %collective-permute-start.6 = (bf16[128,1024]{1,0:T(8,128)(2,1)S(1)}, bf16[128,1024]{1,0:T(8,128)(2,1)}, u32[]{:S(2)}, u32[]{:S(2)}) collective-permute-start(bf16[128,1024]{1,0:T(8,128)(2,1)S(1)} %collective-permute-done.5.refs_5_), channel_id=1, source_target_pairs={{4,0},{5,1},{8,4},{9,5},{12,8},{13,9},{14,12},{15,13},{10,14},{11,... | collective-permute-start | bytes 786440 | tf_op jit(solution)/shard_map/ppermute | solution.py:358
  36.4 20.1 %collective-permute-start.12 = (bf16[128,1024]{1,0:T(8,128)(2,1)S(1)}, bf16[128,1024]{1,0:T(8,128)(2,1)S(1)}, u32[]{:S(2)}, u32[]{:S(2)}) collective-permute-start(bf16[128,1024]{1,0:T(8,128)(2,1)S(1)} %collective-permute-done.11.refs_1_), channel_id=1, source_target_pairs={{0,4},{1,5},{4,8},{5,9},{8,12},{9,13},{12,14},{13,15},{14,10},{15,... | collective-permute-start | bytes 786440 | tf_op jit(solution)/shard_map/ppermute | solution.py:357
  38.1 18.5 %collective-permute-start.17 = (bf16[128,1024]{1,0:T(8,128)(2,1)S(1)}, bf16[128,1024]{1,0:T(8,128)(2,1)S(1)}, u32[]{:S(2)}, u32[]{:S(2)}) collective-permute-start(bf16[128,1024]{1,0:T(8,128)(2,1)S(1)} %collective-permute-done.16.refs_4_), channel_id=1, source_target_pairs={{4,0},{5,1},{8,4},{9,5},{12,8},{13,9},{14,12},{15,13},{10,14},{11,... | collective-permute-start | bytes 786440 | tf_op jit(solution)/shard_map/ppermute | solution.py:358
  38.5 18.6 %collective-permute-start.13 = (bf16[128,1024]{1,0:T(8,128)(2,1)S(1)}, bf16[128,1024]{1,0:T(8,128)(2,1)S(1)}, u32[]{:S(2)}, u32[]{:S(2)}) collective-permute-start(bf16[128,1024]{1,0:T(8,128)(2,1)S(1)} %collective-permute-done.2.refs_0_), channel_id=1, source_target_pairs={{0,1},{1,0},{2,3},{3,2},{4,5},{5,4},{6,7},{7,6},{8,9},{9,8},{10,11... | collective-permute-start | bytes 786440 | tf_op jit(solution)/shard_map/ppermute | solution.py:359
  38.5 20.1 %collective-permute-start.3 = (bf16[128,1024]{1,0:T(8,128)(2,1)S(1)}, bf16[128,1024]{1,0:T(8,128)(2,1)S(1)}, u32[]{:S(2)}, u32[]{:S(2)}) collective-permute-start(bf16[128,1024]{1,0:T(8,128)(2,1)S(1)} %collective-permute-done.2.refs_0_), channel_id=1, source_target_pairs={{0,4},{1,5},{4,8},{5,9},{8,12},{9,13},{12,14},{13,15},{14,10},{15,... | collective-permute-start | bytes 786440 | tf_op jit(solution)/shard_map/ppermute | solution.py:357
  45.0 14.1 %collective-permute-start.7 = (bf16[128,1024]{1,0:T(8,128)(2,1)}, bf16[128,1024]{1,0:T(8,128)(2,1)S(1)}, u32[]{:S(2)}, u32[]{:S(2)}) collective-permute-start(bf16[128,1024]{1,0:T(8,128)(2,1)} %collective-permute-done.6.refs_5_), channel_id=1, source_target_pairs={{4,0},{5,1},{8,4},{9,5},{12,8},{13,9},{14,12},{15,13},{10,14},{11,... | collective-permute-start | bytes 786440 | tf_op jit(solution)/shard_map/ppermute | solution.py:358
  58.7 8.4 %collective-permute-start.8 = (bf16[128,1024]{1,0:T(8,128)(2,1)S(1)}, bf16[128,1024]{1,0:T(8,128)(2,1)S(1)}, u32[]{:S(2)}, u32[]{:S(2)}) collective-permute-start(bf16[128,1024]{1,0:T(8,128)(2,1)S(1)} %collective-permute-done.3.refs_0_), channel_id=1, source_target_pairs={{0,1},{1,0},{2,3},{3,2},{4,5},{5,4},{6,7},{7,6},{8,9},{9,8},{10,11... | collective-permute-start | bytes 786440 | tf_op jit(solution)/shard_map/ppermute | solution.py:359
  71.7 51.4 %collective-permute-start.30 = (bf16[16,4096]{1,0:T(8,128)(2,1)S(1)}, bf16[16,4096]{1,0:T(8,128)(2,1)S(1)}, u32[]{:S(2)}, u32[]{:S(2)}) collective-permute-start(bf16[16,4096]{1,0:T(8,128)(2,1)S(1)} %get-tuple-element.24.refs_0_), channel_id=1, source_target_pairs={{0,4},{1,5},{4,8},{5,9},{8,12},{9,13},{12,14},{13,15},{14,10},{15,... | collective-permute-start | bytes 393224 | tf_op jit(solution)/shard_map/ppermute | solution.py:357
  97.4 30.0 %collective-permute-start.48 = (bf16[16,4096]{1,0:T(8,128)(2,1)S(1)}, bf16[16,4096]{1,0:T(8,128)(2,1)S(1)}, u32[]{:S(2)}, u32[]{:S(2)}) collective-permute-start(bf16[16,4096]{1,0:T(8,128)(2,1)S(1)} %get-tuple-element.25.refs_16_), channel_id=1, source_target_pairs={{4,0},{5,1},{8,4},{9,5},{12,8},{13,9},{14,12},{15,13},{10,14},{11,... | collective-permute-start | bytes 393224 | tf_op jit(solution)/shard_map/ppermute | solution.py:358
  97.4 57.5 %collective-permute-start.33 = (bf16[16,4096]{1,0:T(8,128)(2,1)S(1)}, bf16[16,4096]{1,0:T(8,128)(2,1)S(1)}, u32[]{:S(2)}, u32[]{:S(2)}) collective-permute-start(bf16[16,4096]{1,0:T(8,128)(2,1)S(1)} %get-tuple-element.24.refs_0_), channel_id=1, source_target_pairs={{4,0},{5,1},{8,4},{9,5},{12,8},{13,9},{14,12},{15,13},{10,14},{11,... | collective-permute-start | bytes 393224 | tf_op jit(solution)/shard_map/ppermute | solution.py:358
  109.2 45.7 %collective-permute-start.45 = (bf16[16,4096]{1,0:T(8,128)(2,1)S(1)}, bf16[16,4096]{1,0:T(8,128)(2,1)S(1)}, u32[]{:S(2)}, u32[]{:S(2)}) collective-permute-start(bf16[16,4096]{1,0:T(8,128)(2,1)S(1)} %get-tuple-element.25.refs_16_), channel_id=1, source_target_pairs={{0,4},{1,5},{4,8},{5,9},{8,12},{9,13},{12,14},{13,15},{14,10},{15,... | collective-permute-start | bytes 393224 | tf_op jit(solution)/shard_map/ppermute | solution.py:357
  123.1 45.3 %collective-permute-start.37 = (bf16[16,4096]{1,0:T(8,128)(2,1)S(1)}, bf16[16,4096]{1,0:T(8,128)(2,1)S(1)}, u32[]{:S(2)}, u32[]{:S(2)}) collective-permute-start(bf16[16,4096]{1,0:T(8,128)(2,1)S(1)} %get-tuple-element.24.refs_0_), channel_id=1, source_target_pairs={{0,1},{1,0},{2,3},{3,2},{4,5},{5,4},{6,7},{7,6},{8,9},{9,8},{10,11... | collective-permute-start | bytes 393224 | tf_op jit(solution)/shard_map/ppermute | solution.py:359
  123.1 45.6 %collective-permute-start.52 = (bf16[16,4096]{1,0:T(8,128)(2,1)S(1)}, bf16[16,4096]{1,0:T(8,128)(2,1)S(1)}, u32[]{:S(2)}, u32[]{:S(2)}) collective-permute-start(bf16[16,4096]{1,0:T(8,128)(2,1)S(1)} %get-tuple-element.25.refs_16_), channel_id=1, source_target_pairs={{0,1},{1,0},{2,3},{3,2},{4,5},{5,4},{6,7},{7,6},{8,9},{9,8},{10,11... | collective-permute-start | bytes 393224 | tf_op jit(solution)/shard_map/ppermute | solution.py:359
  127.4 41.3 %collective-permute-start.31 = (bf16[16,4096]{1,0:T(8,128)(2,1)S(1)}, bf16[16,4096]{1,0:T(8,128)(2,1)S(1)}, u32[]{:S(2)}, u32[]{:S(2)}) collective-permute-start(bf16[16,4096]{1,0:T(8,128)(2,1)S(1)} %collective-permute-done.30.refs_1_), channel_id=1, source_target_pairs={{0,4},{1,5},{4,8},{5,9},{8,12},{9,13},{12,14},{13,15},{14,10},{15,... | collective-permute-start | bytes 393224 | tf_op jit(solution)/shard_map/ppermute | solution.py:357
  154.9 17.4 %collective-permute-start.49 = (bf16[16,4096]{1,0:T(8,128)(2,1)S(1)}, bf16[16,4096]{1,0:T(8,128)(2,1)S(1)}, u32[]{:S(2)}, u32[]{:S(2)}) collective-permute-start(bf16[16,4096]{1,0:T(8,128)(2,1)S(1)} %collective-permute-done.48.refs_20_), channel_id=1, source_target_pairs={{4,0},{5,1},{8,4},{9,5},{12,8},{13,9},{14,12},{15,13},{10,14},{11,... | collective-permute-start | bytes 393224 | tf_op jit(solution)/shard_map/ppermute | solution.py:358
  154.9 18.8 %collective-permute-start.34 = (bf16[16,4096]{1,0:T(8,128)(2,1)S(1)}, bf16[16,4096]{1,0:T(8,128)(2,1)S(1)}, u32[]{:S(2)}, u32[]{:S(2)}) collective-permute-start(bf16[16,4096]{1,0:T(8,128)(2,1)S(1)} %collective-permute-done.33.refs_4_), channel_id=1, source_target_pairs={{4,0},{5,1},{8,4},{9,5},{12,8},{13,9},{14,12},{15,13},{10,14},{11,... | collective-permute-start | bytes 393224 | tf_op jit(solution)/shard_map/ppermute | solution.py:358
  168.7 8.1 %collective-permute-start.38 = (bf16[16,4096]{1,0:T(8,128)(2,1)S(1)}, bf16[16,4096]{1,0:T(8,128)(2,1)S(1)}, u32[]{:S(2)}, u32[]{:S(2)}) collective-permute-start(bf16[16,4096]{1,0:T(8,128)(2,1)S(1)} %collective-permute-done.30.refs_1_), channel_id=1, source_target_pairs={{0,1},{1,0},{2,3},{3,2},{4,5},{5,4},{6,7},{7,6},{8,9},{9,8},{10,11... | collective-permute-start | bytes 393224 | tf_op jit(solution)/shard_map/ppermute | solution.py:359
  176.8 8.4 %collective-permute-start.35 = (bf16[16,4096]{1,0:T(8,128)(2,1)S(1)}, bf16[16,4096]{1,0:T(8,128)(2,1)S(1)}, u32[]{:S(2)}, u32[]{:S(2)}) collective-permute-start(bf16[16,4096]{1,0:T(8,128)(2,1)S(1)} %collective-permute-done.34.refs_5_), channel_id=1, source_target_pairs={{4,0},{5,1},{8,4},{9,5},{12,8},{13,9},{14,12},{15,13},{10,14},{11,... | collective-permute-start | bytes 393224 | tf_op jit(solution)/shard_map/ppermute | solution.py:358
  252.4 8.2 %collective-permute-start.63 = (bf16[16,8192]{1,0:T(8,128)(2,1)S(1)}, bf16[16,8192]{1,0:T(8,128)(2,1)S(1)}, u32[]{:S(2)}, u32[]{:S(2)}) collective-permute-start(bf16[16,8192]{1,0:T(8,128)(2,1)S(1)} %add_convert_fusion.3), channel_id=1, source_target_pairs={{0,4},{1,5},{4,8},{5,9},{8,12},{9,13},{12,14},{13,15},{14,10},{15,... | collective-permute-start | bytes 786440 | tf_op jit(solution)/shard_map/ppermute | solution.py:357
  253.8 11.5 %collective-permute-start.68 = (bf16[16,8192]{1,0:T(8,128)(2,1)S(1)}, bf16[16,8192]{1,0:T(8,128)(2,1)S(1)}, u32[]{:S(2)}, u32[]{:S(2)}) collective-permute-start(bf16[16,8192]{1,0:T(8,128)(2,1)S(1)} %get-tuple-element.30), channel_id=1, source_target_pairs={{4,0},{5,1},{8,4},{9,5},{12,8},{13,9},{14,12},{15,13},{10,14},{11,... | collective-permute-start | bytes 786440 | tf_op jit(solution)/shard_map/ppermute | solution.py:358
  (51 other events, 288.9 us)

commit v2 on v0

v2 whole, which is shorter than its diff:
```python
import functools
import math

import jax
import jax.numpy as jnp
from jax import lax
from jax.experimental import pallas as pl
from jax.experimental.pallas import tpu as pltpu
from jax.sharding import PartitionSpec as P

HQ = 64
HK = 8
DH = 128
CAP = 16
GROUP = HQ // HK
WIDE = GROUP * DH
LOG_SCALE = math.log2(math.e) / math.sqrt(DH)
MASKED = -1e30
PIECES = 2
STACK = 4
MIB = 1 << 20


def ring_order(chips):
    return list(range(0, chips, 2)) + list(range(1, chips, 2))[::-1]


def permutations(chips):
    order = ring_order(chips)
    right, left = [], []
    for place in range(chips):
        here, there = order[place], order[(place + 1) % chips]
        for core in range(2):
            right.append((2 * here + core, 2 * there + core))
            left.append((2 * there + core, 2 * here + core))
    sibling = [(i, i ^ 1) for i in range(2 * chips)]
    return right, left, sibling


def chip_at(me, step, chips):
    chip = me // 2
    place = jnp.where(chip % 2 == 0, chip // 2, chips - 1 - chip // 2)
    source = (place - step + 2 * chips) % chips
    return jnp.where(source < chips // 2, 2 * source, 2 * (chips - 1 - source) + 1)


def head_rows(q_ref, first):
    return jnp.concatenate(
        [q_ref[:, h * DH : (h + 1) * DH] for h in range(first, first + STACK)], axis=0
    )


def with_ones(values):
    return jnp.concatenate([values, jnp.ones_like(values)], axis=1)


def scores_of(queries, keys):
    return LOG_SCALE * lax.dot_general(
        queries, keys, (((1,), (1,)), ((), ())), preferred_element_type=jnp.float32
    )


def weights_of(scores, top):
    return jnp.exp2(scores - jnp.concatenate([top] * (scores.shape[1] // DH), axis=1))


def row_top(scores):
    return jnp.broadcast_to(jnp.max(scores, axis=1, keepdims=True), (scores.shape[0], DH))


def chip_block(own_ref, sib_ref):
    tokens = own_ref.shape[0] // 2
    keys = jnp.concatenate([own_ref[:tokens], sib_ref[:tokens]], axis=0)
    values = jnp.concatenate([own_ref[tokens:], sib_ref[tokens:]], axis=0)
    return keys, with_ones(values)


def own_kernel(me_ref, q_ref, own_ref, sib_ref, acc_ref, total_ref, top_ref):
    tokens = q_ref.shape[0]
    keys, values = chip_block(own_ref, sib_ref)
    shape = (STACK * tokens, 2 * tokens)
    token = lax.broadcasted_iota(jnp.int32, shape, 0) % tokens
    column = lax.broadcasted_iota(jnp.int32, shape, 1)
    limit = jnp.where(me_ref[0] % 2 == 1, 2 * tokens, tokens)
    allowed = column <= jnp.where(column < tokens, token, limit - 1)
    for first in range(0, GROUP, STACK):
        rows = slice(first * tokens, (first + STACK) * tokens)
        scores = jnp.where(allowed, scores_of(head_rows(q_ref, first), keys), MASKED)
        top = row_top(scores)
        weights = weights_of(scores, top).astype(jnp.bfloat16)
        update = jnp.dot(weights, values, preferred_element_type=jnp.float32)
        acc_ref[0, rows, :] = update[:, :DH]
        total_ref[0, rows, :] = update[:, DH:]
        top_ref[0, rows, :] = top


def fold_chip(q_ref, own_ref, sib_ref, acc_ref, total_ref, top_ref):
    tokens = q_ref.shape[0]
    keys, values = chip_block(own_ref, sib_ref)
    for first in range(0, GROUP, STACK):
        rows = slice(first * tokens, (first + STACK) * tokens)
        scores = scores_of(head_rows(q_ref, first), keys)
        old = top_ref[0, rows, :]
        top = jnp.maximum(old, row_top(scores))
        factor = jnp.exp2(old - top)
        weights = weights_of(scores, top).astype(jnp.bfloat16)
        update = jnp.dot(weights, values, preferred_element_type=jnp.float32)
        acc_ref[0, rows, :] = acc_ref[0, rows, :] * factor + update[:, :DH]
        total_ref[0, rows, :] = total_ref[0, rows, :] * factor + update[:, DH:]
        top_ref[0, rows, :] = top


def copy_state(sources, targets):
    for source, target in zip(sources, targets):
        target[...] = source[...]


def step_kernel(chips, step, me_ref, q_ref, *refs):
    pieces, state_in, state = refs[:4], refs[4:7], refs[7:]
    me = me_ref[0]
    copy_state(state_in, state)
    for place, own_ref, sib_ref in ((step, *pieces[:2]), (-step, *pieces[2:])):

        @pl.when(chip_at(me, place, chips) < me // 2)
        def _():
            fold_chip(q_ref, own_ref, sib_ref, *state)


def last_kernel(chips, me_ref, q_ref, *refs):
    (key, value, sib_key, sib_value), state_in = refs[:4], refs[4:7]
    (gain_ref, table_ref, out_ref, picked_ref, own_ref, sib_ref), state = refs[7:13], refs[13:]
    tokens = q_ref.shape[0]
    head = pl.program_id(0)
    me = me_ref[0]
    copy_state(state_in, state)

    @pl.when(chip_at(me, chips // 2, chips) < me // 2)
    def _():
        own_ref[:tokens], own_ref[tokens:] = key[...], value[...]
        sib_ref[:tokens], sib_ref[tokens:] = sib_key[...], sib_value[...]
        fold_chip(q_ref, own_ref, sib_ref, *state)

    acc_ref, total_ref, _ = state
    result = (acc_ref[0] / total_ref[0]).astype(jnp.bfloat16)
    columns = pl.ds(pl.multiple_of(head * WIDE, WIDE), WIDE)
    out_ref[:, columns] = jnp.concatenate(
        [result[h * tokens : (h + 1) * tokens] for h in range(GROUP)], axis=1
    )

    @pl.when(head == HK - 1)
    def _():
        width = out_ref.shape[1]
        picked = jnp.dot(table_ref[...], out_ref[...], preferred_element_type=jnp.float32)
        mean = jnp.sum(picked * picked, axis=1, keepdims=True) / width
        picked_ref[...] = (picked * lax.rsqrt(mean + 1e-05) * gain_ref[...]).astype(jnp.bfloat16)


class Attention:
    def __init__(self, me, queries, chips):
        self.me, self.queries, self.chips = me, queries, chips
        tokens = queries.shape[0]
        self.head_block = pl.BlockSpec((tokens, WIDE), lambda g, me: (0, g))
        self.pair_block = pl.BlockSpec((2 * tokens, DH), lambda g, me: (0, g))
        self.kv_block = pl.BlockSpec((tokens, DH), lambda g, me: (0, g))
        self.state_blocks = [pl.BlockSpec((1, GROUP * tokens, DH), lambda g, me: (g, 0, 0))] * 3
        self.state_shapes = [jax.ShapeDtypeStruct((HK, GROUP * tokens, DH), jnp.float32)] * 3

    def call(self, kernel, name, keys, in_specs, out_specs, out_shape, args, scratch=()):
        tokens, width = self.queries.shape
        return pl.pallas_call(
            kernel,
            grid_spec=pltpu.PrefetchScalarGridSpec(
                num_scalar_prefetch=1,
                grid=(HK,),
                in_specs=[self.head_block] + in_specs,
                out_specs=out_specs,
                scratch_shapes=scratch,
            ),
            out_shape=out_shape,
            compiler_params=pltpu.CompilerParams(
                dimension_semantics=("arbitrary",), vmem_limit_bytes=24 * MIB
            ),
            cost_estimate=pl.CostEstimate(
                flops=8 * tokens * width * keys,
                bytes_accessed=24 * MIB,
                transcendentals=tokens * HQ * keys,
            ),
            name=name,
        )(self.me, self.queries, *args)

    def own(self, own, sib):
        keys = 2 * self.queries.shape[0]
        return self.call(
            own_kernel, "attend_own", keys, [self.pair_block] * 2, self.state_blocks, self.state_shapes, (own, sib)
        )

    def step(self, step, pieces, state):
        keys = 4 * self.queries.shape[0]
        return self.call(
            functools.partial(step_kernel, self.chips, step),
            "attend_step",
            keys,
            [self.pair_block] * 4 + self.state_blocks,
            self.state_blocks,
            self.state_shapes,
            (*pieces, *state),
        )

    def last(self, pieces, state, gain, table):
        tokens, width = self.queries.shape
        whole = lambda shape: pl.BlockSpec(shape, lambda g, me: (0, 0))
        return self.call(
            functools.partial(last_kernel, self.chips),
            "attend_last",
            2 * tokens,
            [self.kv_block] * 4 + self.state_blocks + [whole((1, width)), whole((CAP, tokens))],
            [whole((tokens, width)), whole((CAP, width))],
            [
                jax.ShapeDtypeStruct((tokens, width), jnp.bfloat16),
                jax.ShapeDtypeStruct((CAP, width), jnp.bfloat16),
            ],
            (*pieces, *state, gain, table),
            [pltpu.VMEM((2 * tokens, DH), jnp.bfloat16)] * 2
            + [pltpu.VMEM((1, GROUP * tokens, DH), jnp.float32)] * 3,
        )


def hidden_kernel(chips, *refs):
    blocks, (gate_ref, up_ref, out_ref) = refs[: 2 * chips + 2], refs[2 * chips + 2 : 2 * chips + 5]
    rows_ref, gate_sum, up_sum, sems = refs[2 * chips + 5 :]
    step = pl.program_id(0)
    half = rows_ref.shape[1] // 2
    depth = gate_ref.shape[0]

    @pl.when(step == 0)
    def _():
        copies = []
        for core in range(2):
            mine = blocks[core * (chips + 1) : (core + 1) * (chips + 1)]
            for j in range(chips):
                rows = pl.ds((core * chips + j) * CAP, CAP)
                if j < chips - 1:
                    copies.append((mine[j], rows_ref.at[rows, :]))
                else:
                    copies.append((mine[j], rows_ref.at[rows, pl.ds(0, half)]))
                    copies.append((mine[j + 1], rows_ref.at[rows, pl.ds(half, half)]))
        copies = [
            pltpu.make_async_copy(source, target, sems.at[i])
            for i, (source, target) in enumerate(copies)
        ]
        for copy in copies:
            copy.start()
        gate_sum[...] = jnp.zeros_like(gate_sum)
        up_sum[...] = jnp.zeros_like(up_sum)
        for copy in copies:
            copy.wait()

    columns = pl.ds(pl.multiple_of(step * depth, depth), depth)
    part = rows_ref[:, columns]
    gate_sum[...] += jnp.dot(part, gate_ref[...], preferred_element_type=jnp.float32)
    up_sum[...] += jnp.dot(part, up_ref[...], preferred_element_type=jnp.float32)

    @pl.when(step == pl.num_programs(0) - 1)
    def _():
        gate = gate_sum[...]
        out_ref[...] = (gate / (1.0 + jnp.exp(-gate)) * up_sum[...]).astype(jnp.bfloat16)


def hidden_call(chips, blocks, w_gate, w_up):
    rows = 2 * chips * CAP
    width, units = w_gate.shape
    depth = min(1024, width)
    weight_block = pl.BlockSpec((depth, units), lambda i: (i, 0))
    return pl.pallas_call(
        functools.partial(hidden_kernel, chips),
        grid=(width // depth,),
        in_specs=[pl.BlockSpec(memory_space=pl.ANY)] * len(blocks) + [weight_block] * 2,
        out_specs=pl.BlockSpec((rows, units), lambda i: (0, 0)),
        out_shape=jax.ShapeDtypeStruct((rows, units), jnp.bfloat16),
        scratch_shapes=[
            pltpu.VMEM((rows, width), jnp.bfloat16),
            pltpu.VMEM((rows, units), jnp.float32),
            pltpu.VMEM((rows, units), jnp.float32),
            pltpu.SemaphoreType.DMA((len(blocks),)),
        ],
        compiler_params=pltpu.CompilerParams(
            dimension_semantics=("arbitrary",), vmem_limit_bytes=32 * MIB
        ),
        cost_estimate=pl.CostEstimate(
            flops=4 * rows * width * units,
            bytes_accessed=4 * width * units + 2 * rows * width,
            transcendentals=rows * units,
        ),
        name="hidden",
    )(*blocks, w_gate, w_up)


def down_kernel(hidden_ref, down_ref, own_ref, sib_ref):
    part = jnp.dot(hidden_ref[...], down_ref[...], preferred_element_type=jnp.float32)
    part = part.astype(jnp.bfloat16)
    middle = part.shape[0] // 2
    own_ref[...] = part[:middle]
    sib_ref[...] = part[middle:]


def down_call(hidden, w_down, piece, pieces):
    rows, units = hidden.shape
    width = w_down.shape[1] // pieces
    cols = min(1024, width)
    steps = width // cols
    out_block = pl.BlockSpec((rows // 2, cols), lambda i: (0, i))
    return pl.pallas_call(
        down_kernel,
        grid=(steps,),
        in_specs=[
            pl.BlockSpec((rows, units), lambda i: (0, 0)),
            pl.BlockSpec((units, cols), lambda i: (0, piece * steps + i)),
        ],
        out_specs=[out_block, out_block],
        out_shape=[jax.ShapeDtypeStruct((rows // 2, width), jnp.bfloat16)] * 2,
        compiler_params=pltpu.CompilerParams(
            dimension_semantics=("arbitrary",), vmem_limit_bytes=32 * MIB
        ),
        cost_estimate=pl.CostEstimate(
            flops=2 * rows * width * units,
            bytes_accessed=2 * width * units + 2 * rows * width,
            transcendentals=0,
        ),
        name="down",
    )(hidden, w_down)


def spread_kernel(per_piece, *refs):
    table_ref, weight_ref, out_ref = refs[-3:]
    for piece in range(len(refs[:-3]) // 4):

        @pl.when(pl.program_id(0) // per_piece == piece)
        def _():
            parts = [ref[...].astype(jnp.float32) for ref in refs[4 * piece : 4 * piece + 4]]
            total = parts[0] + parts[1] + parts[2] + parts[3]
            spread = lax.dot_general(
                table_ref[...],
                total.astype(jnp.bfloat16),
                (((0,), (0,)), ((), ())),
                preferred_element_type=jnp.float32,
            )
            out_ref[...] = (spread * weight_ref[...]).astype(jnp.bfloat16)


def spread_call(groups, table, weight):
    tokens = table.shape[1]
    piece_width = groups[0][0].shape[1]
    width = piece_width * len(groups)
    cols = min(2048, piece_width)
    per_piece = piece_width // cols

    def block(piece):
        return pl.BlockSpec(
            (CAP, cols), lambda i: (0, jnp.clip(i - piece * per_piece, 0, per_piece - 1))
        )

    return pl.pallas_call(
        functools.partial(spread_kernel, per_piece),
        grid=(width // cols,),
        in_specs=[block(piece) for piece in range(len(groups)) for _ in range(4)]
        + [pl.BlockSpec((CAP, tokens), lambda i: (0, 0)), pl.BlockSpec((tokens, 1), lambda i: (0, 0))],
        out_specs=pl.BlockSpec((tokens, cols), lambda i: (0, i)),
        out_shape=jax.ShapeDtypeStruct((tokens, width), jnp.bfloat16),
        compiler_params=pltpu.CompilerParams(dimension_semantics=("arbitrary",)),
        name="spread",
    )(*[x for group in groups for x in group], table, weight)


def reduce_chip_rows(mine, other, half, chips, go_right, go_left):
    middle = mine.shape[1] // 2

    def block(index):
        rows = slice(index * CAP, (index + 1) * CAP)
        return mine[rows].astype(jnp.float32) + other[rows].astype(jnp.float32)

    far = block(chips - 1).astype(jnp.bfloat16)
    ahead, back = far[:, :middle], far[:, middle:]
    for distance in range(half - 1, -1, -1):
        ahead, back = lax.optimization_barrier((ahead, back))
        to_right, to_left = go_right(ahead), go_left(back)
        yield
        if distance == 0:
            break
        ahead, back = block(half - 1 + distance), block(distance)
        if distance == half - 1:
            ahead = jnp.concatenate(
                [ahead[:, :middle] + to_right.astype(jnp.float32), ahead[:, middle:]], axis=1
            )
            back = jnp.concatenate(
                [back[:, :middle], back[:, middle:] + to_left.astype(jnp.float32)], axis=1
            )
        else:
            ahead = ahead + to_right.astype(jnp.float32)
            back = back + to_left.astype(jnp.float32)
        ahead, back = ahead.astype(jnp.bfloat16), back.astype(jnp.bfloat16)
    return (mine, other, to_right, to_left)


def run_together(generators):
    results = [None] * len(generators)
    active = list(range(len(generators)))
    while active:
        for i in list(active):
            try:
                next(generators[i])
            except StopIteration as stop:
                results[i] = stop.value
                active.remove(i)
    return results


def per_device(chips, queries, keys, values, norm_gain, expert_ids, gates, w_gate, w_up, w_down):
    right, left, sibling = permutations(chips)
    half = chips // 2
    go_right = lambda x: lax.ppermute(x, "ctx", right)
    go_left = lambda x: lax.ppermute(x, "ctx", left)
    swap = lambda x: lax.ppermute(x, "ctx", sibling)

    me = lax.axis_index("ctx").astype(jnp.int32).reshape(1)
    tokens = queries.shape[0]
    hits = (expert_ids == 0).astype(jnp.float32)
    chosen = jnp.sum(hits, axis=1)
    position = jnp.arange(tokens, dtype=jnp.int32)
    before = (position[None, :] < position[:, None]).astype(jnp.float32)
    slot = jnp.sum(before * chosen[None, :], axis=1).astype(jnp.int32)
    table = jnp.logical_and(
        slot[None, :] == jnp.arange(CAP, dtype=jnp.int32)[:, None], chosen[None, :] > 0
    ).astype(jnp.bfloat16)
    weight = jnp.sum(gates * hits, axis=1, keepdims=True)

    attention = Attention(me, queries, chips)
    own = jnp.concatenate([keys, values], axis=0)
    from_left, from_right, own_sib = go_right(own), go_left(own), swap(own)
    state = attention.own(own, own_sib)
    for step in range(1, half):
        from_left, from_right, state = lax.optimization_barrier((from_left, from_right, state))
        pieces = (from_left, swap(from_left), from_right, swap(from_right))
        if step < half - 1:
            from_left, from_right = go_right(from_left), go_left(from_right)
        else:
            far_keys, far_values = go_right(from_left[:tokens]), go_left(from_right[tokens:])
        state = attention.step(step, pieces, state)
    far_keys, far_values, state = lax.optimization_barrier((far_keys, far_values, state))
    opposite = (far_keys, far_values, swap(far_keys), swap(far_values))
    result, picked = attention.last(opposite, state, norm_gain[None, :], table)

    middle = picked.shape[1] // 2
    blocks_right, blocks_left = [picked], [picked]
    for _ in range(1, half):
        blocks_right.append(go_right(blocks_right[-1]))
        blocks_left.append(go_left(blocks_left[-1]))
    blocks = blocks_right + blocks_left[1:]
    blocks += [go_right(blocks_right[-1][:, :middle]), go_left(blocks_left[-1][:, middle:])]
    blocks += [swap(x) for x in blocks]
    hidden = hidden_call(chips, blocks, w_gate, w_up)

    sums = []
    for piece in range(PIECES):
        mine, theirs = down_call(hidden, w_down, piece, PIECES)
        sums.append(reduce_chip_rows(mine, swap(theirs), half, chips, go_right, go_left))
    mixed = spread_call(run_together(sums), table, weight)
    return (result, mixed)


def solution(mesh):
    placed = (
        P(("groups", "ctx"), None),
        P(("groups", "ctx"), None),
        P(("groups", "ctx"), None),
        P(),
        P(("groups", "ctx"), None),
        P(("groups", "ctx"), None),
        P(None, "ctx"),
        P(None, "ctx"),
        P("ctx", None),
    )
    return jax.shard_map(
        functools.partial(per_device, mesh.shape["ctx"] // 2),
        mesh=mesh,
        in_specs=placed,
        out_specs=(P(("groups", "ctx"), None), P(("groups", "ctx"), None)),
        check_vma=False,
    )
```

time: 367 us -> 174 us (0.47)
  waiting for transfers between devices: 267 us -> 63.6 us
  starting transfers between devices: 0.16 us -> 52.8 us
  matrix products: 46.1 us -> 0 us
  Pallas kernels: 0 us -> 37 us
  between operations: 13.9 us -> 1.05 us
  local copies, waits for them, and re-layouts: 28.2 us -> 18 us
  other arithmetic: 7.95 us -> 0.83 us
    all_gather x3 -> x0, waiting for transfers between devices: 195 us -> none  [the longest x1 102 us: per_device(): piece = lax.all_gather(picked_rows, 'ctx', axis=0, tiled=True)]
    reduce_scatter x1 -> x0, waiting for transfers between devices: 70.4 us -> none  [per_device(): lax.psum_scatter(jnp.dot(hidden, w_down, preferred_element_type=jnp.float...]
    ppermute x0 -> x52, waiting for transfers between devices: none -> 63.6 us  [the longest x16 44.4 us: per_device(): go_right = lambda x: lax.ppermute(x, 'ctx', right)]
    ppermute x0 -> x52, starting transfers between devices: none -> 52.8 us  [the longest x16 44.3 us: per_device(): go_right = lambda x: lax.ppermute(x, 'ctx', right)]
    dot_general x6 -> x0, matrix products: 46.1 us -> none  [the longest x1 19.9 us: per_device(): jnp.dot(hidden, w_down, preferred_element_type=jnp.float32)]
    pallas_call x0 -> x9, Pallas kernels: none -> 37 us  [the longest x5 15 us: call(): pl.pallas_call(kernel, grid_spec=pltpu.PrefetchScalarGridSpec(num_scalar_...]
    reduce_sum x4 -> x2, other arithmetic: 7.49 us -> 0.12 us  [the longest x1 0.1 us: per_device(): slot = jnp.sum(before * chosen[None, :], axis=1).astype(jnp.int32)]
    unnamed x25 -> x43, local copies, waits for them, and re-layouts: 21.9 us -> 16.2 us
  transfers between devices with their start and end apart: 4 -> 52, of which waited for: 4 -> 31; matrix products, arithmetic and copies ran while one was open for 3% -> 1% of each run, Pallas kernels for 0% -> 8%
where the time goes in v2:
time: 174 us; the launch traced here: 173 us
  waiting for transfers between devices  63.6 us (37%)
  starting transfers between devices  52.8 us (30%)
  Pallas kernels  37 us (21%)
  local copies, waits for them, and re-layouts  18 us (10%)
    ppermute x16, waiting for transfers between devices, per_device(): go_right = lambda x: lax.ppermute(x, 'ctx', right)  44.4 us
    ppermute x16, starting transfers between devices, per_device(): go_right = lambda x: lax.ppermute(x, 'ctx', right)  44.3 us
    unnamed x43, local copies, waits for them, and re-layouts  16.2 us
    ppermute x16, waiting for transfers between devices, per_device(): go_left = lambda x: lax.ppermute(x, 'ctx', left)  16.2 us
    pallas_call x5, Pallas kernels, call(): pl.pallas_call(kernel, grid_spec=pltpu.PrefetchScalarGridSpec(num_scalar_...  15 us
    pallas_call x1, Pallas kernels, hidden_call(): pl.pallas_call(functools.partial(hidden_kernel, chips), grid=(width // de...  12 us
    pallas_call x2, Pallas kernels, down_call(): pl.pallas_call(down_kernel, grid=(steps,), in_specs=[pl.BlockSpec((rows,...  5.75 us
    pallas_call x1, Pallas kernels, spread_call(): pl.pallas_call(functools.partial(spread_kernel, per_piece), grid=(width /...  4.31 us
  transfers between devices with their start and end apart: 52, of which 31 were waited for; matrix products, arithmetic and copies ran while one was open for 1% of the time, Pallas kernels for 8%

profile of v2, /device:TPU:0, one launch (start us, length us, event | category | flops | bytes accessed | tf_op | source)
XLA Modules:
  0.0 173.3 jit_solution(17769415500991127174)
XLA Ops:
  3.1 2.6 %collective-permute-start = (bf16[256,1024]{1,0:T(8,128)(2,1)S(1)}, bf16[256,1024]{1,0:T(8,128)(2,1)S(1)}, u32[]{:S(2)}, u32[]{:S(2)}) collective-permute-start(bf16[256,1024]{1,0:T(8,128)(2,1)S(1)} %constant_dynamic-update-slice_fusion.own_ref), channel_id=1, source_target_pairs={{0,4},{1,5},{4,8},{5,9},{8,12},{9,13},{12,14},{13,15},{14,10},{15,... | collective-permute-start | bytes 1572872 | tf_op jit(solution)/shard_map/ppermute | solution.py:420
  7.4 5.5 %attend_own.1 = (f32[8,1024,128]{2,1,0:T(8,128)S(1)}, f32[8,1024,128]{2,1,0:T(8,128)S(1)}, f32[8,1024,128]{2,1,0:T(8,128)S(1)}) custom-call(s32[1]{0:T(128)} %bitcast.me_ref, bf16[128,8192]{1,0:T(8,128)(2,1)S(1)} %copy-done, bf16[256,1024]{1,0:T(8,128)(2,1)S(1)} %constant_dynamic-update-slice_fusion.own_ref, bf16[256,1024]{1,0:T(8,128)(2,1)S(1)} %collective-permute-done.2.sib_ref), custom_call_target="tpu_custom_call" | custom-call | flops 2147483648 | bytes 25165824 | tf_op jit(solution)/shard_map/attend_own/pallas_call | solution.py:170
  12.9 5.3 %collective-permute-done.refs_0_ = bf16[256,1024]{1,0:T(8,128)(2,1)S(1)} collective-permute-done((bf16[256,1024]{1,0:T(8,128)(2,1)S(1)}, bf16[256,1024]{1,0:T(8,128)(2,1)S(1)}, u32[]{:S(2)}, u32[]{:S(2)}) %collective-permute-start) | collective-permute-done | bytes 524320 | tf_op jit(solution)/shard_map/ppermute | solution.py:420
  22.4 1.8 %attend_step.3 = (f32[8,1024,128]{2,1,0:T(8,128)S(1)}, f32[8,1024,128]{2,1,0:T(8,128)S(1)}, f32[8,1024,128]{2,1,0:T(8,128)S(1)}) custom-call(s32[1]{0:T(128)} %bitcast.me_ref, bf16[128,8192]{1,0:T(8,128)(2,1)S(1)} %copy-done, bf16[256,1024]{1,0:T(8,128)(2,1)S(1)} %collective-permute-done.refs_0_, bf16[256,1024]{1,0:T(8,128)(2,1)S(1)} %collective-permute-done.5.refs_1_, ...), custom_call_target="tpu_custom_call" | custom-call | flops 4294967296 | bytes 25165824 | tf_op jit(solution)/shard_map/attend_step/pallas_call | solution.py:170
  24.2 2.0 %copy-done.4 = f32[8,1024,128]{2,1,0:T(8,128)} copy-done((f32[8,1024,128]{2,1,0:T(8,128)}, f32[8,1024,128]{2,1,0:T(8,128)S(1)}, u32[]{:S(2)}) %copy-start.4) | copy-done | bytes 4194328
  26.2 7.8 %collective-permute-done.3.refs_0_ = bf16[256,1024]{1,0:T(8,128)(2,1)S(1)} collective-permute-done((bf16[256,1024]{1,0:T(8,128)(2,1)S(1)}, bf16[256,1024]{1,0:T(8,128)(2,1)S(1)}, u32[]{:S(2)}, u32[]{:S(2)}) %collective-permute-start.3) | collective-permute-done | bytes 524320 | tf_op jit(solution)/shard_map/ppermute | solution.py:420
  38.0 2.2 %copy-done.5 = f32[8,1024,128]{2,1,0:T(8,128)S(1)} copy-done((f32[8,1024,128]{2,1,0:T(8,128)S(1)}, f32[8,1024,128]{2,1,0:T(8,128)}, u32[]{:S(2)}) %copy-start.5) | copy-done | bytes 4194328
  40.2 1.8 %attend_step.4 = (f32[8,1024,128]{2,1,0:T(8,128)S(1)}, f32[8,1024,128]{2,1,0:T(8,128)S(1)}, f32[8,1024,128]{2,1,0:T(8,128)S(1)}) custom-call(s32[1]{0:T(128)} %bitcast.me_ref, bf16[128,8192]{1,0:T(8,128)(2,1)S(1)} %copy-done, bf16[256,1024]{1,0:T(8,128)(2,1)S(1)} %collective-permute-done.3.refs_0_, bf16[256,1024]{1,0:T(8,128)(2,1)S(1)} %collective-permute-done.9.refs_1_, ...), custom_call_target="tpu_custom_call" | custom-call | flops 4294967296 | bytes 25165824 | tf_op jit(solution)/shard_map/attend_step/pallas_call | solution.py:170
  42.1 2.0 %copy-done.2 = f32[8,1024,128]{2,1,0:T(8,128)} copy-done((f32[8,1024,128]{2,1,0:T(8,128)}, f32[8,1024,128]{2,1,0:T(8,128)S(1)}, u32[]{:S(2)}) %copy-start.2) | copy-done | bytes 4194328
  44.1 5.7 %collective-permute-done.7.refs_0_ = bf16[256,1024]{1,0:T(8,128)(2,1)S(1)} collective-permute-done((bf16[256,1024]{1,0:T(8,128)(2,1)S(1)}, bf16[256,1024]{1,0:T(8,128)(2,1)S(1)}, u32[]{:S(2)}, u32[]{:S(2)}) %collective-permute-start.7) | collective-permute-done | bytes 524320 | tf_op jit(solution)/shard_map/ppermute | solution.py:420
  53.8 2.2 %copy-done.3 = f32[8,1024,128]{2,1,0:T(8,128)S(1)} copy-done((f32[8,1024,128]{2,1,0:T(8,128)S(1)}, f32[8,1024,128]{2,1,0:T(8,128)}, u32[]{:S(2)}) %copy-start.3) | copy-done | bytes 4194328
  56.0 1.8 %attend_step.5 = (f32[8,1024,128]{2,1,0:T(8,128)S(1)}, f32[8,1024,128]{2,1,0:T(8,128)S(1)}, f32[8,1024,128]{2,1,0:T(8,128)S(1)}) custom-call(s32[1]{0:T(128)} %bitcast.me_ref, bf16[128,8192]{1,0:T(8,128)(2,1)S(1)} %copy-done, bf16[256,1024]{1,0:T(8,128)(2,1)S(1)} %collective-permute-done.7.refs_0_, bf16[256,1024]{1,0:T(8,128)(2,1)S(1)} %collective-permute-done.13.refs_1_, ...), custom_call_target="tpu_custom_call" | custom-call | flops 4294967296 | bytes 25165824 | tf_op jit(solution)/shard_map/attend_step/pallas_call | solution.py:170
  57.8 2.1 %collective-permute-done.11.refs_0_ = bf16[128,1024]{1,0:T(8,128)(2,1)S(1)} collective-permute-done((bf16[128,1024]{1,0:T(8,128)(2,1)S(1)}, bf16[128,1024]{1,0:T(8,128)(2,1)S(1)}, u32[]{:S(2)}, u32[]{:S(2)}) %collective-permute-start.11) | collective-permute-done | bytes 262176 | tf_op jit(solution)/shard_map/ppermute | solution.py:420
  63.1 3.9 %attend_last.1 = (bf16[128,8192]{1,0:T(8,128)(2,1)}, bf16[16,8192]{1,0:T(8,128)(2,1)S(1)}) custom-call(s32[1]{0:T(128)} %bitcast.me_ref, bf16[128,8192]{1,0:T(8,128)(2,1)S(1)} %copy-done, bf16[128,1024]{1,0:T(8,128)(2,1)S(1)} %collective-permute-done.11.refs_0_, bf16[128,1024]{1,0:T(8,128)(2,1)S(1)} %collective-permute-done.12.refs_1_, ...), custom_call_target="tpu_custom_call" | custom-call | flops 2147483648 | bytes 25165824 | tf_op jit(solution)/shard_map/attend_last/pallas_call | solution.py:170
  67.0 4.5 %collective-permute-start.17 = (bf16[16,8192]{1,0:T(8,128)(2,1)S(1)}, bf16[16,8192]{1,0:T(8,128)(2,1)S(1)}, u32[]{:S(2)}, u32[]{:S(2)}) collective-permute-start(bf16[16,8192]{1,0:T(8,128)(2,1)S(1)} %get-tuple-element.89.refs_0_), channel_id=1, source_target_pairs={{0,4},{1,5},{4,8},{5,9},{8,12},{9,13},{12,14},{13,15},{14,10},{15,... | collective-permute-start | bytes 786440 | tf_op jit(solution)/shard_map/ppermute | solution.py:420
  71.6 5.9 %collective-permute-done.17.refs_1_ = bf16[16,8192]{1,0:T(8,128)(2,1)S(1)} collective-permute-done((bf16[16,8192]{1,0:T(8,128)(2,1)S(1)}, bf16[16,8192]{1,0:T(8,128)(2,1)S(1)}, u32[]{:S(2)}, u32[]{:S(2)}) %collective-permute-start.17) | collective-permute-done | bytes 262176 | tf_op jit(solution)/shard_map/ppermute | solution.py:420
  77.4 8.3 %collective-permute-start.18 = (bf16[16,8192]{1,0:T(8,128)(2,1)S(1)}, bf16[16,8192]{1,0:T(8,128)(2,1)S(1)}, u32[]{:S(2)}, u32[]{:S(2)}) collective-permute-start(bf16[16,8192]{1,0:T(8,128)(2,1)S(1)} %collective-permute-done.17.refs_1_), channel_id=1, source_target_pairs={{0,4},{1,5},{4,8},{5,9},{8,12},{9,13},{12,14},{13,15},{14,10},{15,... | collective-permute-start | bytes 786440 | tf_op jit(solution)/shard_map/ppermute | solution.py:420
  86.2 4.6 %collective-permute-done.18.refs_2_ = bf16[16,8192]{1,0:T(8,128)(2,1)S(1)} collective-permute-done((bf16[16,8192]{1,0:T(8,128)(2,1)S(1)}, bf16[16,8192]{1,0:T(8,128)(2,1)S(1)}, u32[]{:S(2)}, u32[]{:S(2)}) %collective-permute-start.18) | collective-permute-done | bytes 262176 | tf_op jit(solution)/shard_map/ppermute | solution.py:420
  90.7 7.3 %collective-permute-start.19 = (bf16[16,8192]{1,0:T(8,128)(2,1)S(1)}, bf16[16,8192]{1,0:T(8,128)(2,1)S(1)}, u32[]{:S(2)}, u32[]{:S(2)}) collective-permute-start(bf16[16,8192]{1,0:T(8,128)(2,1)S(1)} %collective-permute-done.18.refs_2_), channel_id=1, source_target_pairs={{0,4},{1,5},{4,8},{5,9},{8,12},{9,13},{12,14},{13,15},{14,10},{15,... | collective-permute-start | bytes 786440 | tf_op jit(solution)/shard_map/ppermute | solution.py:420
  100.4 5.0 %collective-permute-done.19.refs_3_ = bf16[16,8192]{1,0:T(8,128)(2,1)S(1)} collective-permute-done((bf16[16,8192]{1,0:T(8,128)(2,1)S(1)}, bf16[16,8192]{1,0:T(8,128)(2,1)S(1)}, u32[]{:S(2)}, u32[]{:S(2)}) %collective-permute-start.19) | collective-permute-done | bytes 262176 | tf_op jit(solution)/shard_map/ppermute | solution.py:420
  109.0 3.4 %collective-permute-done.23.refs_7_ = bf16[16,4096]{1,0:T(8,128)(2,1)S(1)} collective-permute-done((bf16[16,4096]{1,0:T(8,128)(2,1)S(1)}, bf16[16,4096]{1,0:T(8,128)(2,1)S(1)}, u32[]{:S(2)}, u32[]{:S(2)}) %collective-permute-start.23) | collective-permute-done | bytes 131104 | tf_op jit(solution)/shard_map/ppermute | solution.py:420
  115.2 4.6 %copy-done.1 = bf16[8192,768]{1,0:T(8,128)(2,1)S(1)} copy-done((bf16[8192,768]{1,0:T(8,128)(2,1)S(1)}, bf16[8192,768]{1,0:T(8,128)(2,1)}, u32[]{:S(2)}) %copy-start.1) | copy-done | bytes 12582936
  119.8 12.0 %hidden.1.hidden_ref = bf16[256,768]{1,0:T(8,128)(2,1)S(1)} custom-call(bf16[16,8192]{1,0:T(8,128)(2,1)S(1)} %get-tuple-element.89.refs_0_, bf16[16,8192]{1,0:T(8,128)(2,1)S(1)} %collective-permute-done.17.refs_1_, bf16[16,8192]{1,0:T(8,128)(2,1)S(1)} %collective-permute-done.18.refs_2_, bf16[16,8192]{1,0:T(8,128)(2,1)S(1)} %collective-permute-done.19.refs_3_, ...), custom_call_target="tpu_custom_call" | custom-call | flops 6442450944 | bytes 29360128 | tf_op jit(solution)/shard_map/hidden/pallas_call | solution.py:274
  131.8 2.9 %down.3 = (bf16[128,4096]{1,0:T(8,128)(2,1)S(1)}, bf16[128,4096]{1,0:T(8,128)(2,1)S(1)}) custom-call(bf16[256,768]{1,0:T(8,128)(2,1)S(1)} %hidden.1.hidden_ref, bf16[768,8192]{1,0:T(8,128)(2,1)S(1)} %bitcast.4), custom_call_target="tpu_custom_call" | custom-call | flops 1610612736 | bytes 8388608 | tf_op jit(solution)/shard_map/down/pallas_call | solution.py:312
  135.0 2.9 %down.2 = (bf16[128,4096]{1,0:T(8,128)(2,1)S(1)}, bf16[128,4096]{1,0:T(8,128)(2,1)S(1)}) custom-call(bf16[256,768]{1,0:T(8,128)(2,1)S(1)} %hidden.1.hidden_ref, bf16[768,8192]{1,0:T(8,128)(2,1)S(1)} %bitcast.4), custom_call_target="tpu_custom_call" | custom-call | flops 1610612736 | bytes 8388608 | tf_op jit(solution)/shard_map/down/pallas_call | solution.py:312
  145.4 2.0 %collective-permute-start.37 = (bf16[16,4096]{1,0:T(8,128)(2,1)S(1)}, bf16[16,4096]{1,0:T(8,128)(2,1)S(1)}, u32[]{:S(2)}, u32[]{:S(2)}) collective-permute-start(bf16[16,4096]{1,0:T(8,128)(2,1)S(1)} %pad_maximum_fusion), channel_id=1, source_target_pairs={{0,4},{1,5},{4,8},{5,9},{8,12},{9,13},{12,14},{13,15},{14,10},{15,... | collective-permute-start | bytes 393224 | tf_op jit(solution)/shard_map/ppermute | solution.py:420
  153.2 2.1 %collective-permute-start.39 = (bf16[16,4096]{1,0:T(8,128)(2,1)S(1)}, bf16[16,4096]{1,0:T(8,128)(2,1)S(1)}, u32[]{:S(2)}, u32[]{:S(2)}) collective-permute-start(bf16[16,4096]{1,0:T(8,128)(2,1)S(1)} %get-tuple-element.96), channel_id=1, source_target_pairs={{0,4},{1,5},{4,8},{5,9},{8,12},{9,13},{12,14},{13,15},{14,10},{15,... | collective-permute-start | bytes 393224 | tf_op jit(solution)/shard_map/ppermute | solution.py:420
  155.3 2.0 %collective-permute-done.48 = bf16[16,4096]{1,0:T(8,128)(2,1)S(1)} collective-permute-done((bf16[16,4096]{1,0:T(8,128)(2,1)S(1)}, bf16[16,4096]{1,0:T(8,128)(2,1)S(1)}, u32[]{:S(2)}, u32[]{:S(2)}) %collective-permute-start.48) | collective-permute-done | bytes 131104 | tf_op jit(solution)/shard_map/ppermute | solution.py:420
  158.4 1.9 %collective-permute-start.50 = (bf16[16,4096]{1,0:T(8,128)(2,1)S(1)}, bf16[16,4096]{1,0:T(8,128)(2,1)S(1)}, u32[]{:S(2)}, u32[]{:S(2)}) collective-permute-start(bf16[16,4096]{1,0:T(8,128)(2,1)S(1)} %get-tuple-element.108), channel_id=1, source_target_pairs={{0,4},{1,5},{4,8},{5,9},{8,12},{9,13},{12,14},{13,15},{14,10},{15,... | collective-permute-start | bytes 393224 | tf_op jit(solution)/shard_map/ppermute | solution.py:420
  161.0 2.3 %collective-permute-start.41 = (bf16[16,4096]{1,0:T(8,128)(2,1)S(1)}, bf16[16,4096]{1,0:T(8,128)(2,1)S(1)}, u32[]{:S(2)}, u32[]{:S(2)}) collective-permute-start(bf16[16,4096]{1,0:T(8,128)(2,1)S(1)} %get-tuple-element.98), channel_id=1, source_target_pairs={{0,4},{1,5},{4,8},{5,9},{8,12},{9,13},{12,14},{13,15},{14,10},{15,... | collective-permute-start | bytes 393224 | tf_op jit(solution)/shard_map/ppermute | solution.py:420
  166.1 2.2 %collective-permute-done.42.refs_3_ = bf16[16,4096]{1,0:T(8,128)(2,1)S(1)} collective-permute-done((bf16[16,4096]{1,0:T(8,128)(2,1)S(1)}, bf16[16,4096]{1,0:T(8,128)(2,1)S(1)}, u32[]{:S(2)}, u32[]{:S(2)}) %collective-permute-start.42) | collective-permute-done | bytes 131104 | tf_op jit(solution)/shard_map/ppermute | solution.py:421
  169.0 4.3 %spread.1 = bf16[128,8192]{1,0:T(8,128)(2,1)} custom-call(bf16[128,4096]{1,0:T(8,128)(2,1)} %copy-done.7, bf16[128,4096]{1,0:T(8,128)(2,1)} %copy-done.11, bf16[16,4096]{1,0:T(8,128)(2,1)} %copy-done.14, bf16[16,4096]{1,0:T(8,128)(2,1)} %copy-done.15, bf16[128,4096]{1,0:T(8,128)(2,1)} %copy-done.6, bf16[128,4096]{1,0:T(8,128)(2,1)} %copy-done.10, ...), custom_call_target="tpu_custom_call" | custom-call | tf_op jit(solution)/shard_map/spread/pallas_call | solution.py:362
  (156 shorter events, 47.2 us)
Async XLA Ops:
  3.1 15.1 %collective-permute-start = (bf16[256,1024]{1,0:T(8,128)(2,1)S(1)}, bf16[256,1024]{1,0:T(8,128)(2,1)S(1)}, u32[]{:S(2)}, u32[]{:S(2)}) collective-permute-start(bf16[256,1024]{1,0:T(8,128)(2,1)S(1)} %constant_dynamic-update-slice_fusion.own_ref), channel_id=1, source_target_pairs={{0,4},{1,5},{4,8},{5,9},{8,12},{9,13},{12,14},{13,15},{14,10},{15,... | collective-permute-start | bytes 1572872 | tf_op jit(solution)/shard_map/ppermute | solution.py:420
  5.7 14.0 %collective-permute-start.1 = (bf16[256,1024]{1,0:T(8,128)(2,1)S(1)}, bf16[256,1024]{1,0:T(8,128)(2,1)S(1)}, u32[]{:S(2)}, u32[]{:S(2)}) collective-permute-start(bf16[256,1024]{1,0:T(8,128)(2,1)S(1)} %constant_dynamic-update-slice_fusion.own_ref), channel_id=1, source_target_pairs={{4,0},{5,1},{8,4},{9,5},{12,8},{13,9},{14,12},{15,13},{10,14},{11,... | collective-permute-start | bytes 1572872 | tf_op jit(solution)/shard_map/ppermute | solution.py:421
  20.2 13.8 %collective-permute-start.3 = (bf16[256,1024]{1,0:T(8,128)(2,1)S(1)}, bf16[256,1024]{1,0:T(8,128)(2,1)S(1)}, u32[]{:S(2)}, u32[]{:S(2)}) collective-permute-start(bf16[256,1024]{1,0:T(8,128)(2,1)S(1)} %collective-permute-done.refs_0_), channel_id=1, source_target_pairs={{0,4},{1,5},{4,8},{5,9},{8,12},{9,13},{12,14},{13,15},{14,10},{15,... | collective-permute-start | bytes 1572872 | tf_op jit(solution)/shard_map/ppermute | solution.py:420
  21.8 13.6 %collective-permute-start.4 = (bf16[256,1024]{1,0:T(8,128)(2,1)S(1)}, bf16[256,1024]{1,0:T(8,128)(2,1)S(1)}, u32[]{:S(2)}, u32[]{:S(2)}) collective-permute-start(bf16[256,1024]{1,0:T(8,128)(2,1)S(1)} %collective-permute-done.1.refs_2_), channel_id=1, source_target_pairs={{4,0},{5,1},{8,4},{9,5},{12,8},{13,9},{14,12},{15,13},{10,14},{11,... | collective-permute-start | bytes 1572872 | tf_op jit(solution)/shard_map/ppermute | solution.py:421
  35.9 13.9 %collective-permute-start.7 = (bf16[256,1024]{1,0:T(8,128)(2,1)S(1)}, bf16[256,1024]{1,0:T(8,128)(2,1)S(1)}, u32[]{:S(2)}, u32[]{:S(2)}) collective-permute-start(bf16[256,1024]{1,0:T(8,128)(2,1)S(1)} %collective-permute-done.3.refs_0_), channel_id=1, source_target_pairs={{0,4},{1,5},{4,8},{5,9},{8,12},{9,13},{12,14},{13,15},{14,10},{15,... | collective-permute-start | bytes 1572872 | tf_op jit(solution)/shard_map/ppermute | solution.py:420
  37.5 13.6 %collective-permute-start.8 = (bf16[256,1024]{1,0:T(8,128)(2,1)S(1)}, bf16[256,1024]{1,0:T(8,128)(2,1)S(1)}, u32[]{:S(2)}, u32[]{:S(2)}) collective-permute-start(bf16[256,1024]{1,0:T(8,128)(2,1)S(1)} %collective-permute-done.4.refs_2_), channel_id=1, source_target_pairs={{4,0},{5,1},{8,4},{9,5},{12,8},{13,9},{14,12},{15,13},{10,14},{11,... | collective-permute-start | bytes 1572872 | tf_op jit(solution)/shard_map/ppermute | solution.py:421
  51.7 8.3 %collective-permute-start.11 = (bf16[128,1024]{1,0:T(8,128)(2,1)S(1)}, bf16[128,1024]{1,0:T(8,128)(2,1)S(1)}, u32[]{:S(2)}, u32[]{:S(2)}) collective-permute-start(bf16[128,1024]{1,0:T(8,128)(2,1)S(1)} %slice.136), channel_id=1, source_target_pairs={{0,4},{1,5},{4,8},{5,9},{8,12},{9,13},{12,14},{13,15},{14,10},{15,... | collective-permute-start | bytes 786440 | tf_op jit(solution)/shard_map/ppermute | solution.py:420
  53.2 7.9 %collective-permute-start.12 = (bf16[128,1024]{1,0:T(8,128)(2,1)S(1)}, bf16[128,1024]{1,0:T(8,128)(2,1)S(1)}, u32[]{:S(2)}, u32[]{:S(2)}) collective-permute-start(bf16[128,1024]{1,0:T(8,128)(2,1)S(1)} %slice.137), channel_id=1, source_target_pairs={{4,0},{5,1},{8,4},{9,5},{12,8},{13,9},{14,12},{15,13},{10,14},{11,... | collective-permute-start | bytes 786440 | tf_op jit(solution)/shard_map/ppermute | solution.py:421
  67.0 10.4 %collective-permute-start.17 = (bf16[16,8192]{1,0:T(8,128)(2,1)S(1)}, bf16[16,8192]{1,0:T(8,128)(2,1)S(1)}, u32[]{:S(2)}, u32[]{:S(2)}) collective-permute-start(bf16[16,8192]{1,0:T(8,128)(2,1)S(1)} %get-tuple-element.89.refs_0_), channel_id=1, source_target_pairs={{0,4},{1,5},{4,8},{5,9},{8,12},{9,13},{12,14},{13,15},{14,10},{15,... | collective-permute-start | bytes 786440 | tf_op jit(solution)/shard_map/ppermute | solution.py:420
  71.6 14.6 %collective-permute-start.20 = (bf16[16,8192]{1,0:T(8,128)(2,1)S(1)}, bf16[16,8192]{1,0:T(8,128)(2,1)S(1)}, u32[]{:S(2)}, u32[]{:S(2)}) collective-permute-start(bf16[16,8192]{1,0:T(8,128)(2,1)S(1)} %get-tuple-element.89.refs_0_), channel_id=1, source_target_pairs={{4,0},{5,1},{8,4},{9,5},{12,8},{13,9},{14,12},{15,13},{10,14},{11,... | collective-permute-start | bytes 786440 | tf_op jit(solution)/shard_map/ppermute | solution.py:421
  77.4 13.3 %collective-permute-start.18 = (bf16[16,8192]{1,0:T(8,128)(2,1)S(1)}, bf16[16,8192]{1,0:T(8,128)(2,1)S(1)}, u32[]{:S(2)}, u32[]{:S(2)}) collective-permute-start(bf16[16,8192]{1,0:T(8,128)(2,1)S(1)} %collective-permute-done.17.refs_1_), channel_id=1, source_target_pairs={{0,4},{1,5},{4,8},{5,9},{8,12},{9,13},{12,14},{13,15},{14,10},{15,... | collective-permute-start | bytes 786440 | tf_op jit(solution)/shard_map/ppermute | solution.py:420
  86.2 13.1 %collective-permute-start.21 = (bf16[16,8192]{1,0:T(8,128)(2,1)S(1)}, bf16[16,8192]{1,0:T(8,128)(2,1)S(1)}, u32[]{:S(2)}, u32[]{:S(2)}) collective-permute-start(bf16[16,8192]{1,0:T(8,128)(2,1)S(1)} %collective-permute-done.20.refs_4_), channel_id=1, source_target_pairs={{4,0},{5,1},{8,4},{9,5},{12,8},{13,9},{14,12},{15,13},{10,14},{11,... | collective-permute-start | bytes 786440 | tf_op jit(solution)/shard_map/ppermute | solution.py:421
  90.7 14.7 %collective-permute-start.19 = (bf16[16,8192]{1,0:T(8,128)(2,1)S(1)}, bf16[16,8192]{1,0:T(8,128)(2,1)S(1)}, u32[]{:S(2)}, u32[]{:S(2)}) collective-permute-start(bf16[16,8192]{1,0:T(8,128)(2,1)S(1)} %collective-permute-done.18.refs_2_), channel_id=1, source_target_pairs={{0,4},{1,5},{4,8},{5,9},{8,12},{9,13},{12,14},{13,15},{14,10},{15,... | collective-permute-start | bytes 786440 | tf_op jit(solution)/shard_map/ppermute | solution.py:420
  99.3 7.1 %collective-permute-start.22 = (bf16[16,8192]{1,0:T(8,128)(2,1)S(1)}, bf16[16,8192]{1,0:T(8,128)(2,1)S(1)}, u32[]{:S(2)}, u32[]{:S(2)}) collective-permute-start(bf16[16,8192]{1,0:T(8,128)(2,1)S(1)} %collective-permute-done.21.refs_5_), channel_id=1, source_target_pairs={{4,0},{5,1},{8,4},{9,5},{12,8},{13,9},{14,12},{15,13},{10,14},{11,... | collective-permute-start | bytes 786440 | tf_op jit(solution)/shard_map/ppermute | solution.py:421
  99.9 6.5 %collective-permute-start.25 = (bf16[16,8192]{1,0:T(8,128)(2,1)S(1)}, bf16[16,8192]{1,0:T(8,128)(2,1)S(1)}, u32[]{:S(2)}, u32[]{:S(2)}) collective-permute-start(bf16[16,8192]{1,0:T(8,128)(2,1)S(1)} %get-tuple-element.89.refs_0_), channel_id=1, source_target_pairs={{0,1},{1,0},{2,3},{3,2},{4,5},{5,4},{6,7},{7,6},{8,9},{9,8},{10,11... | collective-permute-start | bytes 786440 | tf_op jit(solution)/shard_map/ppermute | solution.py:422
  99.9 8.3 %collective-permute-start.26 = (bf16[16,8192]{1,0:T(8,128)(2,1)S(1)}, bf16[16,8192]{1,0:T(8,128)(2,1)S(1)}, u32[]{:S(2)}, u32[]{:S(2)}) collective-permute-start(bf16[16,8192]{1,0:T(8,128)(2,1)S(1)} %collective-permute-done.17.refs_1_), channel_id=1, source_target_pairs={{0,1},{1,0},{2,3},{3,2},{4,5},{5,4},{6,7},{7,6},{8,9},{9,8},{10,11... | collective-permute-start | bytes 786440 | tf_op jit(solution)/shard_map/ppermute | solution.py:422
  100.4 8.1 %collective-permute-start.29 = (bf16[16,8192]{1,0:T(8,128)(2,1)S(1)}, bf16[16,8192]{1,0:T(8,128)(2,1)S(1)}, u32[]{:S(2)}, u32[]{:S(2)}) collective-permute-start(bf16[16,8192]{1,0:T(8,128)(2,1)S(1)} %collective-permute-done.20.refs_4_), channel_id=1, source_target_pairs={{0,1},{1,0},{2,3},{3,2},{4,5},{5,4},{6,7},{7,6},{8,9},{9,8},{10,11... | collective-permute-start | bytes 786440 | tf_op jit(solution)/shard_map/ppermute | solution.py:422
  106.4 7.5 %collective-permute-start.30 = (bf16[16,8192]{1,0:T(8,128)(2,1)S(1)}, bf16[16,8192]{1,0:T(8,128)(2,1)S(1)}, u32[]{:S(2)}, u32[]{:S(2)}) collective-permute-start(bf16[16,8192]{1,0:T(8,128)(2,1)S(1)} %collective-permute-done.21.refs_5_), channel_id=1, source_target_pairs={{0,1},{1,0},{2,3},{3,2},{4,5},{5,4},{6,7},{7,6},{8,9},{9,8},{10,11... | collective-permute-start | bytes 786440 | tf_op jit(solution)/shard_map/ppermute | solution.py:422
  106.4 6.0 %collective-permute-start.23 = (bf16[16,4096]{1,0:T(8,128)(2,1)S(1)}, bf16[16,4096]{1,0:T(8,128)(2,1)S(1)}, u32[]{:S(2)}, u32[]{:S(2)}) collective-permute-start(bf16[16,4096]{1,0:T(8,128)(2,1)S(1)} %slice.180), channel_id=1, source_target_pairs={{0,4},{1,5},{4,8},{5,9},{8,12},{9,13},{12,14},{13,15},{14,10},{15,... | collective-permute-start | bytes 393224 | tf_op jit(solution)/shard_map/ppermute | solution.py:420
  108.2 5.6 %collective-permute-start.24 = (bf16[16,4096]{1,0:T(8,128)(2,1)S(1)}, bf16[16,4096]{1,0:T(8,128)(2,1)S(1)}, u32[]{:S(2)}, u32[]{:S(2)}) collective-permute-start(bf16[16,4096]{1,0:T(8,128)(2,1)S(1)} %slice.181), channel_id=1, source_target_pairs={{4,0},{5,1},{8,4},{9,5},{12,8},{13,9},{14,12},{15,13},{10,14},{11,... | collective-permute-start | bytes 393224 | tf_op jit(solution)/shard_map/ppermute | solution.py:421
  108.5 6.7 %collective-permute-start.28 = (bf16[16,8192]{1,0:T(8,128)(2,1)S(1)}, bf16[16,8192]{1,0:T(8,128)(2,1)S(1)}, u32[]{:S(2)}, u32[]{:S(2)}) collective-permute-start(bf16[16,8192]{1,0:T(8,128)(2,1)S(1)} %collective-permute-done.19.refs_3_), channel_id=1, source_target_pairs={{0,1},{1,0},{2,3},{3,2},{4,5},{5,4},{6,7},{7,6},{8,9},{9,8},{10,11... | collective-permute-start | bytes 786440 | tf_op jit(solution)/shard_map/ppermute | solution.py:422
  108.5 6.7 %collective-permute-start.31 = (bf16[16,8192]{1,0:T(8,128)(2,1)S(1)}, bf16[16,8192]{1,0:T(8,128)(2,1)S(1)}, u32[]{:S(2)}, u32[]{:S(2)}) collective-permute-start(bf16[16,8192]{1,0:T(8,128)(2,1)S(1)} %collective-permute-done.22.refs_6_), channel_id=1, source_target_pairs={{0,1},{1,0},{2,3},{3,2},{4,5},{5,4},{6,7},{7,6},{8,9},{9,8},{10,11... | collective-permute-start | bytes 786440 | tf_op jit(solution)/shard_map/ppermute | solution.py:422
  143.0 6.1 %collective-permute-start.46 = (bf16[16,4096]{1,0:T(8,128)(2,1)S(1)}, bf16[16,4096]{1,0:T(8,128)(2,1)S(1)}, u32[]{:S(2)}, u32[]{:S(2)}) collective-permute-start(bf16[16,4096]{1,0:T(8,128)(2,1)S(1)} %pad_maximum_fusion.2), channel_id=1, source_target_pairs={{0,4},{1,5},{4,8},{5,9},{8,12},{9,13},{12,14},{13,15},{14,10},{15,... | collective-permute-start | bytes 393224 | tf_op jit(solution)/shard_map/ppermute | solution.py:420
  144.8 6.1 %collective-permute-start.47 = (bf16[16,4096]{1,0:T(8,128)(2,1)S(1)}, bf16[16,4096]{1,0:T(8,128)(2,1)S(1)}, u32[]{:S(2)}, u32[]{:S(2)}) collective-permute-start(bf16[16,4096]{1,0:T(8,128)(2,1)S(1)} %pad_maximum_fusion.3), channel_id=1, source_target_pairs={{4,0},{5,1},{8,4},{9,5},{12,8},{13,9},{14,12},{15,13},{10,14},{11,... | collective-permute-start | bytes 393224 | tf_op jit(solution)/shard_map/ppermute | solution.py:421
  145.4 7.6 %collective-permute-start.37 = (bf16[16,4096]{1,0:T(8,128)(2,1)S(1)}, bf16[16,4096]{1,0:T(8,128)(2,1)S(1)}, u32[]{:S(2)}, u32[]{:S(2)}) collective-permute-start(bf16[16,4096]{1,0:T(8,128)(2,1)S(1)} %pad_maximum_fusion), channel_id=1, source_target_pairs={{0,4},{1,5},{4,8},{5,9},{8,12},{9,13},{12,14},{13,15},{14,10},{15,... | collective-permute-start | bytes 393224 | tf_op jit(solution)/shard_map/ppermute | solution.py:420
  147.5 5.6 %collective-permute-start.38 = (bf16[16,4096]{1,0:T(8,128)(2,1)S(1)}, bf16[16,4096]{1,0:T(8,128)(2,1)S(1)}, u32[]{:S(2)}, u32[]{:S(2)}) collective-permute-start(bf16[16,4096]{1,0:T(8,128)(2,1)S(1)} %pad_maximum_fusion.1), channel_id=1, source_target_pairs={{4,0},{5,1},{8,4},{9,5},{12,8},{13,9},{14,12},{15,13},{10,14},{11,... | collective-permute-start | bytes 393224 | tf_op jit(solution)/shard_map/ppermute | solution.py:421
  151.0 6.3 %collective-permute-start.48 = (bf16[16,4096]{1,0:T(8,128)(2,1)S(1)}, bf16[16,4096]{1,0:T(8,128)(2,1)S(1)}, u32[]{:S(2)}, u32[]{:S(2)}) collective-permute-start(bf16[16,4096]{1,0:T(8,128)(2,1)S(1)} %get-tuple-element.106), channel_id=1, source_target_pairs={{0,4},{1,5},{4,8},{5,9},{8,12},{9,13},{12,14},{13,15},{14,10},{15,... | collective-permute-start | bytes 393224 | tf_op jit(solution)/shard_map/ppermute | solution.py:420
  152.4 5.9 %collective-permute-start.49 = (bf16[16,4096]{1,0:T(8,128)(2,1)S(1)}, bf16[16,4096]{1,0:T(8,128)(2,1)S(1)}, u32[]{:S(2)}, u32[]{:S(2)}) collective-permute-start(bf16[16,4096]{1,0:T(8,128)(2,1)S(1)} %get-tuple-element.107), channel_id=1, source_target_pairs={{4,0},{5,1},{8,4},{9,5},{12,8},{13,9},{14,12},{15,13},{10,14},{11,... | collective-permute-start | bytes 393224 | tf_op jit(solution)/shard_map/ppermute | solution.py:421
  153.2 7.3 %collective-permute-start.39 = (bf16[16,4096]{1,0:T(8,128)(2,1)S(1)}, bf16[16,4096]{1,0:T(8,128)(2,1)S(1)}, u32[]{:S(2)}, u32[]{:S(2)}) collective-permute-start(bf16[16,4096]{1,0:T(8,128)(2,1)S(1)} %get-tuple-element.96), channel_id=1, source_target_pairs={{0,4},{1,5},{4,8},{5,9},{8,12},{9,13},{12,14},{13,15},{14,10},{15,... | collective-permute-start | bytes 393224 | tf_op jit(solution)/shard_map/ppermute | solution.py:420
  155.3 5.7 %collective-permute-start.40 = (bf16[16,4096]{1,0:T(8,128)(2,1)S(1)}, bf16[16,4096]{1,0:T(8,128)(2,1)S(1)}, u32[]{:S(2)}, u32[]{:S(2)}) collective-permute-start(bf16[16,4096]{1,0:T(8,128)(2,1)S(1)} %get-tuple-element.97), channel_id=1, source_target_pairs={{4,0},{5,1},{8,4},{9,5},{12,8},{13,9},{14,12},{15,13},{10,14},{11,... | collective-permute-start | bytes 393224 | tf_op jit(solution)/shard_map/ppermute | solution.py:421
  158.4 5.6 %collective-permute-start.50 = (bf16[16,4096]{1,0:T(8,128)(2,1)S(1)}, bf16[16,4096]{1,0:T(8,128)(2,1)S(1)}, u32[]{:S(2)}, u32[]{:S(2)}) collective-permute-start(bf16[16,4096]{1,0:T(8,128)(2,1)S(1)} %get-tuple-element.108), channel_id=1, source_target_pairs={{0,4},{1,5},{4,8},{5,9},{8,12},{9,13},{12,14},{13,15},{14,10},{15,... | collective-permute-start | bytes 393224 | tf_op jit(solution)/shard_map/ppermute | solution.py:420
  161.0 5.0 %collective-permute-start.41 = (bf16[16,4096]{1,0:T(8,128)(2,1)S(1)}, bf16[16,4096]{1,0:T(8,128)(2,1)S(1)}, u32[]{:S(2)}, u32[]{:S(2)}) collective-permute-start(bf16[16,4096]{1,0:T(8,128)(2,1)S(1)} %get-tuple-element.98), channel_id=1, source_target_pairs={{0,4},{1,5},{4,8},{5,9},{8,12},{9,13},{12,14},{13,15},{14,10},{15,... | collective-permute-start | bytes 393224 | tf_op jit(solution)/shard_map/ppermute | solution.py:420
  (41 other events, 385.9 us)

commit v3 on v2

v3 whole, which is shorter than its diff:
```python
import functools
import math

import jax
import jax.numpy as jnp
from jax import lax
from jax.experimental import pallas as pl
from jax.experimental.pallas import tpu as pltpu
from jax.sharding import PartitionSpec as P

HQ = 64
HK = 8
DH = 128
CAP = 16
GROUP = HQ // HK
WIDE = GROUP * DH
LOG_SCALE = math.log2(math.e) / math.sqrt(DH)
MASKED = -1e30
PIECES = 2
SUM_LIMIT = 2.0**100
PARTS = 3
STACK = 4
MIB = 1 << 20


def in_hbm(x):
    return pltpu.with_memory_space_constraint(x, pltpu.HBM)


def ring_order(chips):
    return list(range(0, chips, 2)) + list(range(1, chips, 2))[::-1]


def permutations(chips):
    order = ring_order(chips)
    right, left = [], []
    for place in range(chips):
        here, there = order[place], order[(place + 1) % chips]
        for core in range(2):
            right.append((2 * here + core, 2 * there + core))
            left.append((2 * there + core, 2 * here + core))
    sibling = [(i, i ^ 1) for i in range(2 * chips)]
    return right, left, sibling


def chip_at(me, step, chips):
    chip = me // 2
    place = jnp.where(chip % 2 == 0, chip // 2, chips - 1 - chip // 2)
    source = (place - step + 2 * chips) % chips
    return jnp.where(source < chips // 2, 2 * source, 2 * (chips - 1 - source) + 1)


def head_rows(q_ref, first):
    return jnp.concatenate(
        [q_ref[:, h * DH : (h + 1) * DH] for h in range(first, first + STACK)], axis=0
    )


def with_ones(values):
    return jnp.concatenate([values, jnp.ones_like(values)], axis=1)


def scores_of(queries, keys):
    return LOG_SCALE * lax.dot_general(
        queries, keys, (((1,), (1,)), ((), ())), preferred_element_type=jnp.float32
    )


def weights_of(scores, shift):
    return jnp.exp2(scores - jnp.concatenate([shift] * (scores.shape[1] // DH), axis=1))


def row_top(scores):
    return jnp.broadcast_to(jnp.max(scores, axis=1, keepdims=True), (scores.shape[0], DH))


def chip_block(own_ref, sib_ref):
    tokens = own_ref.shape[0] // 2
    keys = jnp.concatenate([own_ref[:tokens], sib_ref[:tokens]], axis=0)
    values = jnp.concatenate([own_ref[tokens:], sib_ref[tokens:]], axis=0)
    return keys, with_ones(values)


def allowed_own(me, tokens):
    shape = (STACK * tokens, 2 * tokens)
    token = lax.broadcasted_iota(jnp.int32, shape, 0) % tokens
    column = lax.broadcasted_iota(jnp.int32, shape, 1)
    limit = jnp.where(me % 2 == 1, 2 * tokens, tokens)
    return column <= jnp.where(column < tokens, token, limit - 1)


def own_kernel(me_ref, q_ref, own_ref, sib_ref, acc_ref, total_ref, shift_ref):
    tokens = q_ref.shape[0]
    keys, values = chip_block(own_ref, sib_ref)
    allowed = allowed_own(me_ref[0], tokens)
    for first in range(0, GROUP, STACK):
        rows = slice(first * tokens, (first + STACK) * tokens)
        scores = jnp.where(allowed, scores_of(head_rows(q_ref, first), keys), MASKED)
        shift = row_top(scores)
        weights = weights_of(scores, shift).astype(jnp.bfloat16)
        update = jnp.dot(weights, values, preferred_element_type=jnp.float32)
        acc_ref[0, rows, :] = update[:, :DH]
        total_ref[0, rows, :] = update[:, DH:]
        shift_ref[0, rows, :] = shift


def fold_chip(q_ref, keys, values, shift_ref, acc_ref, total_ref):
    tokens = q_ref.shape[0]
    for first in range(0, GROUP, STACK):
        rows = slice(first * tokens, (first + STACK) * tokens)
        scores = scores_of(head_rows(q_ref, first), keys)
        weights = weights_of(scores, shift_ref[0, rows, :]).astype(jnp.bfloat16)
        update = jnp.dot(weights, values, preferred_element_type=jnp.float32)
        acc_ref[0, rows, :] += update[:, :DH]
        total_ref[0, rows, :] += update[:, DH:]


def step_kernel(chips, step, me_ref, q_ref, *refs):
    pieces, shift_ref, state_in, state = refs[:4], refs[4], refs[5:7], refs[7:9]
    me = me_ref[0]
    for source, target in zip(state_in, state):
        target[...] = source[...]
    for place, own_ref, sib_ref in ((step, *pieces[:2]), (-step, *pieces[2:])):

        @pl.when(chip_at(me, place, chips) < me // 2)
        def _():
            keys, values = chip_block(own_ref, sib_ref)
            fold_chip(q_ref, keys, values, shift_ref, *state)


def running_attention(chips, me, sources, queries, out_ref, scratch, sem):
    q_ref, keys_ref, values_ref, acc_ref, total_ref, top_ref = scratch
    tokens = q_ref.shape[0]
    half = chips // 2
    places = [0] + [p for step in range(1, half) for p in (step, -step)] + [half]

    def fetch(source, target):
        copy = pltpu.make_async_copy(source, target, sem)
        copy.start()
        copy.wait()

    def one_head(head, carry):
        columns = pl.ds(pl.multiple_of(head * DH, DH), DH)
        wide = pl.ds(pl.multiple_of(head * WIDE, WIDE), WIDE)
        fetch(queries.at[:, wide], q_ref)
        for i, place in enumerate(places):
            if place != half:
                for core in range(2):
                    rows = pl.ds(core * tokens, tokens)
                    block = sources[2 * i + core]
                    fetch(block.at[pl.ds(0, tokens), columns], keys_ref.at[i, rows])
                    fetch(block.at[pl.ds(tokens, tokens), columns], values_ref.at[i, rows])
            else:
                key, value, sib_key, sib_value = sources[2 * i :]
                for core, (k, v) in enumerate(((key, value), (sib_key, sib_value))):
                    rows = pl.ds(core * tokens, tokens)
                    fetch(k.at[:, columns], keys_ref.at[i, rows])
                    fetch(v.at[:, columns], values_ref.at[i, rows])
        acc_ref[...] = jnp.zeros_like(acc_ref)
        total_ref[...] = jnp.zeros_like(total_ref)
        top_ref[...] = jnp.full_like(top_ref, 2 * MASKED)

        def one_chip(i, inner):
            forward = (i + 1) // 2
            place = jnp.where(i % 2 == 1, forward, -forward)
            chip = chip_at(me, place, chips)

            @pl.when(chip <= me // 2)
            def _():
                allowed = jnp.logical_or(allowed_own(me, tokens), chip < me // 2)
                keys, values = keys_ref[i], with_ones(values_ref[i])
                for first in range(0, GROUP, STACK):
                    rows = slice(first * tokens, (first + STACK) * tokens)
                    scores = jnp.where(allowed, scores_of(head_rows(q_ref, first), keys), MASKED)
                    old = top_ref[rows, :]
                    top = jnp.maximum(old, row_top(scores))
                    factor = jnp.exp2(old - top)
                    weights = weights_of(scores, top).astype(jnp.bfloat16)
                    update = jnp.dot(weights, values, preferred_element_type=jnp.float32)
                    acc_ref[rows, :] = acc_ref[rows, :] * factor + update[:, :DH]
                    total_ref[rows, :] = total_ref[rows, :] * factor + update[:, DH:]
                    top_ref[rows, :] = top

            return inner

        lax.fori_loop(0, chips, one_chip, 0)
        write_heads(out_ref, head, acc_ref[...], total_ref[...], tokens)
        return carry

    lax.fori_loop(0, HK, one_head, 0)


def write_heads(out_ref, head, acc, total, tokens):
    result = (acc / total).astype(jnp.bfloat16)
    columns = pl.ds(pl.multiple_of(head * WIDE, WIDE), WIDE)
    out_ref[:, columns] = jnp.concatenate(
        [result[h * tokens : (h + 1) * tokens] for h in range(GROUP)], axis=1
    )


def last_kernel(chips, me_ref, q_ref, *refs):
    (key, value, sib_key, sib_value, shift_ref), state_in = refs[:5], refs[5:7]
    gain_ref, table_ref, queries, sources = refs[7], refs[8], refs[9], refs[10 : 12 + 2 * chips]
    out_ref, picked_ref, acc_ref, total_ref, worst_ref, sem = refs[12 + 2 * chips : 18 + 2 * chips]
    scratch = refs[18 + 2 * chips :]
    tokens = q_ref.shape[0]
    head = pl.program_id(0)
    me = me_ref[0]
    acc_ref[...] = state_in[0][...]
    total_ref[...] = state_in[1][...]

    @pl.when(chip_at(me, chips // 2, chips) < me // 2)
    def _():
        keys = jnp.concatenate([key[...], sib_key[...]], axis=0)
        values = with_ones(jnp.concatenate([value[...], sib_value[...]], axis=0))
        fold_chip(q_ref, keys, values, shift_ref, acc_ref, total_ref)

    write_heads(out_ref, head, acc_ref[0], total_ref[0], tokens)

    @pl.when(head == 0)
    def _():
        worst_ref[...] = jnp.zeros_like(worst_ref)

    worst_ref[...] = jnp.maximum(worst_ref[...], total_ref[0])

    @pl.when(head == HK - 1)
    def _():
        fits = jnp.max(worst_ref[...]) <= SUM_LIMIT

        @pl.when(jnp.logical_not(fits))
        def _():
            running_attention(chips, me, sources, queries, out_ref, scratch, sem)

        width = out_ref.shape[1]
        picked = jnp.dot(table_ref[...], out_ref[...], preferred_element_type=jnp.float32)
        mean = jnp.sum(picked * picked, axis=1, keepdims=True) / width
        picked_ref[...] = (picked * lax.rsqrt(mean + 1e-05) * gain_ref[...]).astype(jnp.bfloat16)


class Attention:
    def __init__(self, me, queries, chips):
        self.me, self.queries, self.chips = me, in_hbm(queries), chips
        tokens = queries.shape[0]
        self.head_block = pl.BlockSpec((tokens, WIDE), lambda g, me: (0, g))
        self.pair_block = pl.BlockSpec((2 * tokens, DH), lambda g, me: (0, g))
        self.kv_block = pl.BlockSpec((tokens, DH), lambda g, me: (0, g))
        self.state_block = pl.BlockSpec((1, GROUP * tokens, DH), lambda g, me: (g, 0, 0))
        self.state_shape = jax.ShapeDtypeStruct((HK, GROUP * tokens, DH), jnp.float32)

    def call(self, kernel, name, in_specs, out_specs, out_shape, args, scratch=(), aliases=None):
        tokens, width = self.queries.shape
        return pl.pallas_call(
            kernel,
            grid_spec=pltpu.PrefetchScalarGridSpec(
                num_scalar_prefetch=1,
                grid=(HK,),
                in_specs=[self.head_block] + in_specs,
                out_specs=out_specs,
                scratch_shapes=scratch,
            ),
            out_shape=out_shape,
            input_output_aliases=aliases or {},
            compiler_params=pltpu.CompilerParams(
                dimension_semantics=("arbitrary",), vmem_limit_bytes=16 * MIB
            ),
            cost_estimate=pl.CostEstimate(
                flops=4 * tokens * width * tokens, bytes_accessed=4 * MIB, transcendentals=0
            ),
            name=name,
        )(self.me, self.queries, *args)

    def own(self, own, sib):
        return self.call(
            own_kernel,
            "attend_own",
            [self.pair_block] * 2,
            [self.state_block] * 3,
            [self.state_shape] * 3,
            (own, sib),
        )

    def step(self, step, pieces, shift, state):
        return self.call(
            functools.partial(step_kernel, self.chips, step),
            "attend_step",
            [self.pair_block] * 4 + [self.state_block] * 3,
            [self.state_block] * 2,
            [self.state_shape] * 2,
            (*pieces, shift, *state),
            aliases={7: 0, 8: 1},
        )

    def last(self, pieces, shift, state, gain, table, sources):
        tokens, width = self.queries.shape
        whole = lambda shape: pl.BlockSpec(shape, lambda g, me: (0, 0))
        anywhere = pl.BlockSpec(memory_space=pl.ANY)
        rows = GROUP * tokens
        return self.call(
            functools.partial(last_kernel, self.chips),
            "attend_last",
            [self.kv_block] * 4
            + [self.state_block] * 3
            + [whole((1, width)), whole((CAP, tokens))]
            + [anywhere] * (1 + len(sources)),
            [whole((tokens, width)), whole((CAP, width))],
            [
                jax.ShapeDtypeStruct((tokens, width), jnp.bfloat16),
                jax.ShapeDtypeStruct((CAP, width), jnp.bfloat16),
            ],
            (*pieces, shift, *state, gain, table, self.queries, *sources),
            [
                pltpu.VMEM((1, rows, DH), jnp.float32),
                pltpu.VMEM((1, rows, DH), jnp.float32),
                pltpu.VMEM((rows, DH), jnp.float32),
                pltpu.SemaphoreType.DMA,
                pltpu.VMEM((tokens, WIDE), jnp.bfloat16),
                pltpu.VMEM((self.chips, 2 * tokens, DH), jnp.bfloat16),
                pltpu.VMEM((self.chips, 2 * tokens, DH), jnp.bfloat16),
            ]
            + [pltpu.VMEM((rows, DH), jnp.float32)] * 3,
        )


def stack_kernel(upper_ref, lower_ref, out_ref, sems):
    rows = upper_ref.shape[0]
    copies = [
        pltpu.make_async_copy(ref, out_ref.at[pl.ds(i * rows, rows)], sems.at[i])
        for i, ref in enumerate((upper_ref, lower_ref))
    ]
    for copy in copies:
        copy.start()
    for copy in copies:
        copy.wait()


def stack(upper, lower):
    anywhere = pl.BlockSpec(memory_space=pl.ANY)
    return pl.pallas_call(
        stack_kernel,
        in_specs=[anywhere] * 2,
        out_specs=anywhere,
        out_shape=jax.ShapeDtypeStruct((2 * upper.shape[0], upper.shape[1]), upper.dtype),
        scratch_shapes=[pltpu.SemaphoreType.DMA((2,))],
        name="stack",
    )(in_hbm(upper), in_hbm(lower))


def load_kernel(source_ref, target_ref, sem):
    copy = pltpu.make_async_copy(source_ref, target_ref, sem)
    copy.start()
    copy.wait()


def load(x):
    return pl.pallas_call(
        load_kernel,
        in_specs=[pl.BlockSpec(memory_space=pltpu.HBM)],
        out_specs=pl.BlockSpec(memory_space=pl.ANY),
        out_shape=pltpu.VMEM(x.shape, x.dtype),
        scratch_shapes=[pltpu.SemaphoreType.DMA],
        compiler_params=pltpu.CompilerParams(vmem_limit_bytes=MIB),
        cost_estimate=pl.CostEstimate(flops=0, bytes_accessed=x.size, transcendentals=0),
        name="load",
    )(in_hbm(x))


def hidden_kernel(chips, *refs):
    blocks, (gate_ref, up_ref, out_ref) = refs[: 2 * chips + 2], refs[2 * chips + 2 : 2 * chips + 5]
    rows_ref, gate_sum, up_sum, sems = refs[2 * chips + 5 :]
    width = rows_ref.shape[1]
    half = width // 2
    depth = min(1024, width)
    copies = []
    for core in range(2):
        mine = blocks[core * (chips + 1) : (core + 1) * (chips + 1)]
        for j in range(chips):
            rows = pl.ds((core * chips + j) * CAP, CAP)
            if j < chips - 1:
                copies.append((mine[j], rows_ref.at[rows, :]))
            else:
                copies.append((mine[j], rows_ref.at[rows, pl.ds(0, half)]))
                copies.append((mine[j + 1], rows_ref.at[rows, pl.ds(half, half)]))
    copies = [
        pltpu.make_async_copy(source, target, sems.at[i]) for i, (source, target) in enumerate(copies)
    ]
    for copy in copies:
        copy.start()
    gate_sum[...] = jnp.zeros_like(gate_sum)
    up_sum[...] = jnp.zeros_like(up_sum)
    for copy in copies:
        copy.wait()

    def one_part(step, carry):
        place = pl.ds(pl.multiple_of(step * depth, depth), depth)
        part = rows_ref[:, place]
        gate_sum[...] += jnp.dot(part, gate_ref[place, :], preferred_element_type=jnp.float32)
        up_sum[...] += jnp.dot(part, up_ref[place, :], preferred_element_type=jnp.float32)
        return carry

    lax.fori_loop(0, width // depth, one_part, 0)
    gate = gate_sum[...]
    out_ref[...] = (gate / (1.0 + jnp.exp(-gate)) * up_sum[...]).astype(jnp.bfloat16)


def hidden_call(chips, blocks, w_gate, w_up):
    rows = 2 * chips * CAP
    width, units = w_gate.shape
    vmem = pl.BlockSpec(memory_space=pltpu.VMEM)
    return pl.pallas_call(
        functools.partial(hidden_kernel, chips),
        in_specs=[pl.BlockSpec(memory_space=pl.ANY)] * len(blocks) + [vmem] * 2,
        out_specs=vmem,
        out_shape=jax.ShapeDtypeStruct((rows, units), jnp.bfloat16),
        scratch_shapes=[
            pltpu.VMEM((rows, width), jnp.bfloat16),
            pltpu.VMEM((rows, units), jnp.float32),
            pltpu.VMEM((rows, units), jnp.float32),
            pltpu.SemaphoreType.DMA((len(blocks),)),
        ],
        compiler_params=pltpu.CompilerParams(vmem_limit_bytes=16 * MIB),
        cost_estimate=pl.CostEstimate(
            flops=4 * rows * width * units,
            bytes_accessed=4 * width * units + 2 * rows * width,
            transcendentals=rows * units,
        ),
        name="hidden",
    )(*blocks, w_gate, w_up)


def down_kernel(hidden_ref, down_ref, own_ref, sib_ref):
    part = jnp.dot(hidden_ref[...], down_ref[...], preferred_element_type=jnp.float32)
    part = part.astype(jnp.bfloat16)
    middle = part.shape[0] // 2
    own_ref[...] = part[:middle]
    sib_ref[...] = part[middle:]


def down_call(hidden, w_down, piece, pieces):
    rows, units = hidden.shape
    width = w_down.shape[1] // pieces
    cols = min(1024, width)
    steps = width // cols
    out_block = pl.BlockSpec((rows // 2, cols), lambda i: (0, i))
    return pl.pallas_call(
        down_kernel,
        grid=(steps,),
        in_specs=[
            pl.BlockSpec((rows, units), lambda i: (0, 0)),
            pl.BlockSpec((units, cols), lambda i: (0, piece * steps + i)),
        ],
        out_specs=[out_block, out_block],
        out_shape=[jax.ShapeDtypeStruct((rows // 2, width), jnp.bfloat16)] * 2,
        compiler_params=pltpu.CompilerParams(
            dimension_semantics=("arbitrary",), vmem_limit_bytes=16 * MIB
        ),
        cost_estimate=pl.CostEstimate(
            flops=2 * rows * width * units,
            bytes_accessed=2 * width * units + 2 * rows * width,
            transcendentals=0,
        ),
        name="down",
    )(hidden, w_down)


def spread_kernel(a_ref, b_ref, c_ref, d_ref, table_ref, *rest):
    out_ref = rest[-1]
    total = a_ref[...].astype(jnp.float32) + b_ref[...].astype(jnp.float32)
    total += c_ref[...].astype(jnp.float32) + d_ref[...].astype(jnp.float32)
    total = total.astype(jnp.bfloat16)
    out_ref[...] = lax.dot_general(
        table_ref[...],
        jnp.concatenate([total] * PARTS, axis=0),
        (((0,), (0,)), ((), ())),
        preferred_element_type=jnp.float32,
    ).astype(jnp.bfloat16)


def spread_call(parts, table, piece, pieces, previous):
    tokens = table.shape[1]
    piece_width = parts[0].shape[1]
    cols = min(2048, piece_width)
    steps = piece_width // cols
    earlier = [] if previous is None else [previous]
    return pl.pallas_call(
        spread_kernel,
        grid=(steps,),
        in_specs=[pl.BlockSpec((CAP, cols), lambda i: (0, i))] * 4
        + [pl.BlockSpec((PARTS * CAP, tokens), lambda i: (0, 0))]
        + [pl.BlockSpec(memory_space=pl.ANY)] * len(earlier),
        out_specs=pl.BlockSpec((tokens, cols), lambda i: (0, piece * steps + i)),
        out_shape=jax.ShapeDtypeStruct((tokens, piece_width * pieces), jnp.bfloat16),
        input_output_aliases={5: 0} if earlier else {},
        compiler_params=pltpu.CompilerParams(
            dimension_semantics=("arbitrary",), vmem_limit_bytes=16 * MIB
        ),
        name="spread",
    )(*parts, table, *earlier)


def reduce_chip_rows(mine, other, half, chips, go_right, go_left):
    middle = mine.shape[1] // 2

    def block(index):
        rows = slice(index * CAP, (index + 1) * CAP)
        return mine[rows].astype(jnp.float32) + other[rows].astype(jnp.float32)

    far = block(chips - 1).astype(jnp.bfloat16)
    ahead, back = far[:, :middle], far[:, middle:]
    for distance in range(half - 1, -1, -1):
        ahead, back = lax.optimization_barrier((ahead, back))
        to_right, to_left = go_right(ahead), go_left(back)
        yield
        if distance == 0:
            break
        ahead, back = block(half - 1 + distance), block(distance)
        if distance == half - 1:
            ahead = jnp.concatenate(
                [ahead[:, :middle] + to_right.astype(jnp.float32), ahead[:, middle:]], axis=1
            )
            back = jnp.concatenate(
                [back[:, :middle], back[:, middle:] + to_left.astype(jnp.float32)], axis=1
            )
        else:
            ahead = ahead + to_right.astype(jnp.float32)
            back = back + to_left.astype(jnp.float32)
        ahead, back = ahead.astype(jnp.bfloat16), back.astype(jnp.bfloat16)
    return (mine, other, to_right, to_left)


def run_together(generators):
    results = [None] * len(generators)
    active = list(range(len(generators)))
    while active:
        for i in list(active):
            try:
                next(generators[i])
            except StopIteration as stop:
                results[i] = stop.value
                active.remove(i)
    return results


def per_device(chips, queries, keys, values, norm_gain, expert_ids, gates, w_gate, w_up, w_down):
    right, left, sibling = permutations(chips)
    half = chips // 2
    go_right = lambda x: lax.ppermute(x, "ctx", right)
    go_left = lambda x: lax.ppermute(x, "ctx", left)
    swap = lambda x: lax.ppermute(x, "ctx", sibling)

    me = lax.axis_index("ctx").astype(jnp.int32).reshape(1)
    tokens = queries.shape[0]
    hits = (expert_ids == 0).astype(jnp.float32)
    chosen = jnp.sum(hits, axis=1)
    position = jnp.arange(tokens, dtype=jnp.int32)
    before = (position[None, :] < position[:, None]).astype(jnp.float32)
    slot = jnp.sum(before * chosen[None, :], axis=1).astype(jnp.int32)
    table = jnp.logical_and(
        slot[None, :] == jnp.arange(CAP, dtype=jnp.int32)[:, None], chosen[None, :] > 0
    ).astype(jnp.float32)
    rest = jnp.sum(gates * hits, axis=1)
    weights = []
    for _ in range(PARTS):
        part = lax.reduce_precision(rest, 8, 7)
        weights.append(table * part[None, :])
        rest = rest - part
    weighted = jnp.concatenate(weights, axis=0).astype(jnp.bfloat16)
    table = table.astype(jnp.bfloat16)

    attention = Attention(me, queries, chips)
    own = stack(keys, values)
    from_left, from_right, own_sib = go_right(own), go_left(own), swap(own)
    acc, total, shift = attention.own(own, own_sib)
    state = (acc, total)
    sources = [own, own_sib]
    for step in range(1, half):
        from_left, from_right, state = lax.optimization_barrier((from_left, from_right, state))
        pieces = (from_left, swap(from_left), from_right, swap(from_right))
        sources += pieces
        if step < half - 1:
            from_left, from_right = go_right(from_left), go_left(from_right)
        else:
            far_keys, far_values = go_right(from_left[:tokens]), go_left(from_right[tokens:])
        state = attention.step(step, pieces, shift, state)
    far_keys, far_values, state = lax.optimization_barrier((far_keys, far_values, state))
    opposite = (far_keys, far_values, swap(far_keys), swap(far_values))
    sources += opposite
    result, picked = attention.last(opposite, shift, state, norm_gain[None, :], table, sources)

    picked, loads = lax.optimization_barrier((picked, [w_gate, w_up, w_down]))
    middle = picked.shape[1] // 2
    from_left, from_right, waiting = picked, picked, [picked]
    blocks_right, blocks_left, swapped = [picked], [], []
    for step in range(1, half):
        from_left, from_right = go_right(from_left), go_left(from_right)
        if step <= len(loads):
            loads[step - 1] = load(loads[step - 1])
        from_left, from_right, waiting, loads = lax.optimization_barrier(
            (from_left, from_right, waiting, loads)
        )
        blocks_right.append(from_left)
        blocks_left.append(from_right)
        swapped += [swap(x) for x in waiting]
        waiting = [from_left, from_right]
    far = [go_right(from_left[:, :middle]), go_left(from_right[:, middle:])]
    swapped += [swap(x) for x in waiting + far]
    blocks = blocks_right + blocks_left + far
    others = swapped[:1] + swapped[1:-2:2] + swapped[2:-2:2] + swapped[-2:]
    hidden = hidden_call(chips, blocks + others, *loads[:2])
    w_down = pltpu.with_memory_space_constraint(loads[2], pltpu.VMEM)

    sums = []
    for piece in range(PIECES):
        mine, theirs = down_call(hidden, w_down, piece, PIECES)
        sums.append(reduce_chip_rows(mine, swap(theirs), half, chips, go_right, go_left))
    mixed = None
    for piece, parts in enumerate(run_together(sums)):
        mixed = spread_call(parts, weighted, piece, PIECES, mixed)
    return (result, mixed)


def solution(mesh):
    placed = (
        P(("groups", "ctx"), None),
        P(("groups", "ctx"), None),
        P(("groups", "ctx"), None),
        P(),
        P(("groups", "ctx"), None),
        P(("groups", "ctx"), None),
        P(None, "ctx"),
        P(None, "ctx"),
        P("ctx", None),
    )
    return jax.shard_map(
        functools.partial(per_device, mesh.shape["ctx"] // 2),
        mesh=mesh,
        in_specs=placed,
        out_specs=(P(("groups", "ctx"), None), P(("groups", "ctx"), None)),
        check_vma=False,
    )
```

time: 174 us -> 220 us (1.26)
  Pallas kernels: 37 us -> 76.7 us
  starting transfers between devices: 52.8 us -> 88.6 us
  local copies, waits for them, and re-layouts: 18 us -> 1.21 us
  waiting for transfers between devices: 63.6 us -> 51.2 us
    ppermute x20, starting transfers between devices: 4.23 us -> 52.6 us  [per_device(): swap = lambda x: lax.ppermute(x, 'ctx', sibling)]
    pallas_call x2 -> x7, Pallas kernels: 16.3 us -> 42.7 us  [the longest x1 17 us: stack(): pl.pallas_call(stack_kernel, in_specs=[anywhere] * 2, out_specs=anywhere,...]
    ppermute x16, starting transfers between devices: 44.3 us -> 29.1 us  [per_device(): go_right = lambda x: lax.ppermute(x, 'ctx', right)]
    ppermute x16, waiting for transfers between devices: 44.4 us -> 29.3 us  [per_device(): go_right = lambda x: lax.ppermute(x, 'ctx', right)]
    unnamed x43 -> x10, local copies, waits for them, and re-layouts: 16.2 us -> 1.09 us
    pallas_call x5, Pallas kernels: 15 us -> 28.2 us  [call(): pl.pallas_call(kernel, grid_spec=pltpu.PrefetchScalarGridSpec(num_scalar_...]
    ppermute x16, waiting for transfers between devices: 16.2 us -> 19.1 us  [per_device(): go_left = lambda x: lax.ppermute(x, 'ctx', left)]
    ppermute x16, starting transfers between devices: 4.24 us -> 6.89 us  [per_device(): go_left = lambda x: lax.ppermute(x, 'ctx', left)]
  transfers between devices with their start and end apart: 52 -> 52, of which waited for: 31 -> 33; matrix products, arithmetic and copies ran while one was open for 1% -> 0% of each run, Pallas kernels for 8% -> 18%
where the time goes in v3:
time: 220 us
  starting transfers between devices  88.6 us (40%)
  Pallas kernels  76.7 us (35%)
  waiting for transfers between devices  51.2 us (23%)
    ppermute x20, starting transfers between devices, per_device(): swap = lambda x: lax.ppermute(x, 'ctx', sibling)  52.6 us
    ppermute x16, waiting for transfers between devices, per_device(): go_right = lambda x: lax.ppermute(x, 'ctx', right)  29.3 us
    ppermute x16, starting transfers between devices, per_device(): go_right = lambda x: lax.ppermute(x, 'ctx', right)  29.1 us
    pallas_call x5, Pallas kernels, call(): pl.pallas_call(kernel, grid_spec=pltpu.PrefetchScalarGridSpec(num_scalar_...  28.2 us
    ppermute x16, waiting for transfers between devices, per_device(): go_left = lambda x: lax.ppermute(x, 'ctx', left)  19.1 us
    pallas_call x1, Pallas kernels, stack(): pl.pallas_call(stack_kernel, in_specs=[anywhere] * 2, out_specs=anywhere,...  17 us
    pallas_call x3, Pallas kernels, load(): pl.pallas_call(load_kernel, in_specs=[pl.BlockSpec(memory_space=pltpu.HBM...  13.8 us
    pallas_call x1, Pallas kernels, hidden_call(): pl.pallas_call(functools.partial(hidden_kernel, chips), in_specs=[pl.Bloc...  8.94 us
  transfers between devices with their start and end apart: 52, of which 33 were waited for; matrix products, arithmetic and copies ran while one was open for 0% of the time, Pallas kernels for 18%

profile of v3, /device:TPU:0, one launch (start us, length us, event | category | flops | bytes accessed | tf_op | source)
XLA Modules:
  0.0 219.6 jit_solution(8731566047401416093)
XLA Ops:
  0.6 17.0 %stack.1.own_ref.refs_10_ = bf16[256,1024]{1,0:T(8,128)(2,1)} custom-call(bf16[128,1024]{1,0:T(8,128)(2,1)} %upper_ref.1, bf16[128,1024]{1,0:T(8,128)(2,1)} %lower_ref.1), custom_call_target="tpu_custom_call" | custom-call | tf_op jit(solution)/shard_map/stack/pallas_call | solution.py:338
  18.2 2.6 %collective-permute-start = (bf16[256,1024]{1,0:T(8,128)(2,1)}, bf16[256,1024]{1,0:T(8,128)(2,1)S(1)}, u32[]{:S(2)}, u32[]{:S(2)}) collective-permute-start(bf16[256,1024]{1,0:T(8,128)(2,1)} %stack.1.own_ref.refs_10_), channel_id=1, source_target_pairs={{0,4},{1,5},{4,8},{5,9},{8,12},{9,13},{12,14},{13,15},{14,10},{15,... | collective-permute-start | bytes 1572872 | tf_op jit(solution)/shard_map/ppermute | solution.py:546
  21.9 7.1 %attend_own.1 = (f32[8,1024,128]{2,1,0:T(8,128)S(1)}, f32[8,1024,128]{2,1,0:T(8,128)S(1)}, f32[8,1024,128]{2,1,0:T(8,128)S(1)}) custom-call(s32[1]{0:T(128)} %bitcast.me_ref, bf16[128,8192]{1,0:T(8,128)(2,1)} %refs_9_.1, bf16[256,1024]{1,0:T(8,128)(2,1)S(1)} %copy-done, bf16[256,1024]{1,0:T(8,128)(2,1)S(1)} %collective-permute-done.2.sib_ref.refs_11_), custom_call_target="tpu_custom_call" | custom-call | flops 536870912 | bytes 4194304 | tf_op jit(solution)/shard_map/attend_own/pallas_call | solution.py:252
  29.0 4.5 %collective-permute-done.refs_0_.refs_12_ = bf16[256,1024]{1,0:T(8,128)(2,1)S(1)} collective-permute-done((bf16[256,1024]{1,0:T(8,128)(2,1)}, bf16[256,1024]{1,0:T(8,128)(2,1)S(1)}, u32[]{:S(2)}, u32[]{:S(2)}) %collective-permute-start) | collective-permute-done | bytes 524320 | tf_op jit(solution)/shard_map/ppermute | solution.py:546
  37.7 4.7 %attend_step.3 = (f32[8,1024,128]{2,1,0:T(8,128)S(1)}, f32[8,1024,128]{2,1,0:T(8,128)S(1)}) custom-call(s32[1]{0:T(128)} %bitcast.me_ref, bf16[128,8192]{1,0:T(8,128)(2,1)} %refs_9_.1, bf16[256,1024]{1,0:T(8,128)(2,1)S(1)} %collective-permute-done.refs_0_.refs_12_, ...), custom_call_target="tpu_custom_call", output_to_operand_aliasing={{0}: (7, {}), {1}: (8, {})} | custom-call | flops 536870912 | bytes 4194304 | tf_op jit(solution)/shard_map/attend_step/pallas_call | solution.py:252
  42.3 7.0 %collective-permute-done.3.refs_0_.refs_16_ = bf16[256,1024]{1,0:T(8,128)(2,1)S(1)} collective-permute-done((bf16[256,1024]{1,0:T(8,128)(2,1)S(1)}, bf16[256,1024]{1,0:T(8,128)(2,1)S(1)}, u32[]{:S(2)}, u32[]{:S(2)}) %collective-permute-start.3) | collective-permute-done | bytes 524320 | tf_op jit(solution)/shard_map/ppermute | solution.py:546
  53.3 4.7 %attend_step.4 = (f32[8,1024,128]{2,1,0:T(8,128)S(1)}, f32[8,1024,128]{2,1,0:T(8,128)S(1)}) custom-call(s32[1]{0:T(128)} %bitcast.me_ref, bf16[128,8192]{1,0:T(8,128)(2,1)} %refs_9_.1, bf16[256,1024]{1,0:T(8,128)(2,1)S(1)} %collective-permute-done.3.refs_0_.refs_16_, ...), custom_call_target="tpu_custom_call", output_to_operand_aliasing={{0}: (7, {}), {1}: (8, {})} | custom-call | flops 536870912 | bytes 4194304 | tf_op jit(solution)/shard_map/attend_step/pallas_call | solution.py:252
  58.0 7.1 %collective-permute-done.7.refs_0_.refs_20_ = bf16[256,1024]{1,0:T(8,128)(2,1)S(1)} collective-permute-done((bf16[256,1024]{1,0:T(8,128)(2,1)S(1)}, bf16[256,1024]{1,0:T(8,128)(2,1)S(1)}, u32[]{:S(2)}, u32[]{:S(2)}) %collective-permute-start.7) | collective-permute-done | bytes 524320 | tf_op jit(solution)/shard_map/ppermute | solution.py:546
  69.0 4.7 %attend_step.5 = (f32[8,1024,128]{2,1,0:T(8,128)S(1)}, f32[8,1024,128]{2,1,0:T(8,128)S(1)}) custom-call(s32[1]{0:T(128)} %bitcast.me_ref, bf16[128,8192]{1,0:T(8,128)(2,1)} %refs_9_.1, bf16[256,1024]{1,0:T(8,128)(2,1)S(1)} %collective-permute-done.7.refs_0_.refs_20_, ...), custom_call_target="tpu_custom_call", output_to_operand_aliasing={{0}: (7, {}), {1}: (8, {})} | custom-call | flops 536870912 | bytes 4194304 | tf_op jit(solution)/shard_map/attend_step/pallas_call | solution.py:252
  78.4 7.1 %attend_last.1 = (bf16[128,8192]{1,0:T(8,128)(2,1)}, bf16[16,8192]{1,0:T(8,128)(2,1)S(1)}) custom-call(s32[1]{0:T(128)} %bitcast.me_ref, bf16[128,8192]{1,0:T(8,128)(2,1)} %refs_9_.1, bf16[128,1024]{1,0:T(8,128)(2,1)S(1)} %collective-permute-done.11.refs_0_.refs_24_, bf16[128,1024]{1,0:T(8,128)(2,1)S(1)} %collective-permute-done.12.refs_1_.refs_25_, ...), custom_call_target="tpu_custom_call" | custom-call | flops 536870912 | bytes 4194304 | tf_op jit(solution)/shard_map/attend_last/pallas_call | solution.py:252
  87.6 4.6 %load.3.refs_18_ = bf16[8192,768]{1,0:T(8,128)(2,1)S(1)} custom-call(bf16[8192,768]{1,0:T(8,128)(2,1)} %source_ref), custom_call_target="tpu_custom_call" | custom-call | bytes 6291456 | tf_op jit(solution)/shard_map/load/pallas_call | solution.py:355
  92.2 1.7 collective-permute-done.17.refs_1_
  93.9 2.8 %collective-permute-done.18.refs_4_ = bf16[16,8192]{1,0:T(8,128)(2,1)S(1)} collective-permute-done((bf16[16,8192]{1,0:T(8,128)(2,1)S(1)}, bf16[16,8192]{1,0:T(8,128)(2,1)S(1)}, u32[]{:S(2)}, u32[]{:S(2)}) %collective-permute-start.18) | collective-permute-done | bytes 262176 | tf_op jit(solution)/shard_map/ppermute | solution.py:547
  96.7 4.4 %collective-permute-start.19 = (bf16[16,8192]{1,0:T(8,128)(2,1)S(1)}, bf16[16,8192]{1,0:T(8,128)(2,1)S(1)}, u32[]{:S(2)}, u32[]{:S(2)}) collective-permute-start(bf16[16,8192]{1,0:T(8,128)(2,1)S(1)} %collective-permute-done.17.refs_1_), channel_id=1, source_target_pairs={{0,4},{1,5},{4,8},{5,9},{8,12},{9,13},{12,14},{13,15},{14,10},{15,... | collective-permute-start | bytes 786440 | tf_op jit(solution)/shard_map/ppermute | solution.py:546
  101.1 4.6 %load.4.refs_19_ = bf16[8192,768]{1,0:T(8,128)(2,1)S(1)} custom-call(bf16[8192,768]{1,0:T(8,128)(2,1)} %source_ref.1), custom_call_target="tpu_custom_call" | custom-call | bytes 6291456 | tf_op jit(solution)/shard_map/load/pallas_call | solution.py:355
  109.5 47.8 %collective-permute-start.25 = (bf16[16,8192]{1,0:T(8,128)(2,1)S(1)}, bf16[16,8192]{1,0:T(8,128)(2,1)S(1)}, u32[]{:S(2)}, u32[]{:S(2)}) collective-permute-start(bf16[16,8192]{1,0:T(8,128)(2,1)S(1)} %get-tuple-element.116.refs_0_), channel_id=1, source_target_pairs={{0,1},{1,0},{2,3},{3,2},{4,5},{5,4},{6,7},{7,6},{8,9},{9,8},{10,11... | collective-permute-start | bytes 786440 | tf_op jit(solution)/shard_map/ppermute | solution.py:548
  157.8 4.6 %load.5.down_ref = bf16[768,8192]{1,0:T(8,128)(2,1)S(1)} custom-call(bf16[768,8192]{1,0:T(8,128)(2,1)} %source_ref.2), custom_call_target="tpu_custom_call" | custom-call | bytes 6291456 | tf_op jit(solution)/shard_map/load/pallas_call | solution.py:355
  162.4 1.8 collective-permute-start.23
  165.2 2.8 %collective-permute-done.23.refs_7_ = bf16[16,4096]{1,0:T(8,128)(2,1)S(1)} collective-permute-done((bf16[16,4096]{1,0:T(8,128)(2,1)S(1)}, bf16[16,4096]{1,0:T(8,128)(2,1)S(1)}, u32[]{:S(2)}, u32[]{:S(2)}) %collective-permute-start.23) | collective-permute-done | bytes 131104 | tf_op jit(solution)/shard_map/ppermute | solution.py:546
  168.0 2.5 %collective-permute-done.24.refs_8_ = bf16[16,4096]{1,0:T(8,128)(2,1)S(1)} collective-permute-done((bf16[16,4096]{1,0:T(8,128)(2,1)S(1)}, bf16[16,4096]{1,0:T(8,128)(2,1)S(1)}, u32[]{:S(2)}, u32[]{:S(2)}) %collective-permute-start.24) | collective-permute-done | bytes 131104 | tf_op jit(solution)/shard_map/ppermute | solution.py:547
  172.0 8.9 %hidden.1.hidden_ref = bf16[256,768]{1,0:T(8,128)(2,1)S(1)} custom-call(bf16[16,8192]{1,0:T(8,128)(2,1)S(1)} %get-tuple-element.116.refs_0_, bf16[16,8192]{1,0:T(8,128)(2,1)S(1)} %collective-permute-done.17.refs_1_, bf16[16,8192]{1,0:T(8,128)(2,1)S(1)} %collective-permute-done.19.refs_2_, bf16[16,8192]{1,0:T(8,128)(2,1)S(1)} %collective-permute-done.21.refs_3_, ...), custom_call_target="tpu_custom_call" | custom-call | flops 6442450944 | bytes 29360128 | tf_op jit(solution)/shard_map/hidden/pallas_call | solution.py:409
  181.0 2.9 %down.2 = (bf16[128,4096]{1,0:T(8,128)(2,1)S(1)}, bf16[128,4096]{1,0:T(8,128)(2,1)S(1)}) custom-call(bf16[256,768]{1,0:T(8,128)(2,1)S(1)} %hidden.1.hidden_ref, bf16[768,8192]{1,0:T(8,128)(2,1)S(1)} %load.5.down_ref), custom_call_target="tpu_custom_call" | custom-call | flops 1610612736 | bytes 8388608 | tf_op jit(solution)/shard_map/down/pallas_call | solution.py:444
  184.3 2.9 %down.3 = (bf16[128,4096]{1,0:T(8,128)(2,1)S(1)}, bf16[128,4096]{1,0:T(8,128)(2,1)S(1)}) custom-call(bf16[256,768]{1,0:T(8,128)(2,1)S(1)} %hidden.1.hidden_ref, bf16[768,8192]{1,0:T(8,128)(2,1)S(1)} %load.5.down_ref), custom_call_target="tpu_custom_call" | custom-call | flops 1610612736 | bytes 8388608 | tf_op jit(solution)/shard_map/down/pallas_call | solution.py:444
  187.5 1.8 collective-permute-start.35
  190.0 1.8 collective-permute-start.44
  194.0 1.7 collective-permute-start.37
  197.2 1.7 collective-permute-start.46
  200.6 1.8 collective-permute-start.39
  206.5 2.0 collective-permute-start.41
  209.9 1.7 collective-permute-start.50
  212.0 2.9 %collective-permute-done.50.c_ref = bf16[16,4096]{1,0:T(8,128)(2,1)S(1)} collective-permute-done((bf16[16,4096]{1,0:T(8,128)(2,1)S(1)}, bf16[16,4096]{1,0:T(8,128)(2,1)S(1)}, u32[]{:S(2)}, u32[]{:S(2)}) %collective-permute-start.50) | collective-permute-done | bytes 131104 | tf_op jit(solution)/shard_map/ppermute | solution.py:546
  214.9 1.6 collective-permute-done.51.d_ref
  (128 shorter events, 42.7 us)
Async XLA Ops:
  18.2 15.3 %collective-permute-start = (bf16[256,1024]{1,0:T(8,128)(2,1)}, bf16[256,1024]{1,0:T(8,128)(2,1)S(1)}, u32[]{:S(2)}, u32[]{:S(2)}) collective-permute-start(bf16[256,1024]{1,0:T(8,128)(2,1)} %stack.1.own_ref.refs_10_), channel_id=1, source_target_pairs={{0,4},{1,5},{4,8},{5,9},{8,12},{9,13},{12,14},{13,15},{14,10},{15,... | collective-permute-start | bytes 1572872 | tf_op jit(solution)/shard_map/ppermute | solution.py:546
  20.8 14.2 %collective-permute-start.1 = (bf16[256,1024]{1,0:T(8,128)(2,1)}, bf16[256,1024]{1,0:T(8,128)(2,1)S(1)}, u32[]{:S(2)}, u32[]{:S(2)}) collective-permute-start(bf16[256,1024]{1,0:T(8,128)(2,1)} %stack.1.own_ref.refs_10_), channel_id=1, source_target_pairs={{4,0},{5,1},{8,4},{9,5},{12,8},{13,9},{14,12},{15,13},{10,14},{11,... | collective-permute-start | bytes 1572872 | tf_op jit(solution)/shard_map/ppermute | solution.py:547
  35.5 13.8 %collective-permute-start.3 = (bf16[256,1024]{1,0:T(8,128)(2,1)S(1)}, bf16[256,1024]{1,0:T(8,128)(2,1)S(1)}, u32[]{:S(2)}, u32[]{:S(2)}) collective-permute-start(bf16[256,1024]{1,0:T(8,128)(2,1)S(1)} %collective-permute-done.refs_0_.refs_12_), channel_id=1, source_target_pairs={{0,4},{1,5},{4,8},{5,9},{8,12},{9,13},{12,14},{13,15},{14,10},{15,... | collective-permute-start | bytes 1572872 | tf_op jit(solution)/shard_map/ppermute | solution.py:546
  37.1 13.6 %collective-permute-start.4 = (bf16[256,1024]{1,0:T(8,128)(2,1)S(1)}, bf16[256,1024]{1,0:T(8,128)(2,1)S(1)}, u32[]{:S(2)}, u32[]{:S(2)}) collective-permute-start(bf16[256,1024]{1,0:T(8,128)(2,1)S(1)} %collective-permute-done.1.refs_2_.refs_14_), channel_id=1, source_target_pairs={{4,0},{5,1},{8,4},{9,5},{12,8},{13,9},{14,12},{15,13},{10,14},{11,... | collective-permute-start | bytes 1572872 | tf_op jit(solution)/shard_map/ppermute | solution.py:547
  51.2 13.9 %collective-permute-start.7 = (bf16[256,1024]{1,0:T(8,128)(2,1)S(1)}, bf16[256,1024]{1,0:T(8,128)(2,1)S(1)}, u32[]{:S(2)}, u32[]{:S(2)}) collective-permute-start(bf16[256,1024]{1,0:T(8,128)(2,1)S(1)} %collective-permute-done.3.refs_0_.refs_16_), channel_id=1, source_target_pairs={{0,4},{1,5},{4,8},{5,9},{8,12},{9,13},{12,14},{13,15},{14,10},{15,... | collective-permute-start | bytes 1572872 | tf_op jit(solution)/shard_map/ppermute | solution.py:546
  52.7 13.6 %collective-permute-start.8 = (bf16[256,1024]{1,0:T(8,128)(2,1)S(1)}, bf16[256,1024]{1,0:T(8,128)(2,1)S(1)}, u32[]{:S(2)}, u32[]{:S(2)}) collective-permute-start(bf16[256,1024]{1,0:T(8,128)(2,1)S(1)} %collective-permute-done.4.refs_2_.refs_18_), channel_id=1, source_target_pairs={{4,0},{5,1},{8,4},{9,5},{12,8},{13,9},{14,12},{15,13},{10,14},{11,... | collective-permute-start | bytes 1572872 | tf_op jit(solution)/shard_map/ppermute | solution.py:547
  66.9 8.3 %collective-permute-start.11 = (bf16[128,1024]{1,0:T(8,128)(2,1)S(1)}, bf16[128,1024]{1,0:T(8,128)(2,1)S(1)}, u32[]{:S(2)}, u32[]{:S(2)}) collective-permute-start(bf16[128,1024]{1,0:T(8,128)(2,1)S(1)} %slice.136), channel_id=1, source_target_pairs={{0,4},{1,5},{4,8},{5,9},{8,12},{9,13},{12,14},{13,15},{14,10},{15,... | collective-permute-start | bytes 786440 | tf_op jit(solution)/shard_map/ppermute | solution.py:546
  68.5 7.9 %collective-permute-start.12 = (bf16[128,1024]{1,0:T(8,128)(2,1)S(1)}, bf16[128,1024]{1,0:T(8,128)(2,1)S(1)}, u32[]{:S(2)}, u32[]{:S(2)}) collective-permute-start(bf16[128,1024]{1,0:T(8,128)(2,1)S(1)} %slice.137), channel_id=1, source_target_pairs={{4,0},{5,1},{8,4},{9,5},{12,8},{13,9},{14,12},{15,13},{10,14},{11,... | collective-permute-start | bytes 786440 | tf_op jit(solution)/shard_map/ppermute | solution.py:547
  85.5 8.4 %collective-permute-start.17 = (bf16[16,8192]{1,0:T(8,128)(2,1)S(1)}, bf16[16,8192]{1,0:T(8,128)(2,1)S(1)}, u32[]{:S(2)}, u32[]{:S(2)}) collective-permute-start(bf16[16,8192]{1,0:T(8,128)(2,1)S(1)} %get-tuple-element.116.refs_0_), channel_id=1, source_target_pairs={{0,4},{1,5},{4,8},{5,9},{8,12},{9,13},{12,14},{13,15},{14,10},{15,... | collective-permute-start | bytes 786440 | tf_op jit(solution)/shard_map/ppermute | solution.py:546
  86.0 10.7 %collective-permute-start.18 = (bf16[16,8192]{1,0:T(8,128)(2,1)S(1)}, bf16[16,8192]{1,0:T(8,128)(2,1)S(1)}, u32[]{:S(2)}, u32[]{:S(2)}) collective-permute-start(bf16[16,8192]{1,0:T(8,128)(2,1)S(1)} %get-tuple-element.116.refs_0_), channel_id=1, source_target_pairs={{4,0},{5,1},{8,4},{9,5},{12,8},{13,9},{14,12},{15,13},{10,14},{11,... | collective-permute-start | bytes 786440 | tf_op jit(solution)/shard_map/ppermute | solution.py:547
  96.7 9.4 %collective-permute-start.19 = (bf16[16,8192]{1,0:T(8,128)(2,1)S(1)}, bf16[16,8192]{1,0:T(8,128)(2,1)S(1)}, u32[]{:S(2)}, u32[]{:S(2)}) collective-permute-start(bf16[16,8192]{1,0:T(8,128)(2,1)S(1)} %collective-permute-done.17.refs_1_), channel_id=1, source_target_pairs={{0,4},{1,5},{4,8},{5,9},{8,12},{9,13},{12,14},{13,15},{14,10},{15,... | collective-permute-start | bytes 786440 | tf_op jit(solution)/shard_map/ppermute | solution.py:546
  101.1 6.4 %collective-permute-start.20 = (bf16[16,8192]{1,0:T(8,128)(2,1)S(1)}, bf16[16,8192]{1,0:T(8,128)(2,1)S(1)}, u32[]{:S(2)}, u32[]{:S(2)}) collective-permute-start(bf16[16,8192]{1,0:T(8,128)(2,1)S(1)} %collective-permute-done.18.refs_4_), channel_id=1, source_target_pairs={{4,0},{5,1},{8,4},{9,5},{12,8},{13,9},{14,12},{15,13},{10,14},{11,... | collective-permute-start | bytes 786440 | tf_op jit(solution)/shard_map/ppermute | solution.py:547
  107.5 54.9 %collective-permute-start.21 = (bf16[16,8192]{1,0:T(8,128)(2,1)S(1)}, bf16[16,8192]{1,0:T(8,128)(2,1)S(1)}, u32[]{:S(2)}, u32[]{:S(2)}) collective-permute-start(bf16[16,8192]{1,0:T(8,128)(2,1)S(1)} %collective-permute-done.19.refs_2_), channel_id=1, source_target_pairs={{0,4},{1,5},{4,8},{5,9},{8,12},{9,13},{12,14},{13,15},{14,10},{15,... | collective-permute-start | bytes 786440 | tf_op jit(solution)/shard_map/ppermute | solution.py:546
  108.6 53.8 %collective-permute-start.22 = (bf16[16,8192]{1,0:T(8,128)(2,1)S(1)}, bf16[16,8192]{1,0:T(8,128)(2,1)S(1)}, u32[]{:S(2)}, u32[]{:S(2)}) collective-permute-start(bf16[16,8192]{1,0:T(8,128)(2,1)S(1)} %collective-permute-done.20.refs_5_), channel_id=1, source_target_pairs={{4,0},{5,1},{8,4},{9,5},{12,8},{13,9},{14,12},{15,13},{10,14},{11,... | collective-permute-start | bytes 786440 | tf_op jit(solution)/shard_map/ppermute | solution.py:547
  109.5 54.7 %collective-permute-start.25 = (bf16[16,8192]{1,0:T(8,128)(2,1)S(1)}, bf16[16,8192]{1,0:T(8,128)(2,1)S(1)}, u32[]{:S(2)}, u32[]{:S(2)}) collective-permute-start(bf16[16,8192]{1,0:T(8,128)(2,1)S(1)} %get-tuple-element.116.refs_0_), channel_id=1, source_target_pairs={{0,1},{1,0},{2,3},{3,2},{4,5},{5,4},{6,7},{7,6},{8,9},{9,8},{10,11... | collective-permute-start | bytes 786440 | tf_op jit(solution)/shard_map/ppermute | solution.py:548
  157.3 7.5 %collective-permute-start.26 = (bf16[16,8192]{1,0:T(8,128)(2,1)S(1)}, bf16[16,8192]{1,0:T(8,128)(2,1)S(1)}, u32[]{:S(2)}, u32[]{:S(2)}) collective-permute-start(bf16[16,8192]{1,0:T(8,128)(2,1)S(1)} %collective-permute-done.17.refs_1_), channel_id=1, source_target_pairs={{0,1},{1,0},{2,3},{3,2},{4,5},{5,4},{6,7},{7,6},{8,9},{9,8},{10,11... | collective-permute-start | bytes 786440 | tf_op jit(solution)/shard_map/ppermute | solution.py:548
  157.3 7.8 %collective-permute-start.29 = (bf16[16,8192]{1,0:T(8,128)(2,1)S(1)}, bf16[16,8192]{1,0:T(8,128)(2,1)S(1)}, u32[]{:S(2)}, u32[]{:S(2)}) collective-permute-start(bf16[16,8192]{1,0:T(8,128)(2,1)S(1)} %collective-permute-done.18.refs_4_), channel_id=1, source_target_pairs={{0,1},{1,0},{2,3},{3,2},{4,5},{5,4},{6,7},{7,6},{8,9},{9,8},{10,11... | collective-permute-start | bytes 786440 | tf_op jit(solution)/shard_map/ppermute | solution.py:548
  164.2 6.3 %collective-permute-start.27 = (bf16[16,8192]{1,0:T(8,128)(2,1)S(1)}, bf16[16,8192]{1,0:T(8,128)(2,1)S(1)}, u32[]{:S(2)}, u32[]{:S(2)}) collective-permute-start(bf16[16,8192]{1,0:T(8,128)(2,1)S(1)} %collective-permute-done.19.refs_2_), channel_id=1, source_target_pairs={{0,1},{1,0},{2,3},{3,2},{4,5},{5,4},{6,7},{7,6},{8,9},{9,8},{10,11... | collective-permute-start | bytes 786440 | tf_op jit(solution)/shard_map/ppermute | solution.py:548
  164.3 6.8 %collective-permute-start.28 = (bf16[16,8192]{1,0:T(8,128)(2,1)S(1)}, bf16[16,8192]{1,0:T(8,128)(2,1)S(1)}, u32[]{:S(2)}, u32[]{:S(2)}) collective-permute-start(bf16[16,8192]{1,0:T(8,128)(2,1)S(1)} %collective-permute-done.21.refs_3_), channel_id=1, source_target_pairs={{0,1},{1,0},{2,3},{3,2},{4,5},{5,4},{6,7},{7,6},{8,9},{9,8},{10,11... | collective-permute-start | bytes 786440 | tf_op jit(solution)/shard_map/ppermute | solution.py:548
  164.8 5.7 %collective-permute-start.24 = (bf16[16,4096]{1,0:T(8,128)(2,1)S(1)}, bf16[16,4096]{1,0:T(8,128)(2,1)S(1)}, u32[]{:S(2)}, u32[]{:S(2)}) collective-permute-start(bf16[16,4096]{1,0:T(8,128)(2,1)S(1)} %slice.139), channel_id=1, source_target_pairs={{4,0},{5,1},{8,4},{9,5},{12,8},{13,9},{14,12},{15,13},{10,14},{11,... | collective-permute-start | bytes 393224 | tf_op jit(solution)/shard_map/ppermute | solution.py:547
  165.1 5.9 %collective-permute-start.30 = (bf16[16,8192]{1,0:T(8,128)(2,1)S(1)}, bf16[16,8192]{1,0:T(8,128)(2,1)S(1)}, u32[]{:S(2)}, u32[]{:S(2)}) collective-permute-start(bf16[16,8192]{1,0:T(8,128)(2,1)S(1)} %collective-permute-done.20.refs_5_), channel_id=1, source_target_pairs={{0,1},{1,0},{2,3},{3,2},{4,5},{5,4},{6,7},{7,6},{8,9},{9,8},{10,11... | collective-permute-start | bytes 786440 | tf_op jit(solution)/shard_map/ppermute | solution.py:548
  190.0 5.7 %collective-permute-start.44 = (bf16[16,2048]{1,0:T(8,128)(2,1)S(1)}, bf16[16,2048]{1,0:T(8,128)(2,1)S(1)}, u32[]{:S(2)}, u32[]{:S(2)}) collective-permute-start(bf16[16,2048]{1,0:T(8,128)(2,1)S(1)} %get-tuple-element.136), channel_id=1, source_target_pairs={{0,4},{1,5},{4,8},{5,9},{8,12},{9,13},{12,14},{13,15},{14,10},{15,... | collective-permute-start | bytes 196616 | tf_op jit(solution)/shard_map/ppermute | solution.py:546
  193.6 6.2 %collective-permute-start.38 = (bf16[16,4096]{1,0:T(8,128)(2,1)S(1)}, bf16[16,4096]{1,0:T(8,128)(2,1)S(1)}, u32[]{:S(2)}, u32[]{:S(2)}) collective-permute-start(bf16[16,4096]{1,0:T(8,128)(2,1)S(1)} %pad_maximum_fusion.1), channel_id=1, source_target_pairs={{4,0},{5,1},{8,4},{9,5},{12,8},{13,9},{14,12},{15,13},{10,14},{11,... | collective-permute-start | bytes 393224 | tf_op jit(solution)/shard_map/ppermute | solution.py:547
  194.0 6.3 %collective-permute-start.37 = (bf16[16,4096]{1,0:T(8,128)(2,1)S(1)}, bf16[16,4096]{1,0:T(8,128)(2,1)S(1)}, u32[]{:S(2)}, u32[]{:S(2)}) collective-permute-start(bf16[16,4096]{1,0:T(8,128)(2,1)S(1)} %pad_maximum_fusion), channel_id=1, source_target_pairs={{0,4},{1,5},{4,8},{5,9},{8,12},{9,13},{12,14},{13,15},{14,10},{15,... | collective-permute-start | bytes 393224 | tf_op jit(solution)/shard_map/ppermute | solution.py:546
  196.8 6.0 %collective-permute-start.47 = (bf16[16,4096]{1,0:T(8,128)(2,1)S(1)}, bf16[16,4096]{1,0:T(8,128)(2,1)S(1)}, u32[]{:S(2)}, u32[]{:S(2)}) collective-permute-start(bf16[16,4096]{1,0:T(8,128)(2,1)S(1)} %pad_maximum_fusion.3), channel_id=1, source_target_pairs={{4,0},{5,1},{8,4},{9,5},{12,8},{13,9},{14,12},{15,13},{10,14},{11,... | collective-permute-start | bytes 393224 | tf_op jit(solution)/shard_map/ppermute | solution.py:547
  197.2 6.0 %collective-permute-start.46 = (bf16[16,4096]{1,0:T(8,128)(2,1)S(1)}, bf16[16,4096]{1,0:T(8,128)(2,1)S(1)}, u32[]{:S(2)}, u32[]{:S(2)}) collective-permute-start(bf16[16,4096]{1,0:T(8,128)(2,1)S(1)} %pad_maximum_fusion.2), channel_id=1, source_target_pairs={{0,4},{1,5},{4,8},{5,9},{8,12},{9,13},{12,14},{13,15},{14,10},{15,... | collective-permute-start | bytes 393224 | tf_op jit(solution)/shard_map/ppermute | solution.py:546
  200.3 5.7 %collective-permute-start.40 = (bf16[16,4096]{1,0:T(8,128)(2,1)S(1)}, bf16[16,4096]{1,0:T(8,128)(2,1)S(1)}, u32[]{:S(2)}, u32[]{:S(2)}) collective-permute-start(bf16[16,4096]{1,0:T(8,128)(2,1)S(1)} %get-tuple-element.131), channel_id=1, source_target_pairs={{4,0},{5,1},{8,4},{9,5},{12,8},{13,9},{14,12},{15,13},{10,14},{11,... | collective-permute-start | bytes 393224 | tf_op jit(solution)/shard_map/ppermute | solution.py:547
  200.6 5.8 %collective-permute-start.39 = (bf16[16,4096]{1,0:T(8,128)(2,1)S(1)}, bf16[16,4096]{1,0:T(8,128)(2,1)S(1)}, u32[]{:S(2)}, u32[]{:S(2)}) collective-permute-start(bf16[16,4096]{1,0:T(8,128)(2,1)S(1)} %get-tuple-element.130), channel_id=1, source_target_pairs={{0,4},{1,5},{4,8},{5,9},{8,12},{9,13},{12,14},{13,15},{14,10},{15,... | collective-permute-start | bytes 393224 | tf_op jit(solution)/shard_map/ppermute | solution.py:546
  203.2 6.3 %collective-permute-start.49 = (bf16[16,4096]{1,0:T(8,128)(2,1)S(1)}, bf16[16,4096]{1,0:T(8,128)(2,1)S(1)}, u32[]{:S(2)}, u32[]{:S(2)}) collective-permute-start(bf16[16,4096]{1,0:T(8,128)(2,1)S(1)} %get-tuple-element.141), channel_id=1, source_target_pairs={{4,0},{5,1},{8,4},{9,5},{12,8},{13,9},{14,12},{15,13},{10,14},{11,... | collective-permute-start | bytes 393224 | tf_op jit(solution)/shard_map/ppermute | solution.py:547
  204.0 5.8 %collective-permute-start.48 = (bf16[16,4096]{1,0:T(8,128)(2,1)S(1)}, bf16[16,4096]{1,0:T(8,128)(2,1)S(1)}, u32[]{:S(2)}, u32[]{:S(2)}) collective-permute-start(bf16[16,4096]{1,0:T(8,128)(2,1)S(1)} %get-tuple-element.140), channel_id=1, source_target_pairs={{0,4},{1,5},{4,8},{5,9},{8,12},{9,13},{12,14},{13,15},{14,10},{15,... | collective-permute-start | bytes 393224 | tf_op jit(solution)/shard_map/ppermute | solution.py:546
  206.5 11.6 %collective-permute-start.41 = (bf16[16,4096]{1,0:T(8,128)(2,1)S(1)}, bf16[16,4096]{1,0:T(8,128)(2,1)S(1)}, u32[]{:S(2)}, u32[]{:S(2)}) collective-permute-start(bf16[16,4096]{1,0:T(8,128)(2,1)S(1)} %get-tuple-element.132), channel_id=1, source_target_pairs={{0,4},{1,5},{4,8},{5,9},{8,12},{9,13},{12,14},{13,15},{14,10},{15,... | collective-permute-start | bytes 393224 | tf_op jit(solution)/shard_map/ppermute | solution.py:546
  208.5 9.6 %collective-permute-start.42 = (bf16[16,4096]{1,0:T(8,128)(2,1)S(1)}, bf16[16,4096]{1,0:T(8,128)(2,1)S(1)}, u32[]{:S(2)}, u32[]{:S(2)}) collective-permute-start(bf16[16,4096]{1,0:T(8,128)(2,1)S(1)} %get-tuple-element.133), channel_id=1, source_target_pairs={{4,0},{5,1},{8,4},{9,5},{12,8},{13,9},{14,12},{15,13},{10,14},{11,... | collective-permute-start | bytes 393224 | tf_op jit(solution)/shard_map/ppermute | solution.py:547
  (25 other events, 116.1 us)

commit v4 on v3

--- a/solution.py
+++ b/solution.py
@@ -50,9 +50,9 @@
     return jnp.where(source < chips // 2, 2 * source, 2 * (chips - 1 - source) + 1)
 
 
-def head_rows(q_ref, first):
+def head_rows(queries, first):
     return jnp.concatenate(
-        [q_ref[:, h * DH : (h + 1) * DH] for h in range(first, first + STACK)], axis=0
+        [queries[:, h * DH : (h + 1) * DH] for h in range(first, first + STACK)], axis=0
     )
 
 
@@ -74,10 +74,10 @@
     return jnp.broadcast_to(jnp.max(scores, axis=1, keepdims=True), (scores.shape[0], DH))
 
 
-def chip_block(own_ref, sib_ref):
-    tokens = own_ref.shape[0] // 2
-    keys = jnp.concatenate([own_ref[:tokens], sib_ref[:tokens]], axis=0)
-    values = jnp.concatenate([own_ref[tokens:], sib_ref[tokens:]], axis=0)
+def chip_block(own, sib):
+    tokens = own.shape[0] // 2
+    keys = jnp.concatenate([own[:tokens], sib[:tokens]], axis=0)
+    values = jnp.concatenate([own[tokens:], sib[tokens:]], axis=0)
     return keys, with_ones(values)
 
 
@@ -89,47 +89,65 @@
     return column <= jnp.where(column < tokens, token, limit - 1)
 
 
+def head_group(q_ref, group):
+    return q_ref[:, pl.ds(pl.multiple_of(group * WIDE, WIDE), WIDE)]
+
+
+def for_groups(body):
+    def step(group, carry):
+        body(group, pl.ds(pl.multiple_of(group * DH, DH), DH))
+        return carry
+
+    lax.fori_loop(0, HK, step, 0)
+
+
 def own_kernel(me_ref, q_ref, own_ref, sib_ref, acc_ref, total_ref, shift_ref):
     tokens = q_ref.shape[0]
-    keys, values = chip_block(own_ref, sib_ref)
     allowed = allowed_own(me_ref[0], tokens)
+
+    def one_group(group, columns):
+        keys, values = chip_block(own_ref[:, columns], sib_ref[:, columns])
+        queries = head_group(q_ref, group)
+        for first in range(0, GROUP, STACK):
+            rows = slice(first * tokens, (first + STACK) * tokens)
+            scores = jnp.where(allowed, scores_of(head_rows(queries, first), keys), MASKED)
+            shift = row_top(scores)
+            weights = weights_of(scores, shift).astype(jnp.bfloat16)
+            update = jnp.dot(weights, values, preferred_element_type=jnp.float32)
+            acc_ref[group, rows, :] = update[:, :DH]
+            total_ref[group, rows, :] = update[:, DH:]
+            shift_ref[group, rows, :] = shift
+
+    for_groups(one_group)
+
+
+def fold_chip(queries, keys, values, group, shift_ref, acc_ref, total_ref):
+    tokens = queries.shape[0]
     for first in range(0, GROUP, STACK):
         rows = slice(first * tokens, (first + STACK) * tokens)
-        scores = jnp.where(allowed, scores_of(head_rows(q_ref, first), keys), MASKED)
-        shift = row_top(scores)
-        weights = weights_of(scores, shift).astype(jnp.bfloat16)
+        scores = scores_of(head_rows(queries, first), keys)
+        weights = weights_of(scores, shift_ref[group, rows, :]).astype(jnp.bfloat16)
         update = jnp.dot(weights, values, preferred_element_type=jnp.float32)
-        acc_ref[0, rows, :] = update[:, :DH]
-        total_ref[0, rows, :] = update[:, DH:]
-        shift_ref[0, rows, :] = shift
-
-
-def fold_chip(q_ref, keys, values, shift_ref, acc_ref, total_ref):
-    tokens = q_ref.shape[0]
-    for first in range(0, GROUP, STACK):
-        rows = slice(first * tokens, (first + STACK) * tokens)
-        scores = scores_of(head_rows(q_ref, first), keys)
-        weights = weights_of(scores, shift_ref[0, rows, :]).astype(jnp.bfloat16)
-        update = jnp.dot(weights, values, preferred_element_type=jnp.float32)
-        acc_ref[0, rows, :] += update[:, :DH]
-        total_ref[0, rows, :] += update[:, DH:]
+        acc_ref[group, rows, :] += update[:, :DH]
+        total_ref[group, rows, :] += update[:, DH:]
 
 
 def step_kernel(chips, step, me_ref, q_ref, *refs):
-    pieces, shift_ref, state_in, state = refs[:4], refs[4], refs[5:7], refs[7:9]
+    pieces, shift_ref, state = refs[:4], refs[4], refs[7:9]
     me = me_ref[0]
-    for source, target in zip(state_in, state):
-        target[...] = source[...]
     for place, own_ref, sib_ref in ((step, *pieces[:2]), (-step, *pieces[2:])):
 
         @pl.when(chip_at(me, place, chips) < me // 2)
         def _():
-            keys, values = chip_block(own_ref, sib_ref)
-            fold_chip(q_ref, keys, values, shift_ref, *state)
-
-
-def running_attention(chips, me, sources, queries, out_ref, scratch, sem):
-    q_ref, keys_ref, values_ref, acc_ref, total_ref, top_ref = scratch
+            def one_group(group, columns):
+                keys, values = chip_block(own_ref[:, columns], sib_ref[:, columns])
+                fold_chip(head_group(q_ref, group), keys, values, group, shift_ref, *state)
+
+            for_groups(one_group)
+
+
+def running_attention(chips, me, sources, q_ref, out_ref, scratch, sem):
+    keys_ref, values_ref, acc_ref, total_ref, top_ref = scratch
     tokens = q_ref.shape[0]
     half = chips // 2
     places = [0] + [p for step in range(1, half) for p in (step, -step)] + [half]
@@ -141,8 +159,7 @@
 
     def one_head(head, carry):
         columns = pl.ds(pl.multiple_of(head * DH, DH), DH)
-        wide = pl.ds(pl.multiple_of(head * WIDE, WIDE), WIDE)
-        fetch(queries.at[:, wide], q_ref)
+        queries = head_group(q_ref, head)
         for i, place in enumerate(places):
             if place != half:
                 for core in range(2):
@@ -171,7 +188,7 @@
                 keys, values = keys_ref[i], with_ones(values_ref[i])
                 for first in range(0, GROUP, STACK):
                     rows = slice(first * tokens, (first + STACK) * tokens)
-                    scores = jnp.where(allowed, scores_of(head_rows(q_ref, first), keys), MASKED)
+                    scores = jnp.where(allowed, scores_of(head_rows(queries, first), keys), MASKED)
                     old = top_ref[rows, :]
                     top = jnp.maximum(old, row_top(scores))
                     factor = jnp.exp2(old - top)
@@ -191,7 +208,9 @@
 
 
 def write_heads(out_ref, head, acc, total, tokens):
-    result = (acc / total).astype(jnp.bfloat16)
+    inverse = pl.reciprocal(total, approx=True)
+    inverse = inverse * (2.0 - total * inverse)
+    result = (acc * inverse).astype(jnp.bfloat16)
     columns = pl.ds(pl.multiple_of(head * WIDE, WIDE), WIDE)
     out_ref[:, columns] = jnp.concatenate(
         [result[h * tokens : (h + 1) * tokens] for h in range(GROUP)], axis=1
@@ -199,92 +218,75 @@
 
 
 def last_kernel(chips, me_ref, q_ref, *refs):
-    (key, value, sib_key, sib_value, shift_ref), state_in = refs[:5], refs[5:7]
-    gain_ref, table_ref, queries, sources = refs[7], refs[8], refs[9], refs[10 : 12 + 2 * chips]
-    out_ref, picked_ref, acc_ref, total_ref, worst_ref, sem = refs[12 + 2 * chips : 18 + 2 * chips]
-    scratch = refs[18 + 2 * chips :]
+    key, value, sib_key, sib_value, shift_ref = refs[:5]
+    gain_ref, table_ref, sources = refs[7], refs[8], refs[9 : 11 + 2 * chips]
+    out_ref, picked_ref, *state = refs[11 + 2 * chips : 15 + 2 * chips]
+    worst_ref, sem, *scratch = refs[15 + 2 * chips :]
     tokens = q_ref.shape[0]
-    head = pl.program_id(0)
     me = me_ref[0]
-    acc_ref[...] = state_in[0][...]
-    total_ref[...] = state_in[1][...]
 
     @pl.when(chip_at(me, chips // 2, chips) < me // 2)
     def _():
-        keys = jnp.concatenate([key[...], sib_key[...]], axis=0)
-        values = with_ones(jnp.concatenate([value[...], sib_value[...]], axis=0))
-        fold_chip(q_ref, keys, values, shift_ref, acc_ref, total_ref)
-
-    write_heads(out_ref, head, acc_ref[0], total_ref[0], tokens)
-
-    @pl.when(head == 0)
+        def one_group(group, columns):
+            keys = jnp.concatenate([key[:, columns], sib_key[:, columns]], axis=0)
+            values = jnp.concatenate([value[:, columns], sib_value[:, columns]], axis=0)
+            queries = head_group(q_ref, group)
+            fold_chip(queries, keys, with_ones(values), group, shift_ref, *state)
+
+        for_groups(one_group)
+
+    worst_ref[...] = jnp.zeros_like(worst_ref)
+
+    def finish(group, columns):
+        total = state[1][group]
+        write_heads(out_ref, group, state[0][group], total, tokens)
+        worst_ref[...] = jnp.maximum(worst_ref[...], total)
+
+    for_groups(finish)
+    fits = jnp.max(worst_ref[...]) <= SUM_LIMIT
+
+    @pl.when(jnp.logical_not(fits))
     def _():
-        worst_ref[...] = jnp.zeros_like(worst_ref)
-
-    worst_ref[...] = jnp.maximum(worst_ref[...], total_ref[0])
-
-    @pl.when(head == HK - 1)
-    def _():
-        fits = jnp.max(worst_ref[...]) <= SUM_LIMIT
-
-        @pl.when(jnp.logical_not(fits))
-        def _():
-            running_attention(chips, me, sources, queries, out_ref, scratch, sem)
-
-        width = out_ref.shape[1]
-        picked = jnp.dot(table_ref[...], out_ref[...], preferred_element_type=jnp.float32)
-        mean = jnp.sum(picked * picked, axis=1, keepdims=True) / width
-        picked_ref[...] = (picked * lax.rsqrt(mean + 1e-05) * gain_ref[...]).astype(jnp.bfloat16)
+        running_attention(chips, me, sources, q_ref, out_ref, scratch, sem)
+
+    width = out_ref.shape[1]
+    picked = jnp.dot(table_ref[...], out_ref[...], preferred_element_type=jnp.float32)
+    mean = jnp.sum(picked * picked, axis=1, keepdims=True) / width
+    picked_ref[...] = (picked * lax.rsqrt(mean + 1e-05) * gain_ref[...]).astype(jnp.bfloat16)
 
 
 class Attention:
     def __init__(self, me, queries, chips):
-        self.me, self.queries, self.chips = me, in_hbm(queries), chips
+        self.me, self.queries, self.chips = me, queries, chips
         tokens = queries.shape[0]
-        self.head_block = pl.BlockSpec((tokens, WIDE), lambda g, me: (0, g))
-        self.pair_block = pl.BlockSpec((2 * tokens, DH), lambda g, me: (0, g))
-        self.kv_block = pl.BlockSpec((tokens, DH), lambda g, me: (0, g))
-        self.state_block = pl.BlockSpec((1, GROUP * tokens, DH), lambda g, me: (g, 0, 0))
-        self.state_shape = jax.ShapeDtypeStruct((HK, GROUP * tokens, DH), jnp.float32)
-
-    def call(self, kernel, name, in_specs, out_specs, out_shape, args, scratch=(), aliases=None):
+        self.state_shape = pltpu.VMEM((HK, GROUP * tokens, DH), jnp.float32)
+
+    def call(self, kernel, name, out_shape, args, others=(), scratch=(), aliases=None):
         tokens, width = self.queries.shape
+        vmem = pl.BlockSpec(memory_space=pltpu.VMEM)
         return pl.pallas_call(
             kernel,
-            grid_spec=pltpu.PrefetchScalarGridSpec(
-                num_scalar_prefetch=1,
-                grid=(HK,),
-                in_specs=[self.head_block] + in_specs,
-                out_specs=out_specs,
-                scratch_shapes=scratch,
-            ),
+            in_specs=[pl.BlockSpec(memory_space=pltpu.SMEM)]
+            + [vmem] * (1 + len(args))
+            + [pl.BlockSpec(memory_space=pl.ANY)] * len(others),
+            out_specs=[vmem] * len(out_shape),
             out_shape=out_shape,
+            scratch_shapes=scratch,
             input_output_aliases=aliases or {},
-            compiler_params=pltpu.CompilerParams(
-                dimension_semantics=("arbitrary",), vmem_limit_bytes=16 * MIB
-            ),
+            compiler_params=pltpu.CompilerParams(vmem_limit_bytes=16 * MIB),
             cost_estimate=pl.CostEstimate(
                 flops=4 * tokens * width * tokens, bytes_accessed=4 * MIB, transcendentals=0
             ),
             name=name,
-        )(self.me, self.queries, *args)
+        )(self.me, self.queries, *args, *others)
 
     def own(self, own, sib):
-        return self.call(
-            own_kernel,
-            "attend_own",
-            [self.pair_block] * 2,
-            [self.state_block] * 3,
-            [self.state_shape] * 3,
-            (own, sib),
-        )
+        return self.call(own_kernel, "attend_own", [self.state_shape] * 3, (own, sib))
 
     def step(self, step, pieces, shift, state):
         return self.call(
             functools.partial(step_kernel, self.chips, step),
             "attend_step",
-            [self.pair_block] * 4 + [self.state_block] * 3,
-            [self.state_block] * 2,
             [self.state_shape] * 2,
             (*pieces, shift, *state),
             aliases={7: 0, 8: 1},
@@ -292,57 +294,27 @@
 
     def last(self, pieces, shift, state, gain, table, sources):
         tokens, width = self.queries.shape
-        whole = lambda shape: pl.BlockSpec(shape, lambda g, me: (0, 0))
-        anywhere = pl.BlockSpec(memory_space=pl.ANY)
         rows = GROUP * tokens
         return self.call(
             functools.partial(last_kernel, self.chips),
             "attend_last",
-            [self.kv_block] * 4
-            + [self.state_block] * 3
-            + [whole((1, width)), whole((CAP, tokens))]
-            + [anywhere] * (1 + len(sources)),
-            [whole((tokens, width)), whole((CAP, width))],
             [
-                jax.ShapeDtypeStruct((tokens, width), jnp.bfloat16),
-                jax.ShapeDtypeStruct((CAP, width), jnp.bfloat16),
+                pltpu.VMEM((tokens, width), jnp.bfloat16),
+                pltpu.VMEM((CAP, width), jnp.bfloat16),
+                self.state_shape,
+                self.state_shape,
             ],
-            (*pieces, shift, *state, gain, table, self.queries, *sources),
+            (*pieces, shift, *state, gain, table),
+            sources,
             [
-                pltpu.VMEM((1, rows, DH), jnp.float32),
-                pltpu.VMEM((1, rows, DH), jnp.float32),
                 pltpu.VMEM((rows, DH), jnp.float32),
                 pltpu.SemaphoreType.DMA,
-                pltpu.VMEM((tokens, WIDE), jnp.bfloat16),
                 pltpu.VMEM((self.chips, 2 * tokens, DH), jnp.bfloat16),
                 pltpu.VMEM((self.chips, 2 * tokens, DH), jnp.bfloat16),
             ]
             + [pltpu.VMEM((rows, DH), jnp.float32)] * 3,
-        )
-
-
-def stack_kernel(upper_ref, lower_ref, out_ref, sems):
-    rows = upper_ref.shape[0]
-    copies = [
-        pltpu.make_async_copy(ref, out_ref.at[pl.ds(i * rows, rows)], sems.at[i])
-        for i, ref in enumerate((upper_ref, lower_ref))
-    ]
-    for copy in copies:
-        copy.start()
-    for copy in copies:
-        copy.wait()
-
-
-def stack(upper, lower):
-    anywhere = pl.BlockSpec(memory_space=pl.ANY)
-    return pl.pallas_call(
-        stack_kernel,
-        in_specs=[anywhere] * 2,
-        out_specs=anywhere,
-        out_shape=jax.ShapeDtypeStruct((2 * upper.shape[0], upper.shape[1]), upper.dtype),
-        scratch_shapes=[pltpu.SemaphoreType.DMA((2,))],
-        name="stack",
-    )(in_hbm(upper), in_hbm(lower))
+            aliases={7: 2, 8: 3},
+        )[:2]
 
 
 def load_kernel(source_ref, target_ref, sem):
@@ -366,38 +338,29 @@
 
 def hidden_kernel(chips, *refs):
     blocks, (gate_ref, up_ref, out_ref) = refs[: 2 * chips + 2], refs[2 * chips + 2 : 2 * chips + 5]
-    rows_ref, gate_sum, up_sum, sems = refs[2 * chips + 5 :]
-    width = rows_ref.shape[1]
+    gate_sum, up_sum = refs[2 * chips + 5 :]
+    width = gate_ref.shape[0]
     half = width // 2
-    depth = min(1024, width)
-    copies = []
-    for core in range(2):
-        mine = blocks[core * (chips + 1) : (core + 1) * (chips + 1)]
-        for j in range(chips):
-            rows = pl.ds((core * chips + j) * CAP, CAP)
-            if j < chips - 1:
-                copies.append((mine[j], rows_ref.at[rows, :]))
-            else:
-                copies.append((mine[j], rows_ref.at[rows, pl.ds(0, half)]))
-                copies.append((mine[j + 1], rows_ref.at[rows, pl.ds(half, half)]))
-    copies = [
-        pltpu.make_async_copy(source, target, sems.at[i]) for i, (source, target) in enumerate(copies)
-    ]
-    for copy in copies:
-        copy.start()
+    depth = min(1024, half)
     gate_sum[...] = jnp.zeros_like(gate_sum)
     up_sum[...] = jnp.zeros_like(up_sum)
-    for copy in copies:
-        copy.wait()
-
-    def one_part(step, carry):
-        place = pl.ds(pl.multiple_of(step * depth, depth), depth)
-        part = rows_ref[:, place]
-        gate_sum[...] += jnp.dot(part, gate_ref[place, :], preferred_element_type=jnp.float32)
-        up_sum[...] += jnp.dot(part, up_ref[place, :], preferred_element_type=jnp.float32)
-        return carry
-
-    lax.fori_loop(0, width // depth, one_part, 0)
+    for side in range(2):
+        sides = []
+        for core in range(2):
+            mine = blocks[core * (chips + 1) : (core + 1) * (chips + 1)]
+            sides += [(ref, side * half) for ref in mine[: chips - 1]] + [(mine[chips - 1 + side], 0)]
+
+        def one_part(step, carry):
+            part = jnp.concatenate(
+                [ref[:, pl.ds(pl.multiple_of(start + step * depth, depth), depth)] for ref, start in sides],
+                axis=0,
+            )
+            place = pl.ds(pl.multiple_of(side * half + step * depth, depth), depth)
+            gate_sum[...] += jnp.dot(part, gate_ref[place, :], preferred_element_type=jnp.float32)
+            up_sum[...] += jnp.dot(part, up_ref[place, :], preferred_element_type=jnp.float32)
+            return carry
+
+        lax.fori_loop(0, half // depth, one_part, 0)
     gate = gate_sum[...]
     out_ref[...] = (gate / (1.0 + jnp.exp(-gate)) * up_sum[...]).astype(jnp.bfloat16)
 
@@ -408,15 +371,10 @@
     vmem = pl.BlockSpec(memory_space=pltpu.VMEM)
     return pl.pallas_call(
         functools.partial(hidden_kernel, chips),
-        in_specs=[pl.BlockSpec(memory_space=pl.ANY)] * len(blocks) + [vmem] * 2,
+        in_specs=[vmem] * (len(blocks) + 2),
         out_specs=vmem,
-        out_shape=jax.ShapeDtypeStruct((rows, units), jnp.bfloat16),
-        scratch_shapes=[
-            pltpu.VMEM((rows, width), jnp.bfloat16),
-            pltpu.VMEM((rows, units), jnp.float32),
-            pltpu.VMEM((rows, units), jnp.float32),
-            pltpu.SemaphoreType.DMA((len(blocks),)),
-        ],
+        out_shape=pltpu.VMEM((rows, units), jnp.bfloat16),
+        scratch_shapes=[pltpu.VMEM((rows, units), jnp.float32)] * 2,
         compiler_params=pltpu.CompilerParams(vmem_limit_bytes=16 * MIB),
         cost_estimate=pl.CostEstimate(
             flops=4 * rows * width * units,
@@ -427,32 +385,32 @@
     )(*blocks, w_gate, w_up)
 
 
-def down_kernel(hidden_ref, down_ref, own_ref, sib_ref):
-    part = jnp.dot(hidden_ref[...], down_ref[...], preferred_element_type=jnp.float32)
-    part = part.astype(jnp.bfloat16)
-    middle = part.shape[0] // 2
-    own_ref[...] = part[:middle]
-    sib_ref[...] = part[middle:]
+def down_kernel(start, hidden_ref, down_ref, own_ref, sib_ref):
+    middle, width = own_ref.shape
+    cols = min(1024, width)
+
+    def one_part(step, carry):
+        source = pl.ds(pl.multiple_of(start + step * cols, cols), cols)
+        target = pl.ds(pl.multiple_of(step * cols, cols), cols)
+        part = jnp.dot(hidden_ref[...], down_ref[:, source], preferred_element_type=jnp.float32)
+        part = part.astype(jnp.bfloat16)
+        own_ref[:, target] = part[:middle]
+        sib_ref[:, target] = part[middle:]
+        return carry
+
+    lax.fori_loop(0, width // cols, one_part, 0)
 
 
 def down_call(hidden, w_down, piece, pieces):
     rows, units = hidden.shape
     width = w_down.shape[1] // pieces
-    cols = min(1024, width)
-    steps = width // cols
-    out_block = pl.BlockSpec((rows // 2, cols), lambda i: (0, i))
+    vmem = pl.BlockSpec(memory_space=pltpu.VMEM)
     return pl.pallas_call(
-        down_kernel,
-        grid=(steps,),
-        in_specs=[
-            pl.BlockSpec((rows, units), lambda i: (0, 0)),
-            pl.BlockSpec((units, cols), lambda i: (0, piece * steps + i)),
-        ],
-        out_specs=[out_block, out_block],
-        out_shape=[jax.ShapeDtypeStruct((rows // 2, width), jnp.bfloat16)] * 2,
-        compiler_params=pltpu.CompilerParams(
-            dimension_semantics=("arbitrary",), vmem_limit_bytes=16 * MIB
-        ),
+        functools.partial(down_kernel, piece * width),
+        in_specs=[vmem] * 2,
+        out_specs=[vmem] * 2,
+        out_shape=[pltpu.VMEM((rows // 2, width), jnp.bfloat16)] * 2,
+        compiler_params=pltpu.CompilerParams(vmem_limit_bytes=16 * MIB),
         cost_estimate=pl.CostEstimate(
             flops=2 * rows * width * units,
             bytes_accessed=2 * width * units + 2 * rows * width,
@@ -567,7 +525,7 @@
     table = table.astype(jnp.bfloat16)
 
     attention = Attention(me, queries, chips)
-    own = stack(keys, values)
+    own = jnp.concatenate([keys, values], axis=0)
     from_left, from_right, own_sib = go_right(own), go_left(own), swap(own)
     acc, total, shift = attention.own(own, own_sib)
     state = (acc, total)
@@ -606,7 +564,7 @@
     blocks = blocks_right + blocks_left + far
     others = swapped[:1] + swapped[1:-2:2] + swapped[2:-2:2] + swapped[-2:]
     hidden = hidden_call(chips, blocks + others, *loads[:2])
-    w_down = pltpu.with_memory_space_constraint(loads[2], pltpu.VMEM)
+    w_down = loads[2]
 
     sums = []
     for piece in range(PIECES):

time: 220 us -> 190 us (0.86)
  Pallas kernels: 76.7 us -> 36.6 us
  waiting for transfers between devices: 51.2 us -> 65.6 us
  starting transfers between devices: 88.6 us -> 80.3 us
  local copies, waits for them, and re-layouts: 1.21 us -> 4.98 us
    pallas_call x9 -> x8, Pallas kernels: 59.9 us -> 19.8 us  [the longest x1 8.17 us: hidden_call(): pl.pallas_call(functools.partial(hidden_kernel, chips), in_specs=[vmem] *...]
    ppermute x16, waiting for transfers between devices: 29.3 us -> 43.2 us  [per_device(): go_right = lambda x: lax.ppermute(x, 'ctx', right)]
    ppermute x20, starting transfers between devices: 52.6 us -> 45.5 us  [per_device(): swap = lambda x: lax.ppermute(x, 'ctx', sibling)]
    unnamed x10, local copies, waits for them, and re-layouts: 1.09 us -> 3.89 us
  transfers between devices with their start and end apart: 52 -> 52, of which waited for: 33 -> 33; matrix products, arithmetic and copies ran while one was open for 0% -> 1% of each run, Pallas kernels for 18% -> 12%
where the time goes in v4:
time: 190 us; the launch traced here: 189 us
  starting transfers between devices  80.3 us (42%)
  waiting for transfers between devices  65.6 us (35%)
  Pallas kernels  36.6 us (19%)
  local copies, waits for them, and re-layouts  4.98 us (3%)
    ppermute x20, starting transfers between devices, per_device(): swap = lambda x: lax.ppermute(x, 'ctx', sibling)  45.5 us
    ppermute x16, waiting for transfers between devices, per_device(): go_right = lambda x: lax.ppermute(x, 'ctx', right)  43.2 us
    ppermute x16, starting transfers between devices, per_device(): go_right = lambda x: lax.ppermute(x, 'ctx', right)  27.9 us
    ppermute x16, waiting for transfers between devices, per_device(): go_left = lambda x: lax.ppermute(x, 'ctx', left)  19.6 us
    pallas_call x3, Pallas kernels, load(): pl.pallas_call(load_kernel, in_specs=[pl.BlockSpec(memory_space=pltpu.HBM...  13.8 us
    pallas_call x1, Pallas kernels, hidden_call(): pl.pallas_call(functools.partial(hidden_kernel, chips), in_specs=[vmem] *...  8.17 us
    pallas_call x5, Pallas kernels, call(): pl.pallas_call(kernel, in_specs=[pl.BlockSpec(memory_space=pltpu.SMEM)] +...  7.07 us
    ppermute x16, starting transfers between devices, per_device(): go_left = lambda x: lax.ppermute(x, 'ctx', left)  6.9 us
  transfers between devices with their start and end apart: 52, of which 33 were waited for; matrix products, arithmetic and copies ran while one was open for 1% of the time, Pallas kernels for 12%

profile of v4, /device:TPU:0, one launch (start us, length us, event | category | flops | bytes accessed | tf_op | source)
XLA Modules:
  0.0 189.3 jit_solution(7824022629001817622)
XLA Ops:
  3.1 2.6 %collective-permute-start = (bf16[256,1024]{1,0:T(8,128)(2,1)S(1)}, bf16[256,1024]{1,0:T(8,128)(2,1)S(1)}, u32[]{:S(2)}, u32[]{:S(2)}) collective-permute-start(bf16[256,1024]{1,0:T(8,128)(2,1)S(1)} %constant_dynamic-update-slice_fusion.own_ref.refs_9_), channel_id=1, source_target_pairs={{0,4},{1,5},{4,8},{5,9},{8,12},{9,13},{12,14},{13,15},{14,10},{15,... | collective-permute-start | bytes 1572872 | tf_op jit(solution)/shard_map/ppermute | solution.py:504
  5.8 1.6 copy-done
  7.4 5.1 %attend_own.1 = (f32[8,1024,128]{2,1,0:T(8,128)S(1)}, f32[8,1024,128]{2,1,0:T(8,128)S(1)}, f32[8,1024,128]{2,1,0:T(8,128)S(1)}) custom-call(s32[1]{0:T(128)} %bitcast.me_ref, bf16[128,8192]{1,0:T(8,128)(2,1)S(1)} %copy-done, bf16[256,1024]{1,0:T(8,128)(2,1)S(1)} %constant_dynamic-update-slice_fusion.own_ref.refs_9_, ...), custom_call_target="tpu_custom_call" | custom-call | flops 536870912 | bytes 4194304 | tf_op jit(solution)/shard_map/attend_own/pallas_call | solution.py:267
  12.5 5.7 %collective-permute-done.refs_0_.refs_11_ = bf16[256,1024]{1,0:T(8,128)(2,1)S(1)} collective-permute-done((bf16[256,1024]{1,0:T(8,128)(2,1)S(1)}, bf16[256,1024]{1,0:T(8,128)(2,1)S(1)}, u32[]{:S(2)}, u32[]{:S(2)}) %collective-permute-start) | collective-permute-done | bytes 524320 | tf_op jit(solution)/shard_map/ppermute | solution.py:504
  20.2 1.6 collective-permute-start.3
  22.4 11.7 %collective-permute-done.3.refs_0_.refs_15_ = bf16[256,1024]{1,0:T(8,128)(2,1)S(1)} collective-permute-done((bf16[256,1024]{1,0:T(8,128)(2,1)S(1)}, bf16[256,1024]{1,0:T(8,128)(2,1)S(1)}, u32[]{:S(2)}, u32[]{:S(2)}) %collective-permute-start.3) | collective-permute-done | bytes 524320 | tf_op jit(solution)/shard_map/ppermute | solution.py:504
  35.9 1.6 collective-permute-start.7
  38.0 11.7 %collective-permute-done.7.refs_0_.refs_19_ = bf16[256,1024]{1,0:T(8,128)(2,1)S(1)} collective-permute-done((bf16[256,1024]{1,0:T(8,128)(2,1)S(1)}, bf16[256,1024]{1,0:T(8,128)(2,1)S(1)}, u32[]{:S(2)}, u32[]{:S(2)}) %collective-permute-start.7) | collective-permute-done | bytes 524320 | tf_op jit(solution)/shard_map/ppermute | solution.py:504
  53.8 6.1 %collective-permute-done.11.refs_0_.refs_23_ = bf16[128,1024]{1,0:T(8,128)(2,1)S(1)} collective-permute-done((bf16[128,1024]{1,0:T(8,128)(2,1)S(1)}, bf16[128,1024]{1,0:T(8,128)(2,1)S(1)}, u32[]{:S(2)}, u32[]{:S(2)}) %collective-permute-start.11) | collective-permute-done | bytes 262176 | tf_op jit(solution)/shard_map/ppermute | solution.py:504
  63.1 1.9 %attend_last.1 = (bf16[128,8192]{1,0:T(8,128)(2,1)S(1)}, bf16[16,8192]{1,0:T(8,128)(2,1)S(1)}, f32[8,1024,128]{2,1,0:T(8,128)S(1)}, f32[8,1024,128]{2,1,0:T(8,128)S(1)}) custom-call(s32[1]{0:T(128)} %bitcast.me_ref, bf16[128,8192]{1,0:T(8,128)(2,1)S(1)} %copy-done, ...), custom_call_target="tpu_custom_call", output_to_operand_aliasing={{2}: (7, {}), {3}: (8, {})} | custom-call | flops 536870912 | bytes 4194304 | tf_op jit(solution)/shard_map/attend_last/pallas_call | solution.py:267
  67.1 4.6 %load.3.refs_18_ = bf16[8192,768]{1,0:T(8,128)(2,1)S(1)} custom-call(bf16[8192,768]{1,0:T(8,128)(2,1)} %source_ref), custom_call_target="tpu_custom_call" | custom-call | bytes 6291456 | tf_op jit(solution)/shard_map/load/pallas_call | solution.py:327
  71.7 1.7 collective-permute-done.17.refs_1_
  73.4 3.3 %collective-permute-done.18.refs_4_ = bf16[16,8192]{1,0:T(8,128)(2,1)S(1)} collective-permute-done((bf16[16,8192]{1,0:T(8,128)(2,1)S(1)}, bf16[16,8192]{1,0:T(8,128)(2,1)S(1)}, u32[]{:S(2)}, u32[]{:S(2)}) %collective-permute-start.18) | collective-permute-done | bytes 262176 | tf_op jit(solution)/shard_map/ppermute | solution.py:505
  76.7 3.2 %collective-permute-start.19 = (bf16[16,8192]{1,0:T(8,128)(2,1)S(1)}, bf16[16,8192]{1,0:T(8,128)(2,1)S(1)}, u32[]{:S(2)}, u32[]{:S(2)}) collective-permute-start(bf16[16,8192]{1,0:T(8,128)(2,1)S(1)} %collective-permute-done.17.refs_1_), channel_id=1, source_target_pairs={{0,4},{1,5},{4,8},{5,9},{8,12},{9,13},{12,14},{13,15},{14,10},{15,... | collective-permute-start | bytes 786440 | tf_op jit(solution)/shard_map/ppermute | solution.py:504
  79.9 4.6 %load.4.refs_19_ = bf16[8192,768]{1,0:T(8,128)(2,1)S(1)} custom-call(bf16[8192,768]{1,0:T(8,128)(2,1)} %source_ref.1), custom_call_target="tpu_custom_call" | custom-call | bytes 6291456 | tf_op jit(solution)/shard_map/load/pallas_call | solution.py:327
  88.3 40.6 %collective-permute-start.25 = (bf16[16,8192]{1,0:T(8,128)(2,1)S(1)}, bf16[16,8192]{1,0:T(8,128)(2,1)S(1)}, u32[]{:S(2)}, u32[]{:S(2)}) collective-permute-start(bf16[16,8192]{1,0:T(8,128)(2,1)S(1)} %get-tuple-element.116.refs_0_), channel_id=1, source_target_pairs={{0,1},{1,0},{2,3},{3,2},{4,5},{5,4},{6,7},{7,6},{8,9},{9,8},{10,11... | collective-permute-start | bytes 786440 | tf_op jit(solution)/shard_map/ppermute | solution.py:506
  129.5 4.6 %load.5.down_ref = bf16[768,8192]{1,0:T(8,128)(2,1)S(1)} custom-call(bf16[768,8192]{1,0:T(8,128)(2,1)} %source_ref.2), custom_call_target="tpu_custom_call" | custom-call | bytes 6291456 | tf_op jit(solution)/shard_map/load/pallas_call | solution.py:327
  134.1 1.8 collective-permute-start.23
  136.8 2.8 %collective-permute-done.23.refs_7_ = bf16[16,4096]{1,0:T(8,128)(2,1)S(1)} collective-permute-done((bf16[16,4096]{1,0:T(8,128)(2,1)S(1)}, bf16[16,4096]{1,0:T(8,128)(2,1)S(1)}, u32[]{:S(2)}, u32[]{:S(2)}) %collective-permute-start.23) | collective-permute-done | bytes 131104 | tf_op jit(solution)/shard_map/ppermute | solution.py:504
  139.6 2.5 %collective-permute-done.24.refs_8_ = bf16[16,4096]{1,0:T(8,128)(2,1)S(1)} collective-permute-done((bf16[16,4096]{1,0:T(8,128)(2,1)S(1)}, bf16[16,4096]{1,0:T(8,128)(2,1)S(1)}, u32[]{:S(2)}, u32[]{:S(2)}) %collective-permute-start.24) | collective-permute-done | bytes 131104 | tf_op jit(solution)/shard_map/ppermute | solution.py:505
  143.7 8.2 %hidden.1.hidden_ref = bf16[256,768]{1,0:T(8,128)(2,1)S(1)} custom-call(bf16[16,8192]{1,0:T(8,128)(2,1)S(1)} %get-tuple-element.116.refs_0_, bf16[16,8192]{1,0:T(8,128)(2,1)S(1)} %collective-permute-done.17.refs_1_, bf16[16,8192]{1,0:T(8,128)(2,1)S(1)} %collective-permute-done.19.refs_2_, bf16[16,8192]{1,0:T(8,128)(2,1)S(1)} %collective-permute-done.21.refs_3_, ...), custom_call_target="tpu_custom_call" | custom-call | flops 6442450944 | bytes 29360128 | tf_op jit(solution)/shard_map/hidden/pallas_call | solution.py:372
  151.9 2.3 %down.2 = (bf16[128,4096]{1,0:T(8,128)(2,1)S(1)}, bf16[128,4096]{1,0:T(8,128)(2,1)S(1)}) custom-call(bf16[256,768]{1,0:T(8,128)(2,1)S(1)} %hidden.1.hidden_ref, bf16[768,8192]{1,0:T(8,128)(2,1)S(1)} %load.5.down_ref), custom_call_target="tpu_custom_call" | custom-call | flops 1610612736 | bytes 8388608 | tf_op jit(solution)/shard_map/down/pallas_call | solution.py:408
  154.6 2.3 %down.3 = (bf16[128,4096]{1,0:T(8,128)(2,1)S(1)}, bf16[128,4096]{1,0:T(8,128)(2,1)S(1)}) custom-call(bf16[256,768]{1,0:T(8,128)(2,1)S(1)} %hidden.1.hidden_ref, bf16[768,8192]{1,0:T(8,128)(2,1)S(1)} %load.5.down_ref), custom_call_target="tpu_custom_call" | custom-call | flops 1610612736 | bytes 8388608 | tf_op jit(solution)/shard_map/down/pallas_call | solution.py:408
  157.2 1.8 collective-permute-start.35
  159.8 1.8 collective-permute-start.44
  163.7 1.7 collective-permute-start.37
  166.9 1.7 collective-permute-start.46
  170.3 1.8 collective-permute-start.39
  176.2 2.0 %collective-permute-start.41 = (bf16[16,4096]{1,0:T(8,128)(2,1)S(1)}, bf16[16,4096]{1,0:T(8,128)(2,1)S(1)}, u32[]{:S(2)}, u32[]{:S(2)}) collective-permute-start(bf16[16,4096]{1,0:T(8,128)(2,1)S(1)} %get-tuple-element.132), channel_id=1, source_target_pairs={{0,4},{1,5},{4,8},{5,9},{8,12},{9,13},{12,14},{13,15},{14,10},{15,... | collective-permute-start | bytes 393224 | tf_op jit(solution)/shard_map/ppermute | solution.py:504
  179.6 1.7 collective-permute-start.50
  183.0 1.6 collective-permute-done.50.c_ref
  184.6 1.6 collective-permute-done.51.d_ref
  (128 shorter events, 40.4 us)
Async XLA Ops:
  3.1 15.1 %collective-permute-start = (bf16[256,1024]{1,0:T(8,128)(2,1)S(1)}, bf16[256,1024]{1,0:T(8,128)(2,1)S(1)}, u32[]{:S(2)}, u32[]{:S(2)}) collective-permute-start(bf16[256,1024]{1,0:T(8,128)(2,1)S(1)} %constant_dynamic-update-slice_fusion.own_ref.refs_9_), channel_id=1, source_target_pairs={{0,4},{1,5},{4,8},{5,9},{8,12},{9,13},{12,14},{13,15},{14,10},{15,... | collective-permute-start | bytes 1572872 | tf_op jit(solution)/shard_map/ppermute | solution.py:504
  5.7 14.0 %collective-permute-start.1 = (bf16[256,1024]{1,0:T(8,128)(2,1)S(1)}, bf16[256,1024]{1,0:T(8,128)(2,1)S(1)}, u32[]{:S(2)}, u32[]{:S(2)}) collective-permute-start(bf16[256,1024]{1,0:T(8,128)(2,1)S(1)} %constant_dynamic-update-slice_fusion.own_ref.refs_9_), channel_id=1, source_target_pairs={{4,0},{5,1},{8,4},{9,5},{12,8},{13,9},{14,12},{15,13},{10,14},{11,... | collective-permute-start | bytes 1572872 | tf_op jit(solution)/shard_map/ppermute | solution.py:505
  20.2 13.8 %collective-permute-start.3 = (bf16[256,1024]{1,0:T(8,128)(2,1)S(1)}, bf16[256,1024]{1,0:T(8,128)(2,1)S(1)}, u32[]{:S(2)}, u32[]{:S(2)}) collective-permute-start(bf16[256,1024]{1,0:T(8,128)(2,1)S(1)} %collective-permute-done.refs_0_.refs_11_), channel_id=1, source_target_pairs={{0,4},{1,5},{4,8},{5,9},{8,12},{9,13},{12,14},{13,15},{14,10},{15,... | collective-permute-start | bytes 1572872 | tf_op jit(solution)/shard_map/ppermute | solution.py:504
  21.8 13.6 %collective-permute-start.4 = (bf16[256,1024]{1,0:T(8,128)(2,1)S(1)}, bf16[256,1024]{1,0:T(8,128)(2,1)S(1)}, u32[]{:S(2)}, u32[]{:S(2)}) collective-permute-start(bf16[256,1024]{1,0:T(8,128)(2,1)S(1)} %collective-permute-done.1.refs_2_.refs_13_), channel_id=1, source_target_pairs={{4,0},{5,1},{8,4},{9,5},{12,8},{13,9},{14,12},{15,13},{10,14},{11,... | collective-permute-start | bytes 1572872 | tf_op jit(solution)/shard_map/ppermute | solution.py:505
  35.9 13.9 %collective-permute-start.7 = (bf16[256,1024]{1,0:T(8,128)(2,1)S(1)}, bf16[256,1024]{1,0:T(8,128)(2,1)S(1)}, u32[]{:S(2)}, u32[]{:S(2)}) collective-permute-start(bf16[256,1024]{1,0:T(8,128)(2,1)S(1)} %collective-permute-done.3.refs_0_.refs_15_), channel_id=1, source_target_pairs={{0,4},{1,5},{4,8},{5,9},{8,12},{9,13},{12,14},{13,15},{14,10},{15,... | collective-permute-start | bytes 1572872 | tf_op jit(solution)/shard_map/ppermute | solution.py:504
  37.5 13.6 %collective-permute-start.8 = (bf16[256,1024]{1,0:T(8,128)(2,1)S(1)}, bf16[256,1024]{1,0:T(8,128)(2,1)S(1)}, u32[]{:S(2)}, u32[]{:S(2)}) collective-permute-start(bf16[256,1024]{1,0:T(8,128)(2,1)S(1)} %collective-permute-done.4.refs_2_.refs_17_), channel_id=1, source_target_pairs={{4,0},{5,1},{8,4},{9,5},{12,8},{13,9},{14,12},{15,13},{10,14},{11,... | collective-permute-start | bytes 1572872 | tf_op jit(solution)/shard_map/ppermute | solution.py:505
  51.7 8.3 %collective-permute-start.11 = (bf16[128,1024]{1,0:T(8,128)(2,1)S(1)}, bf16[128,1024]{1,0:T(8,128)(2,1)S(1)}, u32[]{:S(2)}, u32[]{:S(2)}) collective-permute-start(bf16[128,1024]{1,0:T(8,128)(2,1)S(1)} %slice.136), channel_id=1, source_target_pairs={{0,4},{1,5},{4,8},{5,9},{8,12},{9,13},{12,14},{13,15},{14,10},{15,... | collective-permute-start | bytes 786440 | tf_op jit(solution)/shard_map/ppermute | solution.py:504
  53.2 7.9 %collective-permute-start.12 = (bf16[128,1024]{1,0:T(8,128)(2,1)S(1)}, bf16[128,1024]{1,0:T(8,128)(2,1)S(1)}, u32[]{:S(2)}, u32[]{:S(2)}) collective-permute-start(bf16[128,1024]{1,0:T(8,128)(2,1)S(1)} %slice.137), channel_id=1, source_target_pairs={{4,0},{5,1},{8,4},{9,5},{12,8},{13,9},{14,12},{15,13},{10,14},{11,... | collective-permute-start | bytes 786440 | tf_op jit(solution)/shard_map/ppermute | solution.py:505
  65.0 8.4 %collective-permute-start.17 = (bf16[16,8192]{1,0:T(8,128)(2,1)S(1)}, bf16[16,8192]{1,0:T(8,128)(2,1)S(1)}, u32[]{:S(2)}, u32[]{:S(2)}) collective-permute-start(bf16[16,8192]{1,0:T(8,128)(2,1)S(1)} %get-tuple-element.116.refs_0_), channel_id=1, source_target_pairs={{0,4},{1,5},{4,8},{5,9},{8,12},{9,13},{12,14},{13,15},{14,10},{15,... | collective-permute-start | bytes 786440 | tf_op jit(solution)/shard_map/ppermute | solution.py:504
  65.5 11.2 %collective-permute-start.18 = (bf16[16,8192]{1,0:T(8,128)(2,1)S(1)}, bf16[16,8192]{1,0:T(8,128)(2,1)S(1)}, u32[]{:S(2)}, u32[]{:S(2)}) collective-permute-start(bf16[16,8192]{1,0:T(8,128)(2,1)S(1)} %get-tuple-element.116.refs_0_), channel_id=1, source_target_pairs={{4,0},{5,1},{8,4},{9,5},{12,8},{13,9},{14,12},{15,13},{10,14},{11,... | collective-permute-start | bytes 786440 | tf_op jit(solution)/shard_map/ppermute | solution.py:505
  76.7 8.2 %collective-permute-start.19 = (bf16[16,8192]{1,0:T(8,128)(2,1)S(1)}, bf16[16,8192]{1,0:T(8,128)(2,1)S(1)}, u32[]{:S(2)}, u32[]{:S(2)}) collective-permute-start(bf16[16,8192]{1,0:T(8,128)(2,1)S(1)} %collective-permute-done.17.refs_1_), channel_id=1, source_target_pairs={{0,4},{1,5},{4,8},{5,9},{8,12},{9,13},{12,14},{13,15},{14,10},{15,... | collective-permute-start | bytes 786440 | tf_op jit(solution)/shard_map/ppermute | solution.py:504
  79.9 6.4 %collective-permute-start.20 = (bf16[16,8192]{1,0:T(8,128)(2,1)S(1)}, bf16[16,8192]{1,0:T(8,128)(2,1)S(1)}, u32[]{:S(2)}, u32[]{:S(2)}) collective-permute-start(bf16[16,8192]{1,0:T(8,128)(2,1)S(1)} %collective-permute-done.18.refs_4_), channel_id=1, source_target_pairs={{4,0},{5,1},{8,4},{9,5},{12,8},{13,9},{14,12},{15,13},{10,14},{11,... | collective-permute-start | bytes 786440 | tf_op jit(solution)/shard_map/ppermute | solution.py:505
  86.3 47.8 %collective-permute-start.21 = (bf16[16,8192]{1,0:T(8,128)(2,1)S(1)}, bf16[16,8192]{1,0:T(8,128)(2,1)S(1)}, u32[]{:S(2)}, u32[]{:S(2)}) collective-permute-start(bf16[16,8192]{1,0:T(8,128)(2,1)S(1)} %collective-permute-done.19.refs_2_), channel_id=1, source_target_pairs={{0,4},{1,5},{4,8},{5,9},{8,12},{9,13},{12,14},{13,15},{14,10},{15,... | collective-permute-start | bytes 786440 | tf_op jit(solution)/shard_map/ppermute | solution.py:504
  87.4 46.6 %collective-permute-start.22 = (bf16[16,8192]{1,0:T(8,128)(2,1)S(1)}, bf16[16,8192]{1,0:T(8,128)(2,1)S(1)}, u32[]{:S(2)}, u32[]{:S(2)}) collective-permute-start(bf16[16,8192]{1,0:T(8,128)(2,1)S(1)} %collective-permute-done.20.refs_5_), channel_id=1, source_target_pairs={{4,0},{5,1},{8,4},{9,5},{12,8},{13,9},{14,12},{15,13},{10,14},{11,... | collective-permute-start | bytes 786440 | tf_op jit(solution)/shard_map/ppermute | solution.py:505
  88.3 47.6 %collective-permute-start.25 = (bf16[16,8192]{1,0:T(8,128)(2,1)S(1)}, bf16[16,8192]{1,0:T(8,128)(2,1)S(1)}, u32[]{:S(2)}, u32[]{:S(2)}) collective-permute-start(bf16[16,8192]{1,0:T(8,128)(2,1)S(1)} %get-tuple-element.116.refs_0_), channel_id=1, source_target_pairs={{0,1},{1,0},{2,3},{3,2},{4,5},{5,4},{6,7},{7,6},{8,9},{9,8},{10,11... | collective-permute-start | bytes 786440 | tf_op jit(solution)/shard_map/ppermute | solution.py:506
  128.9 7.5 %collective-permute-start.26 = (bf16[16,8192]{1,0:T(8,128)(2,1)S(1)}, bf16[16,8192]{1,0:T(8,128)(2,1)S(1)}, u32[]{:S(2)}, u32[]{:S(2)}) collective-permute-start(bf16[16,8192]{1,0:T(8,128)(2,1)S(1)} %collective-permute-done.17.refs_1_), channel_id=1, source_target_pairs={{0,1},{1,0},{2,3},{3,2},{4,5},{5,4},{6,7},{7,6},{8,9},{9,8},{10,11... | collective-permute-start | bytes 786440 | tf_op jit(solution)/shard_map/ppermute | solution.py:506
  128.9 7.8 %collective-permute-start.29 = (bf16[16,8192]{1,0:T(8,128)(2,1)S(1)}, bf16[16,8192]{1,0:T(8,128)(2,1)S(1)}, u32[]{:S(2)}, u32[]{:S(2)}) collective-permute-start(bf16[16,8192]{1,0:T(8,128)(2,1)S(1)} %collective-permute-done.18.refs_4_), channel_id=1, source_target_pairs={{0,1},{1,0},{2,3},{3,2},{4,5},{5,4},{6,7},{7,6},{8,9},{9,8},{10,11... | collective-permute-start | bytes 786440 | tf_op jit(solution)/shard_map/ppermute | solution.py:506
  135.9 6.3 %collective-permute-start.27 = (bf16[16,8192]{1,0:T(8,128)(2,1)S(1)}, bf16[16,8192]{1,0:T(8,128)(2,1)S(1)}, u32[]{:S(2)}, u32[]{:S(2)}) collective-permute-start(bf16[16,8192]{1,0:T(8,128)(2,1)S(1)} %collective-permute-done.19.refs_2_), channel_id=1, source_target_pairs={{0,1},{1,0},{2,3},{3,2},{4,5},{5,4},{6,7},{7,6},{8,9},{9,8},{10,11... | collective-permute-start | bytes 786440 | tf_op jit(solution)/shard_map/ppermute | solution.py:506
  135.9 6.8 %collective-permute-start.28 = (bf16[16,8192]{1,0:T(8,128)(2,1)S(1)}, bf16[16,8192]{1,0:T(8,128)(2,1)S(1)}, u32[]{:S(2)}, u32[]{:S(2)}) collective-permute-start(bf16[16,8192]{1,0:T(8,128)(2,1)S(1)} %collective-permute-done.21.refs_3_), channel_id=1, source_target_pairs={{0,1},{1,0},{2,3},{3,2},{4,5},{5,4},{6,7},{7,6},{8,9},{9,8},{10,11... | collective-permute-start | bytes 786440 | tf_op jit(solution)/shard_map/ppermute | solution.py:506
  136.5 5.7 %collective-permute-start.24 = (bf16[16,4096]{1,0:T(8,128)(2,1)S(1)}, bf16[16,4096]{1,0:T(8,128)(2,1)S(1)}, u32[]{:S(2)}, u32[]{:S(2)}) collective-permute-start(bf16[16,4096]{1,0:T(8,128)(2,1)S(1)} %slice.139), channel_id=1, source_target_pairs={{4,0},{5,1},{8,4},{9,5},{12,8},{13,9},{14,12},{15,13},{10,14},{11,... | collective-permute-start | bytes 393224 | tf_op jit(solution)/shard_map/ppermute | solution.py:505
  136.8 5.9 %collective-permute-start.30 = (bf16[16,8192]{1,0:T(8,128)(2,1)S(1)}, bf16[16,8192]{1,0:T(8,128)(2,1)S(1)}, u32[]{:S(2)}, u32[]{:S(2)}) collective-permute-start(bf16[16,8192]{1,0:T(8,128)(2,1)S(1)} %collective-permute-done.20.refs_5_), channel_id=1, source_target_pairs={{0,1},{1,0},{2,3},{3,2},{4,5},{5,4},{6,7},{7,6},{8,9},{9,8},{10,11... | collective-permute-start | bytes 786440 | tf_op jit(solution)/shard_map/ppermute | solution.py:506
  159.8 5.7 %collective-permute-start.44 = (bf16[16,2048]{1,0:T(8,128)(2,1)S(1)}, bf16[16,2048]{1,0:T(8,128)(2,1)S(1)}, u32[]{:S(2)}, u32[]{:S(2)}) collective-permute-start(bf16[16,2048]{1,0:T(8,128)(2,1)S(1)} %get-tuple-element.136), channel_id=1, source_target_pairs={{0,4},{1,5},{4,8},{5,9},{8,12},{9,13},{12,14},{13,15},{14,10},{15,... | collective-permute-start | bytes 196616 | tf_op jit(solution)/shard_map/ppermute | solution.py:504
  163.3 6.2 %collective-permute-start.38 = (bf16[16,4096]{1,0:T(8,128)(2,1)S(1)}, bf16[16,4096]{1,0:T(8,128)(2,1)S(1)}, u32[]{:S(2)}, u32[]{:S(2)}) collective-permute-start(bf16[16,4096]{1,0:T(8,128)(2,1)S(1)} %pad_maximum_fusion.1), channel_id=1, source_target_pairs={{4,0},{5,1},{8,4},{9,5},{12,8},{13,9},{14,12},{15,13},{10,14},{11,... | collective-permute-start | bytes 393224 | tf_op jit(solution)/shard_map/ppermute | solution.py:505
  163.7 6.3 %collective-permute-start.37 = (bf16[16,4096]{1,0:T(8,128)(2,1)S(1)}, bf16[16,4096]{1,0:T(8,128)(2,1)S(1)}, u32[]{:S(2)}, u32[]{:S(2)}) collective-permute-start(bf16[16,4096]{1,0:T(8,128)(2,1)S(1)} %pad_maximum_fusion), channel_id=1, source_target_pairs={{0,4},{1,5},{4,8},{5,9},{8,12},{9,13},{12,14},{13,15},{14,10},{15,... | collective-permute-start | bytes 393224 | tf_op jit(solution)/shard_map/ppermute | solution.py:504
  166.5 6.0 %collective-permute-start.47 = (bf16[16,4096]{1,0:T(8,128)(2,1)S(1)}, bf16[16,4096]{1,0:T(8,128)(2,1)S(1)}, u32[]{:S(2)}, u32[]{:S(2)}) collective-permute-start(bf16[16,4096]{1,0:T(8,128)(2,1)S(1)} %pad_maximum_fusion.3), channel_id=1, source_target_pairs={{4,0},{5,1},{8,4},{9,5},{12,8},{13,9},{14,12},{15,13},{10,14},{11,... | collective-permute-start | bytes 393224 | tf_op jit(solution)/shard_map/ppermute | solution.py:505
  166.9 6.0 %collective-permute-start.46 = (bf16[16,4096]{1,0:T(8,128)(2,1)S(1)}, bf16[16,4096]{1,0:T(8,128)(2,1)S(1)}, u32[]{:S(2)}, u32[]{:S(2)}) collective-permute-start(bf16[16,4096]{1,0:T(8,128)(2,1)S(1)} %pad_maximum_fusion.2), channel_id=1, source_target_pairs={{0,4},{1,5},{4,8},{5,9},{8,12},{9,13},{12,14},{13,15},{14,10},{15,... | collective-permute-start | bytes 393224 | tf_op jit(solution)/shard_map/ppermute | solution.py:504
  170.1 5.7 %collective-permute-start.40 = (bf16[16,4096]{1,0:T(8,128)(2,1)S(1)}, bf16[16,4096]{1,0:T(8,128)(2,1)S(1)}, u32[]{:S(2)}, u32[]{:S(2)}) collective-permute-start(bf16[16,4096]{1,0:T(8,128)(2,1)S(1)} %get-tuple-element.131), channel_id=1, source_target_pairs={{4,0},{5,1},{8,4},{9,5},{12,8},{13,9},{14,12},{15,13},{10,14},{11,... | collective-permute-start | bytes 393224 | tf_op jit(solution)/shard_map/ppermute | solution.py:505
  170.3 5.8 %collective-permute-start.39 = (bf16[16,4096]{1,0:T(8,128)(2,1)S(1)}, bf16[16,4096]{1,0:T(8,128)(2,1)S(1)}, u32[]{:S(2)}, u32[]{:S(2)}) collective-permute-start(bf16[16,4096]{1,0:T(8,128)(2,1)S(1)} %get-tuple-element.130), channel_id=1, source_target_pairs={{0,4},{1,5},{4,8},{5,9},{8,12},{9,13},{12,14},{13,15},{14,10},{15,... | collective-permute-start | bytes 393224 | tf_op jit(solution)/shard_map/ppermute | solution.py:504
  173.0 6.3 %collective-permute-start.49 = (bf16[16,4096]{1,0:T(8,128)(2,1)S(1)}, bf16[16,4096]{1,0:T(8,128)(2,1)S(1)}, u32[]{:S(2)}, u32[]{:S(2)}) collective-permute-start(bf16[16,4096]{1,0:T(8,128)(2,1)S(1)} %get-tuple-element.141), channel_id=1, source_target_pairs={{4,0},{5,1},{8,4},{9,5},{12,8},{13,9},{14,12},{15,13},{10,14},{11,... | collective-permute-start | bytes 393224 | tf_op jit(solution)/shard_map/ppermute | solution.py:505
  173.7 5.8 %collective-permute-start.48 = (bf16[16,4096]{1,0:T(8,128)(2,1)S(1)}, bf16[16,4096]{1,0:T(8,128)(2,1)S(1)}, u32[]{:S(2)}, u32[]{:S(2)}) collective-permute-start(bf16[16,4096]{1,0:T(8,128)(2,1)S(1)} %get-tuple-element.140), channel_id=1, source_target_pairs={{0,4},{1,5},{4,8},{5,9},{8,12},{9,13},{12,14},{13,15},{14,10},{15,... | collective-permute-start | bytes 393224 | tf_op jit(solution)/shard_map/ppermute | solution.py:504
  176.2 11.6 %collective-permute-start.41 = (bf16[16,4096]{1,0:T(8,128)(2,1)S(1)}, bf16[16,4096]{1,0:T(8,128)(2,1)S(1)}, u32[]{:S(2)}, u32[]{:S(2)}) collective-permute-start(bf16[16,4096]{1,0:T(8,128)(2,1)S(1)} %get-tuple-element.132), channel_id=1, source_target_pairs={{0,4},{1,5},{4,8},{5,9},{8,12},{9,13},{12,14},{13,15},{14,10},{15,... | collective-permute-start | bytes 393224 | tf_op jit(solution)/shard_map/ppermute | solution.py:504
  178.2 9.6 %collective-permute-start.42 = (bf16[16,4096]{1,0:T(8,128)(2,1)S(1)}, bf16[16,4096]{1,0:T(8,128)(2,1)S(1)}, u32[]{:S(2)}, u32[]{:S(2)}) collective-permute-start(bf16[16,4096]{1,0:T(8,128)(2,1)S(1)} %get-tuple-element.133), channel_id=1, source_target_pairs={{4,0},{5,1},{8,4},{9,5},{12,8},{13,9},{14,12},{15,13},{10,14},{11,... | collective-permute-start | bytes 393224 | tf_op jit(solution)/shard_map/ppermute | solution.py:505
  (24 other events, 106.7 us)
